TPU v7x, 32 devices: a whole 2x2x4 slice. The times are simulated.
32 devices in a mesh: ctx: 8 (over z, y), wa: 4 (over x, core).
Axes of the slice: x: 2, y: 2, z: 4, core: 2. Of those that a mesh axis runs over, the one named last changes fastest.
Arguments:
- tokens: bfloat16 [8, 1024, 960], P('wa', 'ctx'), may hold values from -6 to 6
- w_query: bfloat16 [960, 960], P('wa'), may hold values from -0.1875 to 0.1875
- w_key: bfloat16 [960, 320], P('wa'), may hold values from -0.1875 to 0.1875
- w_value: bfloat16 [960, 320], P('wa'), may hold values from -0.1875 to 0.1875
- w_out: bfloat16 [960, 960], P('wa'), may hold values from -1.5 to 1.5
- w_gate: bfloat16 [960, 2560], P('wa'), may hold values from -0.1875 to 0.1875
- w_up: bfloat16 [960, 2560], P('wa'), may hold values from -0.1875 to 0.1875
- w_down: bfloat16 [2560, 960], P('wa'), may hold values from -0.125 to 0.125
- norm_attn: bfloat16 [960], P('wa'), may hold values from 0.5 to 1.5
- norm_ffn: bfloat16 [960], P('wa'), may hold values from 0.5 to 1.5
- cotangent: bfloat16 [8, 1024, 960], P('wa', 'ctx'), may hold values from -6 to 6
Outputs:
- mixed: bfloat16 [8, 1024, 960], P('wa', 'ctx')
- input_grad: bfloat16 [8, 1024, 960], P('wa', 'ctx')
- grad_query: float32 [960, 960], P('wa')
- grad_key: float32 [960, 320], P('wa')
- grad_value: float32 [960, 320], P('wa')
- grad_out: float32 [960, 960], P('wa')
- grad_gate: float32 [960, 2560], P('wa')
- grad_up: float32 [960, 2560], P('wa')
- grad_down: float32 [2560, 960], P('wa')
- grad_norm_attn: float32 [960], P('wa')
- grad_norm_ffn: float32 [960], P('wa')
All inputs are finite; a program needn't handle non-finite values.
Results may differ from a plain program's by a relative error of at most 0.018.
Values may be sent and summed in bfloat16 or wider, within the bound.
No kernel may reach another device: no remote copies, remote signals or barrier semaphores. Data moves between devices by JAX's collectives and lax.ppermute only.
A program may use at most 192 MiB of HBM per device.

v0:
```python
import jax
import jax.numpy as jnp
from jax import lax
from jax.sharding import PartitionSpec as P

HEAD = 64
KEYB = 512


epsilon = 1e-05


def for_sending(array):

    def short(part):
        return part.astype(jnp.bfloat16) if part.dtype == jnp.float32 else part

    return jax.tree.map(short, array)


def rms_scale(values_in, gain_vec):
    return (
        values_in
        * lax.rsqrt(jnp.mean(values_in * values_in, axis=-1, keepdims=True) + epsilon)
        * gain_vec
    )


def rotate(values_in, position):
    half_size = values_in.shape[-1] // 2
    frequency = 10000.0 ** (-jnp.arange(half_size).astype(jnp.float32) / half_size)
    angles = position[:, None] * frequency[None, :]
    cosines = jnp.cos(angles)[:, None, :]
    sines = jnp.sin(angles)[:, None, :]
    front_half = values_in[..., :half_size]
    back_half = values_in[..., half_size:]
    return jnp.concatenate(
        [front_half * cosines - back_half * sines, back_half * cosines + front_half * sines],
        axis=-1,
    )


def swiglu(gate, up_part):
    return jax.nn.silu(gate) * up_part


def make_scores(query_b, all_keys, all_values, row_places, groups):
    score_scale = HEAD ** (-0.5)

    def block_scores(block_index):
        block_start = block_index * KEYB
        key_block = lax.dynamic_slice_in_dim(all_keys, block_start, KEYB, 0).reshape(
            KEYB, groups, HEAD
        )
        value_block = lax.dynamic_slice_in_dim(all_values, block_start, KEYB, 0).reshape(
            KEYB, groups, HEAD
        )
        raw_score = (
            jnp.einsum("tgrd,kgd->tgrk", query_b, key_block, preferred_element_type=jnp.float32)
            * score_scale
        )
        key_places = block_start + jnp.arange(KEYB, dtype=jnp.int32)
        allowed = (key_places[None, :] <= row_places[:, None])[:, None, None, :]
        return (raw_score, allowed, block_start, key_block, value_block)

    return block_scores


def forward_pass(source, weights, row_places, position, last_block):
    (
        full_query,
        full_key,
        full_value,
        full_out,
        full_gate,
        full_up,
        full_down,
        full_gain1,
        full_gain2,
    ) = weights
    rows_here = source.shape[0]
    num_heads = full_query.shape[1] // HEAD
    groups = full_key.shape[1] // HEAD
    per_group = num_heads // groups
    normed = rms_scale(source, full_gain1.astype(jnp.float32))
    normed_b = normed.astype(jnp.bfloat16)
    query_raw = jnp.dot(normed_b, full_query, preferred_element_type=jnp.float32).reshape(
        rows_here, num_heads, HEAD
    )
    query_b = (
        rotate(query_raw, position).astype(jnp.bfloat16).reshape(rows_here, groups, per_group, HEAD)
    )
    key_raw = jnp.dot(normed_b, full_key, preferred_element_type=jnp.float32).reshape(
        rows_here, groups, HEAD
    )
    key_b = rotate(key_raw, position).astype(jnp.bfloat16).reshape(rows_here, groups * HEAD)
    value_b = jnp.dot(normed_b, full_value, preferred_element_type=jnp.float32).astype(jnp.bfloat16)
    all_keys, all_values = (
        lax.all_gather(key_b, "ctx", axis=0, tiled=True),
        lax.all_gather(value_b, "ctx", axis=0, tiled=True),
    )
    block_scores = make_scores(query_b, all_keys, all_values, row_places, groups)

    def total_step(block_index, running):
        row_max, row_sum = running
        raw_score, allowed, block_start, key_block, value_block = block_scores(block_index)
        masked = jnp.where(allowed, raw_score, -1e30)
        new_max = jnp.maximum(row_max, jnp.max(masked, axis=-1, keepdims=True))
        row_sum = row_sum * jnp.exp(row_max - new_max) + jnp.sum(
            jnp.exp(masked - new_max), axis=-1, keepdims=True
        )
        return (new_max, row_sum)

    stat_shape = (rows_here, groups, per_group, 1)
    row_max, row_sum = lax.fori_loop(
        0,
        last_block,
        total_step,
        (jnp.full(stat_shape, -1e30, jnp.float32), jnp.zeros(stat_shape, jnp.float32)),
    )
    log_total = row_max + jnp.log(row_sum)

    def value_step(block_index, accum):
        raw_score, allowed, block_start, key_block, value_block = block_scores(block_index)
        softmax_b = jnp.where(allowed, jnp.exp(raw_score - log_total), 0.0).astype(jnp.bfloat16)
        return accum + jnp.einsum(
            "tgrk,kgd->tgrd", softmax_b, value_block, preferred_element_type=jnp.float32
        )

    attended = lax.fori_loop(
        0, last_block, value_step, jnp.zeros((rows_here, groups, per_group, HEAD), jnp.float32)
    )
    heads_out = attended.reshape(rows_here, num_heads * HEAD).astype(jnp.bfloat16)
    resid_mid = source + jnp.dot(heads_out, full_out, preferred_element_type=jnp.float32)
    normed_two = rms_scale(resid_mid, full_gain2.astype(jnp.float32)).astype(jnp.bfloat16)
    gate = jnp.dot(normed_two, full_gate, preferred_element_type=jnp.float32)
    up_part = jnp.dot(normed_two, full_up, preferred_element_type=jnp.float32)
    activated = swiglu(gate, up_part).astype(jnp.bfloat16)
    mixed_out = (
        resid_mid + jnp.dot(activated, full_down, preferred_element_type=jnp.float32)
    ).astype(jnp.bfloat16)
    return {
        "source": source,
        "normed_b": normed_b,
        "query_raw": query_raw,
        "query_b": query_b,
        "key_raw": key_raw,
        "key_b": key_b,
        "value_b": value_b,
        "all_keys": all_keys,
        "all_values": all_values,
        "log_total": log_total,
        "attended": attended,
        "heads_out": heads_out,
        "resid_mid": resid_mid,
        "normed_two": normed_two,
        "gate": gate,
        "up_part": up_part,
        "activated": activated,
        "mixed": mixed_out,
    }


def backward_pass(state, grad_output, back_weights, row_places, position, last_block):
    (
        back_query,
        back_key,
        back_value,
        back_out,
        back_gate,
        back_up,
        back_down,
        back_gain1,
        back_gain2,
    ) = back_weights
    source = state["source"]
    normed_b = state["normed_b"]
    query_raw = state["query_raw"]
    query_b = state["query_b"]
    key_raw = state["key_raw"]
    all_keys = state["all_keys"]
    log_total = state["log_total"]
    attended = state["attended"]
    heads_out = state["heads_out"]
    resid_mid = state["resid_mid"]
    normed_two = state["normed_two"]
    gate = state["gate"]
    up_part = state["up_part"]
    activated = state["activated"]
    rows_here = source.shape[0]
    num_heads = back_query.shape[1] // HEAD
    groups = back_key.shape[1] // HEAD
    per_group = num_heads // groups
    score_scale = HEAD ** (-0.5)
    block_scores = make_scores(query_b, all_keys, state["all_values"], row_places, groups)
    grad_down = jnp.einsum("tf,td->fd", activated, grad_output, preferred_element_type=jnp.float32)
    d_activated = jnp.einsum(
        "td,fd->tf", grad_output, back_down, preferred_element_type=jnp.float32
    )
    unused_value, swiglu_back = jax.vjp(swiglu, gate, up_part)
    d_gate, d_up = swiglu_back(d_activated)
    d_gate_b = d_gate.astype(jnp.bfloat16)
    d_up_b = d_up.astype(jnp.bfloat16)
    grad_gate = jnp.einsum("td,tf->df", normed_two, d_gate_b, preferred_element_type=jnp.float32)
    grad_up = jnp.einsum("td,tf->df", normed_two, d_up_b, preferred_element_type=jnp.float32)
    d_normed_two = jnp.einsum("tf,df->td", d_gate_b, back_gate, preferred_element_type=jnp.float32)
    d_normed_two = d_normed_two + jnp.einsum(
        "tf,df->td", d_up_b, back_up, preferred_element_type=jnp.float32
    )
    unused_norm, norm_two_back = jax.vjp(rms_scale, resid_mid, back_gain2.astype(jnp.float32))
    d_resid_norm, grad_norm_ffn = norm_two_back(d_normed_two)
    d_resid = grad_output.astype(jnp.float32) + d_resid_norm
    d_resid_b = d_resid.astype(jnp.bfloat16)
    grad_out = jnp.einsum("tc,td->cd", heads_out, d_resid_b, preferred_element_type=jnp.float32)
    d_heads_b = jnp.einsum(
        "td,cd->tc", d_resid_b, back_out, preferred_element_type=jnp.float32
    ).astype(jnp.bfloat16)
    d_heads = d_heads_b.reshape(rows_here, groups, per_group, HEAD)
    row_delta = jnp.sum(d_heads.astype(jnp.float32) * attended, axis=-1, keepdims=True)
    grad_shape = (rows_here, groups, per_group, HEAD)

    def query_grad_terms(block_index):
        raw_score, allowed, block_start, key_block, value_block = block_scores(block_index)
        softmax_p = jnp.where(allowed, jnp.exp(raw_score - log_total), 0.0)
        d_softmax = jnp.einsum(
            "tgrd,kgd->tgrk", d_heads, value_block, preferred_element_type=jnp.float32
        )
        d_score_b = (softmax_p * (d_softmax - row_delta)).astype(jnp.bfloat16)
        d_query_add = (
            jnp.einsum("tgrk,kgd->tgrd", d_score_b, key_block, preferred_element_type=jnp.float32)
            * score_scale
        )
        return (softmax_p, d_score_b, d_query_add, block_start)

    def grad_step(block_index, running):
        d_query, key_terms, value_terms = running
        softmax_p, d_score_b, d_query_add, block_start = query_grad_terms(block_index)
        d_key = (
            jnp.einsum("tgrk,tgrd->kgd", d_score_b, query_b, preferred_element_type=jnp.float32)
            * score_scale
        )
        d_value = jnp.einsum(
            "tgrk,tgrd->kgd",
            softmax_p.astype(jnp.bfloat16),
            d_heads,
            preferred_element_type=jnp.float32,
        )
        key_terms = lax.dynamic_update_slice_in_dim(
            key_terms, d_key.reshape(KEYB, groups * HEAD), block_start, 0
        )
        value_terms = lax.dynamic_update_slice_in_dim(
            value_terms, d_value.reshape(KEYB, groups * HEAD), block_start, 0
        )
        return (d_query + d_query_add, key_terms, value_terms)

    term_shape = (all_keys.shape[0], groups * HEAD)
    d_query, key_terms, value_terms = lax.fori_loop(
        0,
        last_block,
        grad_step,
        (
            jnp.zeros(grad_shape, jnp.float32),
            jnp.zeros(term_shape, jnp.float32),
            jnp.zeros(term_shape, jnp.float32),
        ),
    )
    key_grad, value_grad = (
        lax.psum_scatter(key_terms, "ctx", scatter_dimension=0, tiled=True),
        lax.psum_scatter(value_terms, "ctx", scatter_dimension=0, tiled=True),
    )
    unused_query, query_turn_back = jax.vjp(lambda turned: rotate(turned, position), query_raw)
    d_query_b = (
        query_turn_back(d_query.reshape(rows_here, num_heads, HEAD))[0]
        .reshape(rows_here, num_heads * HEAD)
        .astype(jnp.bfloat16)
    )
    unused_key, key_turn_back = jax.vjp(lambda turned: rotate(turned, position), key_raw)
    d_key_b = (
        key_turn_back(key_grad.reshape(rows_here, groups, HEAD))[0]
        .reshape(rows_here, groups * HEAD)
        .astype(jnp.bfloat16)
    )
    d_value_b = value_grad.astype(jnp.bfloat16)
    grad_query = jnp.einsum("td,tc->dc", normed_b, d_query_b, preferred_element_type=jnp.float32)
    grad_key = jnp.einsum("td,tc->dc", normed_b, d_key_b, preferred_element_type=jnp.float32)
    grad_value = jnp.einsum("td,tc->dc", normed_b, d_value_b, preferred_element_type=jnp.float32)
    d_normed = jnp.einsum("tc,dc->td", d_query_b, back_query, preferred_element_type=jnp.float32)
    d_normed = d_normed + jnp.einsum(
        "tc,dc->td", d_key_b, back_key, preferred_element_type=jnp.float32
    )
    d_normed = d_normed + jnp.einsum(
        "tc,dc->td", d_value_b, back_value, preferred_element_type=jnp.float32
    )
    unused_first, norm_one_back = jax.vjp(rms_scale, source, back_gain1.astype(jnp.float32))
    d_source_norm, grad_norm_attn = norm_one_back(d_normed)
    input_grad = (d_resid + d_source_norm).astype(jnp.bfloat16)
    gradients = (
        grad_query,
        grad_key,
        grad_value,
        grad_out,
        grad_gate,
        grad_up,
        grad_down,
        grad_norm_attn,
        grad_norm_ffn,
    )
    return (input_grad, gradients)


def local(
    tokens, w_query, w_key, w_value, w_out, w_gate, w_up, w_down, norm_attn, norm_ffn, cotangent
):
    shards = (w_query, w_key, w_value, w_out, w_gate, w_up, w_down, norm_attn, norm_ffn)
    gathered = (
        lax.all_gather(shards[0], "wa", axis=0, tiled=True),
        lax.all_gather(shards[1], "wa", axis=0, tiled=True),
        lax.all_gather(shards[2], "wa", axis=0, tiled=True),
        lax.all_gather(shards[3], "wa", axis=0, tiled=True),
        lax.all_gather(shards[4], "wa", axis=0, tiled=True),
        lax.all_gather(shards[5], "wa", axis=0, tiled=True),
        lax.all_gather(shards[6], "wa", axis=0, tiled=True),
        lax.all_gather(shards[7], "wa", axis=0, tiled=True),
        lax.all_gather(shards[8], "wa", axis=0, tiled=True),
    )
    seq_count = tokens.shape[0]
    rows_here = tokens.shape[1]
    offset_rows = lax.axis_index("ctx") * rows_here
    row_places = offset_rows + jnp.arange(rows_here, dtype=jnp.int32)
    position = row_places.astype(jnp.float32)
    last_block = (offset_rows + rows_here + KEYB - 1) // KEYB
    states = [
        forward_pass(tokens[index].astype(jnp.float32), gathered, row_places, position, last_block)
        for index in range(seq_count)
    ]
    mixed_out = jnp.stack([state["mixed"] for state in states])
    back_weights = (
        lax.all_gather(shards[0], "wa", axis=0, tiled=True),
        lax.all_gather(shards[1], "wa", axis=0, tiled=True),
        lax.all_gather(shards[2], "wa", axis=0, tiled=True),
        lax.all_gather(shards[3], "wa", axis=0, tiled=True),
        lax.all_gather(shards[4], "wa", axis=0, tiled=True),
        lax.all_gather(shards[5], "wa", axis=0, tiled=True),
        lax.all_gather(shards[6], "wa", axis=0, tiled=True),
        lax.all_gather(shards[7], "wa", axis=0, tiled=True),
        lax.all_gather(shards[8], "wa", axis=0, tiled=True),
    )
    input_grads = []
    totals = None
    for index in range(seq_count):
        input_grad, gradients = backward_pass(
            states[index], cotangent[index], back_weights, row_places, position, last_block
        )
        input_grads.append(input_grad)
        if totals is None:
            totals = gradients
        else:
            totals = tuple((left + right for left, right in zip(totals, gradients)))
    owned = jax.tree.map(
        lambda part: part.astype(jnp.float32),
        lax.psum_scatter(for_sending(totals), "wa", scatter_dimension=0, tiled=True),
    )
    summed = lax.psum(owned, "ctx")
    return (
        mixed_out,
        jnp.stack(input_grads),
        summed[0],
        summed[1],
        summed[2],
        summed[3],
        summed[4],
        summed[5],
        summed[6],
        summed[7],
        summed[8],
    )


def solution(mesh):
    in_specs = (
        P("wa", "ctx", None),
        P("wa", None),
        P("wa", None),
        P("wa", None),
        P("wa", None),
        P("wa", None),
        P("wa", None),
        P("wa", None),
        P("wa"),
        P("wa"),
        P("wa", "ctx", None),
    )
    out_specs = (
        P("wa", "ctx", None),
        P("wa", "ctx", None),
        P("wa", None),
        P("wa", None),
        P("wa", None),
        P("wa", None),
        P("wa", None),
        P("wa", None),
        P("wa", None),
        P("wa"),
        P("wa"),
    )
    return jax.shard_map(local, mesh=mesh, in_specs=in_specs, out_specs=out_specs, check_vma=False)
```

profile of v0, /device:TPU:0, one launch (start us, length us, event | category | flops | bytes accessed | tf_op | source)
XLA Modules:
  0.0 1190.1 jit_solution(10273332246935910379)
XLA Ops:
  12.5 8.3 all-reduce.14
  21.0 11.4 all-gather.1
  34.4 8.0 all-gather
  44.7 28.8 %all_gather.52 = bf16[1024,320]{0,1:T(8,128)(2,1)S(1)} all-gather(bf16[128,320]{0,1:T(8,128)(2,1)S(1)} %bitcast.613), channel_id=1, replica_groups=mesh['ctx'=8,'wa'=4] {'ctx'}, dimensions={0}, use_global_device_ids=true | all-gather | bytes 737280 | tf_op jit(solution)/shard_map/all_gather | solution.py:99
  73.5 29.4 %all_gather.50 = bf16[1024,320]{0,1:T(8,128)(2,1)} all-gather(bf16[128,320]{0,1:T(8,128)(2,1)S(1)} %convolution_convert_fusion.3), channel_id=1, replica_groups=mesh['ctx'=8,'wa'=4] {'ctx'}, dimensions={0}, use_global_device_ids=true | all-gather | bytes 737280 | tf_op jit(solution)/shard_map/all_gather | solution.py:100
  102.9 27.4 %all_gather.60 = bf16[1024,320]{0,1:T(8,128)(2,1)S(1)} all-gather(bf16[128,320]{0,1:T(8,128)(2,1)S(1)} %bitcast.614), channel_id=1, replica_groups=mesh['ctx'=8,'wa'=4] {'ctx'}, dimensions={0}, use_global_device_ids=true | all-gather | bytes 737280 | tf_op jit(solution)/shard_map/all_gather | solution.py:99
  130.2 28.0 %all_gather.59 = bf16[1024,320]{0,1:T(8,128)(2,1)S(1)} all-gather(bf16[128,320]{0,1:T(8,128)(2,1)S(1)} %convolution_convert_fusion.2), channel_id=1, replica_groups=mesh['ctx'=8,'wa'=4] {'ctx'}, dimensions={0}, use_global_device_ids=true | all-gather | bytes 737280 | tf_op jit(solution)/shard_map/all_gather | solution.py:100
  158.2 3.8 copy.54
  162.1 2.4 fusion.111
  164.5 2.3 fusion.117
  167.7 1.9 while.78
  169.7 1.9 while.80
  172.4 5.3 while.79
  174.6 3.1 fusion.308
  180.3 4.0 while.81
  181.3 3.1 fusion.315
  186.1 2.6 multiply_reduce_fusion.7
  188.7 3.5 multiply_reduce_fusion.6
  193.1 4.5 fusion.160
  197.6 4.5 fusion.161
  202.1 5.4 multiply_convert_fusion.1
  207.5 4.3 fusion.164
  215.7 2.3 multiply_convert_fusion
  225.6 6.5 while.82
  232.1 2.3 convolution_convert_fusion
  238.0 6.2 while.83
  246.6 2.0 add_convert_fusion.3
  250.0 2.0 add_convert_fusion.4
  252.3 63.8 %reduce-scatter.20.cloned.1.call-done = f32[128,320]{0,1:T(8,128)} async-done(((f32[1024,320]{0,1:T(8,128)}), f32[128,320]{0,1:T(8,128)}) %reduce-scatter.20.cloned.1.call-update) | async-done | bytes 163856 | tf_op jit(solution)/shard_map/reduce_scatter | solution.py:269
  316.1 2.4 fusion.137
  318.6 64.8 %reduce-scatter.24.cloned.1.call-done = f32[128,320]{0,1:T(8,128)} async-done(((f32[1024,320]{0,1:T(8,128)}), f32[128,320]{0,1:T(8,128)}) %reduce-scatter.24.cloned.1.call-update) | async-done | bytes 163856 | tf_op jit(solution)/shard_map/reduce_scatter | solution.py:269
  386.5 64.2 %reduce-scatter.18.cloned.1.call-done = f32[128,320]{0,1:T(8,128)} async-done(((f32[1024,320]{0,1:T(8,128)}), f32[128,320]{0,1:T(8,128)}) %reduce-scatter.18.cloned.1.call-update) | async-done | bytes 163856 | tf_op jit(solution)/shard_map/reduce_scatter | solution.py:268
  450.7 68.0 %reduce-scatter.22.cloned.1.call-done = f32[128,320]{0,1:T(8,128)} async-done(((f32[1024,320]{0,1:T(8,128)}), f32[128,320]{0,1:T(8,128)}) %reduce-scatter.22.cloned.1.call-update) | async-done | bytes 163856 | tf_op jit(solution)/shard_map/reduce_scatter | solution.py:268
  523.6 3.7 add_convert_fusion
  527.2 8.0 copy.81
  537.9 3.7 add_convert_fusion.1
  544.1 3.6 add_convert_fusion.2
  548.9 3.9 fusion.71
  552.9 4.0 fusion.70
  561.2 5.7 all-reduce.13
  568.1 17.2 %reduce-scatter.26.cloned.1.call-done = bf16[240,960]{1,0:T(8,128)(2,1)} async-done(((bf16[960,960]{1,0:T(8,128)(2,1)}), bf16[240,960]{1,0:T(8,128)(2,1)}) %reduce-scatter.26.cloned.1.call-update) | async-done | bytes 460816 | tf_op jit(solution)/shard_map/reduce_scatter | solution.py:361
  585.3 26.0 %reduce-scatter.36.cloned.1.call-done = bf16[240,320]{1,0:T(8,128)(2,1)} async-done(((bf16[960,320]{1,0:T(8,128)(2,1)}), bf16[240,320]{1,0:T(8,128)(2,1)}) %reduce-scatter.36.cloned.1.call-update) | async-done | bytes 153616
  612.3 25.2 %reduce-scatter.34.cloned.1.call-done = bf16[240,320]{1,0:T(8,128)(2,1)} async-done(((bf16[960,320]{1,0:T(8,128)(2,1)}), bf16[240,320]{1,0:T(8,128)(2,1)}) %reduce-scatter.34.cloned.1.call-update) | async-done | bytes 153616
  638.5 52.8 %reduce-scatter.38.cloned.1.call-done = bf16[640,960]{1,0:T(8,128)(2,1)} async-done(((bf16[2560,960]{1,0:T(8,128)(2,1)}), bf16[640,960]{1,0:T(8,128)(2,1)}) %reduce-scatter.38.cloned.1.call-update) | async-done | bytes 1228816
  691.3 2.1 copy.82
  693.4 49.7 %reduce-scatter.32.cloned.1.call-done = bf16[240,2560]{1,0:T(8,128)(2,1)} async-done(((bf16[960,2560]{1,0:T(8,128)(2,1)}), bf16[240,2560]{1,0:T(8,128)(2,1)}) %reduce-scatter.32.cloned.1.call-update) | async-done | bytes 1228816 | tf_op jit(solution)/shard_map/reduce_scatter | solution.py:361
  743.2 51.7 %reduce-scatter.30.cloned.1.call-done = bf16[240,2560]{1,0:T(8,128)(2,1)} async-done(((bf16[960,2560]{1,0:T(8,128)(2,1)}), bf16[240,2560]{1,0:T(8,128)(2,1)}) %reduce-scatter.30.cloned.1.call-update) | async-done | bytes 1228816 | tf_op jit(solution)/shard_map/reduce_scatter | solution.py:361
  794.8 388.2 %all-reduce.16 = (f32[240,960]{1,0:T(8,128)}, f32[240,320]{0,1:T(8,128)}, f32[240,320]{0,1:T(8,128)}, f32[240,960]{1,0:T(8,128)}, f32[240,2560]{1,0:T(8,128)}, /...) all-reduce(bf16[240,960]{1,0:T(8,128)(2,1)} %reduce-scatter.26.clon, ...), channel_id=1, replica_groups=mesh['ctx'=8,'wa'=4] {'ctx'}, use_global_device_ids=true, to_apply=%region_31.32 | all-reduce | flops 2458080 | bytes 14749440 | tf_op jit(solution)/shard_map/psum | solution.py:363
  (334 shorter events, 74.3 us)
Async XLA Ops:
  7.2 3.6 copy-start.68
  7.2 4.8 copy-start.73
  7.2 5.0 copy-start.74
  7.2 13.6 %copy-start.2 = (bf16[2,128,960]{1,2,0:T(8,128)(2,1)S(1)}, bf16[2,128,960]{1,2,0:T(8,128)(2,1)}, u32[]{:S(2)}) copy-start(bf16[2,128,960]{1,2,0:T(8,128)(2,1)} %param.23) | copy-start | bytes 1474564
  7.2 13.8 %copy-start.62 = (bf16[240,320]{0,1:T(8,128)(2,1)S(1)}, bf16[240,320]{0,1:T(8,128)(2,1)}, u32[]{:S(2)}) copy-start(bf16[240,320]{0,1:T(8,128)(2,1)} %param.25) | copy-start | bytes 460804
  7.2 151.0 %all-gather.8.cloned.1.call-start = ((), (), s32[]{:S(2)}) async-start(), calls=%async_computation.11 | async-start | bytes 2457600 | tf_op jit(solution)/shard_map/all_gather | solution.py:316
  8.0 178.1 %all-gather.10.cloned.1.call-start = ((), (), s32[]{:S(2)}) async-start(), calls=%async_computation.12 | async-start | bytes 2457600 | tf_op jit(solution)/shard_map/all_gather | solution.py:319
  8.7 184.4 %all-gather.12.cloned.1.call-start = ((), (), s32[]{:S(2)}) async-start(), calls=%async_computation.13 | async-start | bytes 6144000 | tf_op jit(solution)/shard_map/all_gather | solution.py:320
  9.4 188.1 %all-gather.14.cloned.1.call-start = ((), (), s32[]{:S(2)}) async-start(), calls=%async_computation.14 | async-start | bytes 6144000 | tf_op jit(solution)/shard_map/all_gather | solution.py:321
  10.0 24.4 %copy-start.63 = (bf16[240,320]{0,1:T(8,128)(2,1)S(1)}, bf16[240,320]{0,1:T(8,128)(2,1)}, u32[]{:S(2)}) copy-start(bf16[240,320]{0,1:T(8,128)(2,1)} %param.26) | copy-start | bytes 460804
  10.0 192.0 %all-gather.16.cloned.1.call-start = ((), (), s32[]{:S(2)}) async-start(), calls=%async_computation.15 | async-start | bytes 6144000 | tf_op jit(solution)/shard_map/all_gather | solution.py:322
  10.6 305.5 %reduce-scatter.20.cloned.1.call-start = ((), (), s32[]{:S(2)}) async-start(), calls=%async_computation.17 | async-start | bytes 1474560 | tf_op jit(solution)/shard_map/reduce_scatter | solution.py:269
  20.8 143.7 %copy-start.54 = (f32[960]{0:T(1024)}, f32[960]{0:T(1024)S(1)}, u32[]{:S(2)}) copy-start(f32[960]{0:T(1024)S(1)} %convert_element_type.279) | copy-start | bytes 11524
  21.0 22.5 %copy-start.69 = (f32[128]{0:T(128)}, f32[128]{0:T(128)S(1)}, u32[]{:S(2)}) copy-start(f32[128]{0:T(128)S(1)} %get-tuple-element.491) | copy-start | bytes 1540
  21.0 22.5 %copy-start.71 = (f32[128]{0:T(128)}, f32[128]{0:T(128)S(1)}, u32[]{:S(2)}) copy-start(f32[128]{0:T(128)S(1)} %get-tuple-element.492) | copy-start | bytes 1540
  21.0 141.1 %copy-start.64 = (f32[128]{0:T(128)}, f32[128]{0:T(128)S(1)}, u32[]{:S(2)}) copy-start(f32[128]{0:T(128)S(1)} %fusion.147) | copy-start | bytes 1540
  21.0 143.5 %copy-start.66 = (f32[128]{0:T(128)}, f32[128]{0:T(128)S(1)}, u32[]{:S(2)}) copy-start(f32[128]{0:T(128)S(1)} %fusion.145) | copy-start | bytes 1540
  33.5 10.9 copy-start.15
  44.6 122.2 %copy-start.58 = (f32[128,32]{0,1:T(8,128)}, f32[128,32]{0,1:T(8,128)S(1)}, u32[]{:S(2)}) copy-start(f32[128,32]{0,1:T(8,128)S(1)} %get-tuple-element.661) | copy-start | bytes 49156
  44.6 122.2 %copy-start.60 = (f32[128,32]{0,1:T(8,128)}, f32[128,32]{0,1:T(8,128)S(1)}, u32[]{:S(2)}) copy-start(f32[128,32]{0,1:T(8,128)S(1)} %get-tuple-element.662) | copy-start | bytes 49156
  188.7 32.3 %copy-start.5 = (f32[128,960]{0,1:T(8,128)}, f32[128,960]{0,1:T(8,128)S(1)}, u32[]{:S(2)}) copy-start(f32[128,960]{0,1:T(8,128)S(1)} %get-tuple-element.666) | copy-start | bytes 1474564
  207.5 4.3 copy-start.34
  207.5 6.0 copy-start.28
  207.5 4.4 copy-start
  207.5 4.4 copy-start.7
  207.5 6.9 slice-start
  212.0 3.4 slice-start.2
  235.5 147.9 %reduce-scatter.24.cloned.1.call-start = ((), (), s32[]{:S(2)}) async-start(), calls=%async_computation.19 | async-start | bytes 1474560 | tf_op jit(solution)/shard_map/reduce_scatter | solution.py:269
  244.3 206.3 %reduce-scatter.18.cloned.1.call-start = ((), (), s32[]{:S(2)}) async-start(), calls=%async_computation.16 | async-start | bytes 1474560 | tf_op jit(solution)/shard_map/reduce_scatter | solution.py:268
  245.1 273.6 %reduce-scatter.22.cloned.1.call-start = ((), (), s32[]{:S(2)}) async-start(), calls=%async_computation.18 | async-start | bytes 1474560 | tf_op jit(solution)/shard_map/reduce_scatter | solution.py:268
  245.8 322.3 %reduce-scatter.28.cloned.1.call-start = ((), (), s32[]{:S(2)}) async-start(), calls=%async_computation.21 | async-start | bytes 2457600 | tf_op jit(solution)/shard_map/reduce_scatter | solution.py:361
  248.6 336.7 %reduce-scatter.26.cloned.1.call-start = ((), (), s32[]{:S(2)}) async-start(), calls=%async_computation.20 | async-start | bytes 2457600 | tf_op jit(solution)/shard_map/reduce_scatter | solution.py:361
  252.0 359.2 %reduce-scatter.36.cloned.1.call-start = ((), (), s32[]{:S(2)}) async-start(), calls=%async_computation.25 | async-start | bytes 921600
  386.4 135.7 %copy-start.30 = (bf16[128,2560]{1,0:T(8,128)(2,1)S(1)}, bf16[128,2560]{1,0:T(8,128)(2,1)}, u32[]{:S(2)}) copy-start(bf16[128,2560]{1,0:T(8,128)(2,1)} %get-tuple-element.628) | copy-start | bytes 1966084
  386.4 135.7 %copy-start.41 = (bf16[2,128,960]{1,2,0:T(8,128)(2,1)S(1)}, bf16[2,128,960]{1,2,0:T(8,128)(2,1)}, u32[]{:S(2)}) copy-start(bf16[2,128,960]{1,2,0:T(8,128)(2,1)} %param.33) | copy-start | bytes 1474564
  386.4 251.1 %reduce-scatter.34.cloned.1.call-start = ((), (), s32[]{:S(2)}) async-start(), calls=%async_computation.24 | async-start | bytes 921600
  522.0 169.3 %reduce-scatter.38.cloned.1.call-start = ((), (), s32[]{:S(2)}) async-start(), calls=%async_computation.26 | async-start | bytes 6553600
  535.3 207.9 %reduce-scatter.32.cloned.1.call-start = ((), (), s32[]{:S(2)}) async-start(), calls=%async_computation.23 | async-start | bytes 6144000 | tf_op jit(solution)/shard_map/reduce_scatter | solution.py:361
  541.6 253.3 %reduce-scatter.30.cloned.1.call-start = ((), (), s32[]{:S(2)}) async-start(), calls=%async_computation.22 | async-start | bytes 6144000 | tf_op jit(solution)/shard_map/reduce_scatter | solution.py:361
  547.7 5.1 copy-start.8
  548.9 3.9 copy-start.33
  552.8 4.9 copy-start.16
  552.8 4.9 copy-start.49
  552.8 5.3 copy-start.51
  552.9 5.7 copy-start.18
  552.9 5.7 copy-start.53
  559.5 7.4 copy-start.70
  559.5 7.4 copy-start.72
  (47 other events, 79.0 us)
Sparse Core Ops, SparseCore 0:
  9.6 28.0 all-gather.7
  39.3 21.8 all-gather.9
  62.7 38.6 all-gather.11
  102.8 38.5 all-gather.13
  142.8 38.5 all-gather.15
  235.6 80.4 reduce-scatter.19
  319.5 63.7 reduce-scatter.23
  386.8 63.8 reduce-scatter.17
  454.7 63.9 reduce-scatter.21
  521.7 29.5 reduce-scatter.27
  554.6 30.6 reduce-scatter.25
  588.2 22.9 reduce-scatter.35
  614.5 22.9 reduce-scatter.33
  639.9 51.3 reduce-scatter.37
  693.9 49.1 reduce-scatter.31
  745.6 49.1 reduce-scatter.29
where the time goes:
time: 1200 us; the launch traced here: 1190 us
  blocking collectives  535 us (45%)
  waiting for transfers between devices  488 us (41%)
  matrix products  95.9 us (8%)
  local copies, waits for them, and re-layouts  38 us (3%)
  between operations  17 us (1%)
  other arithmetic  13.9 us (1%)
    psum x1, blocking collectives, local(): summed = lax.psum(owned, 'ctx')  388 us
    reduce_scatter x2, waiting for transfers between devices, backward_pass(): lax.psum_scatter(key_terms, 'ctx', scatter_dimension=0, tiled=True)  132 us
    reduce_scatter x2, waiting for transfers between devices, backward_pass(): lax.psum_scatter(value_terms, 'ctx', scatter_dimension=0, tiled=True)  129 us
    reduce_scatter x4, waiting for transfers between devices, local(): lax.psum_scatter(for_sending(totals), 'wa', scatter_dimension=0, tiled=True)  119 us
    unnamed x19, waiting for transfers between devices  109 us
    all_gather x2, blocking collectives, forward_pass(): lax.all_gather(value_b, 'ctx', axis=0, tiled=True)  57.4 us
    all_gather x2, blocking collectives, forward_pass(): lax.all_gather(key_b, 'ctx', axis=0, tiled=True)  56.2 us
  transfers between devices with their start and end apart: 16, of which 10 were waited for; matrix products, arithmetic and copies ran while one was open for 9% of the time, Pallas kernels for 0%

commit v1 on v0

v1 whole, which is shorter than its diff:
```python
import functools

import jax
import jax.numpy as jnp
from jax import lax
from jax.experimental import pallas as pl
from jax.experimental.pallas import tpu as pltpu
from jax.sharding import PartitionSpec as P

HEAD = 64
EPS = 1e-05
BF = jnp.bfloat16
F32 = jnp.float32
VMEM_LIMIT = 60 * 1024 * 1024


def mm(a, b, ca, cb):
    return lax.dot_general(a, b, (((ca,), (cb,)), ((), ())), preferred_element_type=F32)


def bits_of(n):
    return max(n - 1, 0).bit_length()


def swap(a, axis, n, bit):
    return lax.ppermute(a, axis, [(i, i ^ (1 << bit)) for i in range(n)])


def my_bit(axis, bit):
    return (lax.axis_index(axis) >> bit) & 1


def ordered(mine, theirs, bit, dim):
    return jnp.where(
        bit == 0,
        jnp.concatenate([mine, theirs], axis=dim),
        jnp.concatenate([theirs, mine], axis=dim),
    )


def gather_rows(a, n):
    nb = bits_of(n)
    out = a.reshape((1,) * nb + a.shape)
    for bit in reversed(range(nb)):
        dim = nb - 1 - bit
        out = ordered(out, swap(out, "wa", n, bit), my_bit("wa", bit), dim)
    return out.reshape((n,) + a.shape)


def gather_relative(a, n):
    blocks = {0: a}
    for bit in reversed(range(bits_of(n))):
        for place in list(blocks):
            blocks[place | (1 << bit)] = swap(blocks[place], "wa", n, bit)
    return jnp.concatenate(list(blocks.values()), axis=0)


def scatter_relative(a, n):
    for bit in range(bits_of(n)):
        half = a.shape[0] // 2
        a = a[:half] + swap(a[half:].astype(BF), "wa", n, bit).astype(F32)
    return a


def scatter_rows(a, n):
    nb = bits_of(n)
    a = a.reshape((2,) * nb + a.shape[1:])
    for bit in range(nb):
        dim = nb - 1 - bit
        mine = my_bit("wa", bit)
        keep = lax.dynamic_slice_in_dim(a, mine, 1, dim)
        send = lax.dynamic_slice_in_dim(a, 1 - mine, 1, dim).astype(BF)
        a = (keep.astype(F32) + swap(send, "wa", n, bit).astype(F32)).astype(BF)
    return a.reshape(a.shape[nb:])


def exchange_blocks(take, n, place):
    me = lax.axis_index("wa")
    result = place(None, take(me), me)
    for step in range(1, n):
        got = lax.ppermute(take(me ^ step), "wa", [(i, i ^ step) for i in range(n)])
        result = place(result, got, me ^ step)
    return result


def reduce_halves(a, n, plan):
    trail = []
    for bit, dim in plan:
        size = a.shape[dim]
        half = -(-size // 16) * 8
        mine = my_bit("ctx", bit)
        if half >= size:
            got = swap(a.astype(BF), "ctx", n, bit)
            a = (a.astype(F32) + got.astype(F32)).astype(BF)
            trail.append((bit, dim, None))
            continue
        keep = lax.dynamic_slice_in_dim(a, mine * (size - half), half, dim)
        send = lax.dynamic_slice_in_dim(a, (1 - mine) * (size - half), half, dim).astype(BF)
        a = (keep.astype(F32) + swap(send, "ctx", n, bit).astype(F32)).astype(BF)
        trail.append((bit, dim, size))
    return a, trail


def gather_halves(a, n, trail):
    for bit, dim, size in reversed(trail):
        if size is None:
            continue
        got = swap(a, "ctx", n, bit)
        mine = my_bit("ctx", bit)
        if 2 * a.shape[dim] == size:
            a = ordered(a, got, mine, dim)
        else:
            low = jnp.where(mine == 0, a, got)
            high = jnp.where(mine == 0, got, a)
            extra = 2 * a.shape[dim] - size
            high = lax.slice_in_dim(high, extra, a.shape[dim], axis=dim)
            a = jnp.concatenate([low, high], axis=dim)
    return a


def all_reduce_ctx(a, n, plan):
    part, trail = reduce_halves(a, n, plan)
    return gather_halves(part, n, trail)


def doubled(a, n, order):
    for bit in order:
        a = jnp.concatenate([a, swap(a, "ctx", n, bit)], axis=0)
    return a


def halved(a, n, order):
    for bit in reversed(order):
        half = a.shape[0] // 2
        got = swap(a[half:], "ctx", n, bit)
        a = (a[:half].astype(F32) + got.astype(F32)).astype(BF if half > 1 else F32)
    return a


def slot_offsets(order):
    offsets = [0]
    for bit in order:
        offsets = offsets + [offset ^ (1 << bit) for offset in offsets]
    return offsets


def group_columns(ref, group, per_group):
    return jnp.concatenate(
        [
            ref[(group * per_group + r) * HEAD : (group * per_group + r + 1) * HEAD, :]
            for r in range(per_group)
        ],
        axis=1,
    )


def slot_columns(ref, first, count, row):
    return jnp.concatenate(
        [ref[first + s, row : row + HEAD, :] for s in range(count)], axis=1
    )


def attend_kernel(groups, per_group, chunk, q_ref, kv_ref, bias_ref, o_ref, lse_ref):
    rows = q_ref.shape[1]
    slots = kv_ref.shape[0]
    wide = per_group * rows
    for group in range(groups):
        q = group_columns(q_ref, group, per_group)

        def step(index, running):
            first = index * chunk
            k = slot_columns(kv_ref, first, chunk, group * HEAD)
            v = slot_columns(kv_ref, first, chunk, (groups + group) * HEAD)
            bias = bias_ref[pl.ds(first * rows, chunk * rows), :]
            s = mm(k, q, 0, 0) + jnp.concatenate([bias] * per_group, axis=1)
            top = jnp.max(s, axis=0, keepdims=True)
            if running is not None:
                top = jnp.maximum(top, running[0])
            p = jnp.exp(s - top)
            total = jnp.sum(p, axis=0, keepdims=True)
            out = mm(v, p.astype(BF), 1, 0)
            if running is not None:
                shrink = jnp.exp(running[0] - top)
                total = total + running[1] * shrink
                out = out + running[2] * shrink
            return (top, total, out)

        if slots == chunk:
            top, total, out = step(0, None)
        else:
            top, total, out = lax.fori_loop(
                0,
                slots // chunk,
                step,
                (
                    jnp.full((1, wide), -1e30, F32),
                    jnp.zeros((1, wide), F32),
                    jnp.zeros((HEAD, wide), F32),
                ),
            )
        out = out / total
        lse = top + jnp.log(total)
        for r in range(per_group):
            head = group * per_group + r
            o_ref[head * HEAD : (head + 1) * HEAD, :] = out[:, r * rows : (r + 1) * rows]
            lse_ref[head : head + 1, :] = lse[:, r * rows : (r + 1) * rows]


def attend_back_kernel(
    groups, per_group, chunk, q_ref, kv_ref, bias_ref, lse_ref, do_ref, o_ref, dq_ref, dkv_ref
):
    rows = q_ref.shape[1]
    slots = kv_ref.shape[0]
    wide = per_group * rows
    for group in range(groups):
        q = group_columns(q_ref, group, per_group)
        do = group_columns(do_ref, group, per_group)
        o = group_columns(o_ref, group, per_group)
        delta = jnp.sum(do.astype(F32) * o, axis=0, keepdims=True)
        lse = jnp.concatenate(
            [
                lse_ref[group * per_group + r : group * per_group + r + 1, :]
                for r in range(per_group)
            ],
            axis=1,
        )

        def step(index, dq):
            first = index * chunk
            k = slot_columns(kv_ref, first, chunk, group * HEAD)
            v = slot_columns(kv_ref, first, chunk, (groups + group) * HEAD)
            bias = bias_ref[pl.ds(first * rows, chunk * rows), :]
            s = mm(k, q, 0, 0) + jnp.concatenate([bias] * per_group, axis=1)
            p = jnp.exp(s - lse)
            dp = mm(v, do, 0, 0)
            ds = (p * (dp - delta)).astype(BF)
            dk = mm(q, ds, 1, 1).astype(BF)
            dv = mm(do, p.astype(BF), 1, 1).astype(BF)
            for s_index in range(chunk):
                columns = slice(s_index * rows, (s_index + 1) * rows)
                dkv_ref[first + s_index, group * HEAD : (group + 1) * HEAD, :] = dk[:, columns]
                dkv_ref[
                    first + s_index, (groups + group) * HEAD : (groups + group + 1) * HEAD, :
                ] = dv[:, columns]
            return dq + mm(k, ds, 1, 0)

        dq = jnp.zeros((HEAD, wide), F32)
        dq = step(0, dq) if slots == chunk else lax.fori_loop(0, slots // chunk, step, dq)
        dq = dq * HEAD ** (-0.5)
        for r in range(per_group):
            head = group * per_group + r
            dq_ref[head * HEAD : (head + 1) * HEAD, :] = dq[:, r * rows : (r + 1) * rows]


def attend(groups, per_group, q, kv, bias):
    rows, slots = q.shape[1], kv.shape[0]
    heads = groups * per_group
    cost = pl.CostEstimate(
        flops=4 * heads * HEAD * rows * rows * slots * 2,
        bytes_accessed=q.size * 6 + kv.size * 2 + bias.size * 4,
        transcendentals=heads * rows * rows * slots,
    )
    return pl.pallas_call(
        functools.partial(attend_kernel, groups, per_group, min(slots, 8)),
        out_shape=(
            jax.ShapeDtypeStruct(q.shape, F32),
            jax.ShapeDtypeStruct((heads, rows), F32),
        ),
        cost_estimate=cost,
        compiler_params=pltpu.CompilerParams(vmem_limit_bytes=VMEM_LIMIT),
    )(q, kv, bias)


def attend_back(groups, per_group, q, kv, bias, lse, do, o):
    rows, slots = q.shape[1], kv.shape[0]
    heads = groups * per_group
    cost = pl.CostEstimate(
        flops=10 * heads * HEAD * rows * rows * slots * 2,
        bytes_accessed=q.size * 12 + kv.size * 4 + bias.size * 4,
        transcendentals=heads * rows * rows * slots,
    )
    return pl.pallas_call(
        functools.partial(attend_back_kernel, groups, per_group, min(slots, 8)),
        out_shape=(
            jax.ShapeDtypeStruct(q.shape, F32),
            jax.ShapeDtypeStruct(kv.shape, BF),
        ),
        cost_estimate=cost,
        compiler_params=pltpu.CompilerParams(vmem_limit_bytes=VMEM_LIMIT),
    )(q, kv, bias, lse, do, o)


def rms(x, gain):
    r = lax.rsqrt(jnp.mean(x * x, axis=-1, keepdims=True) + EPS)
    return x * r * gain, r


def rms_back(dh, x, r, gain):
    xn = x * r
    d_gain = jnp.sum(dh * xn, axis=0)
    dxn = dh * gain
    return r * (dxn - xn * jnp.mean(dxn * xn, axis=-1, keepdims=True)), d_gain


def turn(z, cosines, sines, back=False):
    if back:
        sines = -sines
    half = HEAD // 2
    parts = z.reshape(z.shape[0] // HEAD, HEAD, z.shape[1])
    a, b = parts[:, :half], parts[:, half:]
    return jnp.concatenate([a * cosines - b * sines, b * cosines + a * sines], axis=1).reshape(
        z.shape
    )


def local(
    n_ctx,
    n_wa,
    tokens,
    w_query,
    w_key,
    w_value,
    w_out,
    w_gate,
    w_up,
    w_down,
    norm_attn,
    norm_ffn,
    cotangent,
):
    seqs, rows, width = tokens.shape
    q_width, k_width = w_query.shape[1], w_key.shape[1]
    per_group = q_width // k_width
    groups = k_width // HEAD
    shard = w_query.shape[0]
    ff_part = w_down.shape[0]
    c_bits = bits_of(n_ctx)
    each = range(seqs)
    here = lax.axis_index("ctx")

    gains = gather_rows(jnp.stack([norm_attn, norm_ffn]), n_wa)
    gains = gains.transpose(1, 0, 2).reshape(2, width).astype(F32)
    w_qkv = gather_rows(jnp.concatenate([w_query, w_key, w_value], axis=1), n_wa)
    w_qkv = w_qkv.reshape(width, q_width + 2 * k_width)
    w_o = gather_rows(w_out, n_wa).reshape(q_width, width)

    def take_columns(device):
        return jnp.concatenate(
            [
                lax.dynamic_slice_in_dim(w, device * ff_part, ff_part, 1)
                for w in (w_gate, w_up)
            ],
            axis=1,
        )

    def place_rows(result, block, device):
        if result is None:
            result = jnp.zeros((width, 2 * ff_part), BF)
        return lax.dynamic_update_slice_in_dim(result, block, device * shard, 0)

    w_gu = exchange_blocks(take_columns, n_wa, place_rows)
    dy_all = [gather_relative(cotangent[i], n_wa) for i in each]

    half = HEAD // 2
    frequency = 10000.0 ** (-jnp.arange(half).astype(F32) / half)
    position = (here * rows + jnp.arange(rows, dtype=jnp.int32)).astype(F32)
    angles = frequency[:, None] * position[None, :]
    cosines, sines = lax.optimization_barrier((jnp.cos(angles), jnp.sin(angles)))
    high_first = list(reversed(range(c_bits)))
    low_swapped = high_first[:-2] + high_first[-2:][::-1]
    orders = [high_first if i % 2 == 0 else low_swapped for i in each]

    def bias_of(order):
        block = here ^ jnp.array(slot_offsets(order), jnp.int32)
        key_place = (block[:, None] * rows + jnp.arange(rows, dtype=jnp.int32)[None, :]).reshape(-1)
        query_place = here * rows + jnp.arange(rows, dtype=jnp.int32)
        return jnp.where(key_place[:, None] <= query_place[None, :], 0.0, -1e30).astype(F32)

    biases = [bias_of(order) for order in orders]

    x, h1, r1, q, kv = [], [], [], [], []
    for i in each:
        xi = tokens[i].astype(F32)
        hi, ri = rms(xi, gains[0])
        hi = hi.astype(BF)
        qkv = mm(w_qkv, hi, 0, 1)
        qi = turn(qkv[:q_width], cosines, sines).astype(BF) * BF(HEAD ** (-0.5))
        ki = turn(qkv[q_width : q_width + k_width], cosines, sines).astype(BF)
        vi = qkv[q_width + k_width :].astype(BF)
        x.append(xi)
        h1.append(hi)
        r1.append(ri)
        q.append(qi)
        kv.append(doubled(jnp.concatenate([ki, vi], axis=0)[None], n_ctx, orders[i]))

    o, lse, o_b, x1, r2, h2_all = [], [], [], [], [], []
    for i in each:
        oi, li = attend(groups, per_group, q[i], kv[i], biases[i])
        ob = oi.astype(BF)
        x1i = x[i] + mm(ob, w_o, 0, 0)
        h2, r2i = rms(x1i, gains[1])
        o.append(oi)
        lse.append(li)
        o_b.append(ob)
        x1.append(x1i)
        r2.append(r2i)
        h2_all.append(gather_relative(h2.astype(BF), n_wa))

    mixed, dh2, act_all, dgu_all = [], [], [], []
    for i in each:
        gu = mm(h2_all[i], w_gu, 1, 0)
        gate, up = gu[:, :ff_part], gu[:, ff_part:]
        sig = jax.nn.sigmoid(gate)
        silu = gate * sig
        act = (silu * up).astype(BF)
        dact = mm(dy_all[i], w_down, 1, 1)
        dgate = (dact * up * sig * (1.0 + gate * (1.0 - sig))).astype(BF)
        dup = (dact * silu).astype(BF)
        dgu = jnp.concatenate([dgate, dup], axis=1)
        dh2.append(scatter_relative(mm(dgu, w_gu, 1, 1), n_wa))
        mixed.append((x1[i] + scatter_relative(mm(act, w_down, 1, 0), n_wa)).astype(BF))
        act_all.append(act)
        dgu_all.append(dgu)
    act_all = jnp.concatenate(act_all, axis=0)
    dgu_all = jnp.concatenate(dgu_all, axis=0)
    h2_cat = jnp.concatenate(h2_all, axis=0)
    dy_cat = jnp.concatenate(dy_all, axis=0)

    low_first = list(range(c_bits))
    middle_first = low_first[1:] + low_first[:1]
    g_gu = mm(h2_cat, dgu_all, 0, 0).astype(BF).reshape(n_wa, shard, 2 * ff_part)
    g_down = mm(act_all, dy_cat, 0, 0).astype(BF)
    gu_part, gu_trail = reduce_halves(
        g_gu, n_ctx, [(bit, 2 if index == 0 else 1) for index, bit in enumerate(low_first)]
    )

    def place_sources(result, block, device):
        if result is None:
            result = jnp.zeros_like(gu_part)
        return lax.dynamic_update_slice_in_dim(result, block, device, 0)

    gu_part = exchange_blocks(
        lambda device: lax.dynamic_slice_in_dim(gu_part, device, 1, 0), n_wa, place_sources
    )
    g_gu = gather_halves(gu_part, n_ctx, gu_trail)
    g_gate, g_up = [
        g_gu[:, :, s * ff_part : (s + 1) * ff_part]
        .transpose(1, 0, 2)
        .reshape(shard, n_wa * ff_part)
        .astype(F32)
        for s in range(2)
    ]
    g_down = all_reduce_ctx(g_down, n_ctx, [(bit, 0) for bit in middle_first]).astype(F32)

    dx1, dx1_b, dq_b, dkv, dg2 = [], [], [], [], []
    for i in each:
        norm_part, dgi = rms_back(dh2[i], x1[i], r2[i], gains[1])
        dx1i = cotangent[i].astype(F32) + norm_part
        dx1b = dx1i.astype(BF)
        do = mm(w_o, dx1b, 1, 1).astype(BF)
        dqi, dkvi = attend_back(groups, per_group, q[i], kv[i], biases[i], lse[i], do, o[i])
        dx1.append(dx1i)
        dx1_b.append(dx1b)
        dg2.append(dgi)
        dq_b.append(turn(dqi, cosines, sines, back=True).astype(BF))
        dkv.append(halved(dkvi, n_ctx, orders[i])[0])

    h1_cat = jnp.concatenate(h1, axis=0)
    g_out = mm(jnp.concatenate(o_b, axis=1), jnp.concatenate(dx1_b, axis=0), 1, 0)
    g_query = mm(h1_cat, jnp.concatenate(dq_b, axis=1), 0, 1)
    g_oq = jnp.concatenate([g_out, g_query], axis=1).astype(BF).reshape(n_wa, shard, -1)
    plan = [(bit, 0) for bit in low_first]
    g_oq = all_reduce_ctx(scatter_rows(g_oq, n_wa), n_ctx, plan).astype(F32)

    input_grad, dkv_b, dg1 = [], [], []
    for i in each:
        dk = turn(dkv[i][:k_width], cosines, sines, back=True)
        dkvb = jnp.concatenate([dk, dkv[i][k_width:]], axis=0).astype(BF)
        dh1 = mm(dq_b[i], w_qkv[:, :q_width], 0, 1) + mm(dkvb, w_qkv[:, q_width:], 0, 1)
        norm_part, dgi = rms_back(dh1, x[i], r1[i], gains[0])
        input_grad.append((dx1[i] + norm_part).astype(BF))
        dkv_b.append(dkvb)
        dg1.append(dgi)
    g_kv = mm(h1_cat, jnp.concatenate(dkv_b, axis=1), 0, 1).reshape(n_wa, shard, -1)
    g_gain = jnp.stack([sum(dg1), sum(dg2)]).reshape(2, n_wa, shard).transpose(1, 0, 2)
    g_gain = jnp.pad(g_gain, ((0, 0), (0, 6), (0, g_kv.shape[2] - shard)))
    g_kv = jnp.concatenate([g_kv, g_gain], axis=1).astype(BF)
    g_kv = all_reduce_ctx(scatter_rows(g_kv, n_wa), n_ctx, plan).astype(F32)

    return (
        jnp.stack(mixed),
        jnp.stack(input_grad),
        g_oq[:, width:],
        g_kv[:shard, :k_width],
        g_kv[:shard, k_width:],
        g_oq[:, :width],
        g_gate,
        g_up,
        g_down,
        g_kv[shard, :shard],
        g_kv[shard + 1, :shard],
    )


def solution(mesh):
    rows, weight, vector = P("wa", "ctx", None), P("wa", None), P("wa")
    specs = (weight,) * 7 + (vector,) * 2
    return jax.shard_map(
        functools.partial(local, mesh.shape["ctx"], mesh.shape["wa"]),
        mesh=mesh,
        in_specs=(rows,) + specs + (rows,),
        out_specs=(rows, rows) + specs,
        check_vma=False,
    )
```

time: 1200 us -> 471 us (0.39)
  blocking collectives: 535 us -> 0 us
  waiting for transfers between devices: 488 us -> 179 us
  starting transfers between devices: 1.1 us -> 69.9 us
  other arithmetic: 13.9 us -> 70.6 us
  matrix products: 95.9 us -> 41.3 us
  local copies, waits for them, and re-layouts: 38 us -> 73.2 us
  Pallas kernels: 0 us -> 28.4 us
  between operations: 17 us -> 2.82 us
    psum x1 -> x0, blocking collectives: 388 us -> none  [local(): summed = lax.psum(owned, 'ctx')]
    reduce_scatter x8 -> x0, waiting for transfers between devices: 379 us -> none  [the longest x2 132 us: backward_pass(): lax.psum_scatter(key_terms, 'ctx', scatter_dimension=0, tiled=True)]
    ppermute x0 -> x72, waiting for transfers between devices: none -> 179 us  [the longest x66 164 us: swap(): return lax.ppermute(a, axis, [(i, i ^ 1 << bit) for i in range(n)])]
    all_gather x6 -> x0, blocking collectives: 133 us -> none  [the longest x2 57.4 us: forward_pass(): lax.all_gather(value_b, 'ctx', axis=0, tiled=True)]
    unnamed x19 -> x0, waiting for transfers between devices: 109 us -> none
    ppermute x0 -> x72, starting transfers between devices: none -> 69.9 us  [the longest x66 66 us: swap(): return lax.ppermute(a, axis, [(i, i ^ 1 << bit) for i in range(n)])]
    dot_general x56 -> x23, matrix products: 95.9 us -> 41.3 us  [mm(): lax.dot_general(a, b, (((ca,), (cb,)), ((), ())), preferred_element_type=...]
    pallas_call x0 -> x4, Pallas kernels: none -> 28.4 us  [the longest x2 15.7 us: attend_back(): pl.pallas_call(functools.partial(attend_back_kernel, groups, per_group, m...]
  transfers between devices with their start and end apart: 16 -> 72, of which waited for: 10 -> 29; matrix products, arithmetic and copies ran while one was open for 9% -> 37% of each run, Pallas kernels for 0% -> 6%
where the time goes in v1:
time: 471 us; the launch traced here: 466 us
  waiting for transfers between devices  179 us (38%)
  local copies, waits for them, and re-layouts  73.2 us (16%)
  other arithmetic  70.6 us (15%)
  starting transfers between devices  69.9 us (15%)
  matrix products  41.3 us (9%)
  Pallas kernels  28.4 us (6%)
    ppermute x66, waiting for transfers between devices, swap(): return lax.ppermute(a, axis, [(i, i ^ 1 << bit) for i in range(n)])  164 us
    ppermute x66, starting transfers between devices, swap(): return lax.ppermute(a, axis, [(i, i ^ 1 << bit) for i in range(n)])  66 us
    dot_general x23, matrix products, mm(): lax.dot_general(a, b, (((ca,), (cb,)), ((), ())), preferred_element_type=...  41.3 us
    unnamed x211, local copies, waits for them, and re-layouts  24 us
    pallas_call x2, Pallas kernels, attend_back(): pl.pallas_call(functools.partial(attend_back_kernel, groups, per_group, m...  15.7 us
    ppermute x6, waiting for transfers between devices, exchange_blocks(): got = lax.ppermute(take(me ^ step), 'wa', [(i, i ^ step) for i in range(n)])  15.6 us
    select_n x13, other arithmetic, ordered(): jnp.where(bit == 0, jnp.concatenate([mine, theirs], axis=dim), jnp.concat...  13.6 us
    pallas_call x2, Pallas kernels, attend(): pl.pallas_call(functools.partial(attend_kernel, groups, per_group, min(sl...  12.6 us
  transfers between devices with their start and end apart: 72, of which 29 were waited for; matrix products, arithmetic and copies ran while one was open for 37% of the time, Pallas kernels for 6%

profile of v1, /device:TPU:0, one launch (start us, length us, event | category | flops | bytes accessed | tf_op | source)
XLA Modules:
  0.0 465.5 jit_solution(15775558794040054782)
XLA Ops:
  2.7 2.9 collective-permute-start.25
  21.4 8.5 %collective-permute-done.2 = bf16[1,1,2,240]{3,2,1,0:T(2,128)(2,1)S(1)} collective-permute-done((bf16[1,1,2,240]{3,2,1,0:T(2,128)(2,1)S(1)}, bf16[1,1,2,240]{3,2,1,0:T(2,128)(2,1)S(1)}, u32[]{:S(2)}, u32[]{:S(2)}) %collective-permute-start.2) | collective-permute-done | bytes 992 | tf_op jit(solution)/shard_map/ppermute | solution.py:26
  38.6 7.3 %collective-permute-done.7 = bf16[1,1,240,960]{3,2,1,0:T(8,128)(2,1)S(1)} collective-permute-done((bf16[1,1,240,960]{3,2,1,0:T(8,128)(2,1)S(1)}, bf16[1,1,240,960]{3,2,1,0:T(8,128)(2,1)S(1)}, u32[]{:S(2)}, u32[]{:S(2)}) %collective-permute-start.7) | collective-permute-done | bytes 460832 | tf_op jit(solution)/shard_map/ppermute | solution.py:26
  52.0 10.7 %collective-permute-done.13 = bf16[240,1280]{1,0:T(8,128)(2,1)S(1)} collective-permute-done((bf16[240,1280]{1,0:T(8,128)(2,1)S(1)}, bf16[240,1280]{1,0:T(8,128)(2,1)S(1)}, u32[]{:S(2)}, u32[]{:S(2)}) %collective-permute-start.13) | collective-permute-done | bytes 614432 | tf_op jit(solution)/shard_map/ppermute | solution.py:81
  70.2 4.9 %collective-permute-done.14 = bf16[240,1280]{1,0:T(8,128)(2,1)S(1)} collective-permute-done((bf16[240,1280]{1,0:T(8,128)(2,1)S(1)}, bf16[240,1280]{1,0:T(8,128)(2,1)S(1)}, u32[]{:S(2)}, u32[]{:S(2)}) %collective-permute-start.14) | collective-permute-done | bytes 614432 | tf_op jit(solution)/shard_map/ppermute | solution.py:81
  78.3 3.4 collective-permute-start.17
  82.2 7.9 %collective-permute-done.5 = bf16[2,640,128]{2,1,0:T(8,128)(2,1)S(1)} collective-permute-done((bf16[2,640,128]{2,1,0:T(8,128)(2,1)S(1)}, bf16[2,640,128]{2,1,0:T(8,128)(2,1)S(1)}, u32[]{:S(2)}, u32[]{:S(2)}) %collective-permute-start.5) | collective-permute-done | bytes 327712 | tf_op jit(solution)/shard_map/ppermute | solution.py:26
  94.0 18.1 %collective-permute-done.18 = bf16[2,640,128]{2,1,0:T(8,128)(2,1)S(1)} collective-permute-done((bf16[2,640,128]{2,1,0:T(8,128)(2,1)S(1)}, bf16[2,640,128]{2,1,0:T(8,128)(2,1)S(1)}, u32[]{:S(2)}, u32[]{:S(2)}) %collective-permute-start.18) | collective-permute-done | bytes 327712 | tf_op jit(solution)/shard_map/ppermute | solution.py:26
  115.0 6.1 %shard_map.212 = (f32[960,128]{1,0:T(8,128)}, f32[15,128]{1,0:T(8,128)}) custom-call(bf16[960,128]{1,0:T(8,128)(2,1)} %bitcast.233, bf16[8,640,128]{2,1,0:T(8,128)(2,1)} %pad_maximum_fusion.kv_ref, f32[1024,128]{1,0:T(8,128)} %get-tuple-element.128.bias_ref), custom_call_target="tpu_custom_call" | custom-call | flops 1006632960 | bytes 2572288 | tf_op jit(solution)/shard_map/pallas_call | solution.py:263
  130.2 6.6 %shard_map.213 = (f32[960,128]{1,0:T(8,128)}, f32[15,128]{1,0:T(8,128)}) custom-call(bf16[960,128]{1,0:T(8,128)(2,1)} %bitcast.235, bf16[8,640,128]{2,1,0:T(8,128)(2,1)} %pad_maximum_fusion.1.kv_ref, f32[1024,128]{1,0:T(8,128)} %get-tuple-element.129.bias_ref), custom_call_target="tpu_custom_call" | custom-call | flops 1006632960 | bytes 2572288 | tf_op jit(solution)/shard_map/pallas_call | solution.py:263
  143.6 3.6 fusion.37
  147.3 2.7 multiply_convert_fusion.3
  150.0 3.2 fusion.13
  157.4 3.3 fusion.45
  160.8 2.6 multiply_convert_fusion.1
  163.4 3.2 fusion.17
  173.5 4.3 convolution_convert_fusion
  182.4 2.6 constant_dynamic-slice_fusion.9
  190.8 8.3 %collective-permute-done.66 = bf16[320,960]{1,0:T(8,128)(2,1)S(1)} collective-permute-done((bf16[320,960]{1,0:T(8,128)(2,1)}, bf16[320,960]{1,0:T(8,128)(2,1)S(1)}, u32[]{:S(2)}, u32[]{:S(2)}) %collective-permute-start.66) | collective-permute-done | bytes 614432 | tf_op jit(solution)/shard_map/ppermute | solution.py:26
  205.6 4.8 %collective-permute-start.67 = (bf16[160,960]{0,1:T(8,128)(2,1)S(1)}, bf16[160,960]{0,1:T(8,128)(2,1)}, u32[]{:S(2)}, u32[]{:S(2)}) collective-permute-start(bf16[160,960]{0,1:T(8,128)(2,1)S(1)} %constant_dynamic-slice_fusion.1), channel_id=1, source_target_pairs={{0,16},{4,20},{8,24},{12,28},{16,0},{20,4},{24,8},{28,12},{1,17},{... | collective-permute-start | bytes 921608 | tf_op jit(solution)/shard_map/ppermute | solution.py:26
  212.2 2.9 fusion.164
  217.2 7.8 %shard_map.215 = (f32[960,128]{1,0:T(8,128)}, bf16[8,640,128]{2,1,0:T(8,128)(2,1)}) custom-call(bf16[960,128]{1,0:T(8,128)(2,1)} %bitcast.236, bf16[8,640,128]{2,1,0:T(8,128)(2,1)} %pad_maximum_fusion.1.kv_ref, f32[1024,128]{1,0:T(8,128)} %get-tuple-element.129.bias_ref, f32[15,128]{1,0:T(8,128)} %get-tuple-element.28.lse_ref, ...), custom_call_target="tpu_custom_call" | custom-call | flops 2516582400 | bytes 4620288 | tf_op jit(solution)/shard_map/pallas_call | solution.py:282
  230.0 7.9 %shard_map.214 = (f32[960,128]{1,0:T(8,128)}, bf16[8,640,128]{2,1,0:T(8,128)(2,1)}) custom-call(bf16[960,128]{1,0:T(8,128)(2,1)} %bitcast.234, bf16[8,640,128]{2,1,0:T(8,128)(2,1)} %pad_maximum_fusion.kv_ref, f32[1024,128]{1,0:T(8,128)} %get-tuple-element.128.bias_ref, f32[15,128]{1,0:T(8,128)} %get-tuple-element.25.lse_ref, ...), custom_call_target="tpu_custom_call" | custom-call | flops 2516582400 | bytes 4620288 | tf_op jit(solution)/shard_map/pallas_call | solution.py:282
  247.8 12.9 %collective-permute-done.68 = bf16[80,960]{0,1:T(8,128)(2,1)S(1)} collective-permute-done((bf16[80,960]{0,1:T(8,128)(2,1)S(1)}, bf16[80,960]{0,1:T(8,128)(2,1)S(1)}, u32[]{:S(2)}, u32[]{:S(2)}) %collective-permute-start.68) | collective-permute-done | bytes 153632 | tf_op jit(solution)/shard_map/ppermute | solution.py:26
  263.3 3.9 collective-permute-done.69
  272.9 2.7 add_convert_fusion.1
  276.8 2.5 collective-permute-start.40
  279.3 7.0 %collective-permute-done.31 = bf16[2,640,128]{2,1,0:T(8,128)(2,1)S(1)} collective-permute-done((bf16[2,640,128]{2,1,0:T(8,128)(2,1)S(1)}, bf16[2,640,128]{2,1,0:T(8,128)(2,1)S(1)}, u32[]{:S(2)}, u32[]{:S(2)}) %collective-permute-start.31) | collective-permute-done | bytes 327712 | tf_op jit(solution)/shard_map/ppermute | solution.py:26
  286.3 3.1 collective-permute-start.32
  289.5 9.8 %collective-permute-done.40 = bf16[1,640,128]{2,1,0:T(8,128)(2,1)S(1)} collective-permute-done((bf16[1,640,128]{2,1,0:T(8,128)(2,1)S(1)}, bf16[1,640,128]{2,1,0:T(8,128)(2,1)S(1)}, u32[]{:S(2)}, u32[]{:S(2)}) %collective-permute-start.40) | collective-permute-done | bytes 163872 | tf_op jit(solution)/shard_map/ppermute | solution.py:26
  299.4 3.3 collective-permute-done.32
  307.3 2.7 fusion.90
  326.8 4.2 collective-permute-done.58
  333.9 17.8 %collective-permute-done.71 = bf16[320,960]{1,0:T(8,128)(2,1)} collective-permute-done((bf16[320,960]{1,0:T(8,128)(2,1)}, bf16[320,960]{1,0:T(8,128)(2,1)}, u32[]{:S(2)}, u32[]{:S(2)}) %collective-permute-start.71) | collective-permute-done | bytes 614432 | tf_op jit(solution)/shard_map/ppermute | solution.py:26
  368.8 2.6 dynamic_update_slice.28
  372.5 2.6 dynamic_update_slice.29
  376.1 2.6 dynamic_update_slice.30
  379.8 2.6 dynamic_update_slice.31
  386.4 14.4 %collective-permute-done.63 = bf16[4,64,640]{2,0,1:T(4,128)(2,1)S(1)} collective-permute-done((bf16[4,64,640]{2,0,1:T(4,128)(2,1)S(1)}, bf16[4,64,640]{2,0,1:T(4,128)(2,1)S(1)}, u32[]{:S(2)}, u32[]{:S(2)}) %collective-permute-start.63) | collective-permute-done | bytes 327712 | tf_op jit(solution)/shard_map/ppermute | solution.py:26
  403.6 2.6 collective-permute-done.54
  408.8 2.9 collective-permute-done.55
  412.4 3.5 collective-permute-done.43
  418.4 5.6 %collective-permute-done.64 = bf16[4,120,640]{2,0,1:T(4,128)(2,1)S(1)} collective-permute-done((bf16[4,120,640]{2,0,1:T(4,128)(2,1)S(1)}, bf16[4,120,640]{2,0,1:T(4,128)(2,1)S(1)}, u32[]{:S(2)}, u32[]{:S(2)}) %collective-permute-start.64) | collective-permute-done | bytes 614432 | tf_op jit(solution)/shard_map/ppermute | solution.py:26
  424.1 4.2 maximum_select_fusion.4
  431.1 7.6 %collective-permute-done.45 = bf16[32,1920]{1,0:T(8,128)(2,1)S(1)} collective-permute-done((bf16[32,1920]{1,0:T(8,128)(2,1)S(1)}, bf16[32,1920]{1,0:T(8,128)(2,1)S(1)}, u32[]{:S(2)}, u32[]{:S(2)}) %collective-permute-start.45) | collective-permute-done | bytes 122912 | tf_op jit(solution)/shard_map/ppermute | solution.py:26
  438.8 6.6 %collective-permute-done.46 = bf16[32,1920]{1,0:T(8,128)(2,1)S(1)} collective-permute-done((bf16[32,1920]{1,0:T(8,128)(2,1)S(1)}, bf16[32,1920]{1,0:T(8,128)(2,1)S(1)}, u32[]{:S(2)}, u32[]{:S(2)}) %collective-permute-start.46) | collective-permute-done | bytes 122912 | tf_op jit(solution)/shard_map/ppermute | solution.py:26
  448.2 3.6 collective-permute-done.47
  455.6 3.8 maximum_select_fusion.1
  (515 shorter events, 194.0 us)
Async XLA Ops:
  2.7 33.1 %collective-permute-start.25 = (bf16[128,960]{0,1:T(8,128)(2,1)}, bf16[128,960]{0,1:T(8,128)(2,1)}, u32[]{:S(2)}, u32[]{:S(2)}) collective-permute-start(bf16[128,960]{0,1:T(8,128)(2,1)} %get-tuple-element.100), channel_id=1, source_target_pairs={{0,2},{1,3},{2,0},{3,1},{4,6},{5,7},{6,4},{7,5},{8,10},{9,11},{10,... | collective-permute-start | bytes 737288 | tf_op jit(solution)/shard_map/ppermute | solution.py:26
  5.7 31.4 %collective-permute-start.26 = (bf16[128,960]{0,1:T(8,128)(2,1)}, bf16[128,960]{0,1:T(8,128)(2,1)}, u32[]{:S(2)}, u32[]{:S(2)}) collective-permute-start(bf16[128,960]{0,1:T(8,128)(2,1)} %get-tuple-element.100), channel_id=1, source_target_pairs={{0,1},{1,0},{2,3},{3,2},{4,5},{5,4},{6,7},{7,6},{8,9},{9,8},{10,11... | collective-permute-start | bytes 737288 | tf_op jit(solution)/shard_map/ppermute | solution.py:26
  9.1 23.0 %collective-permute-start = (bf16[1,1,240,1600]{3,2,1,0:T(8,128)(2,1)S(1)}, bf16[1,1,240,1600]{3,2,1,0:T(8,128)(2,1)}, u32[]{:S(2)}, u32[]{:S(2)}) collective-permute-start(bf16[1,1,240,1600]{3,2,1,0:T(8,128)(2,1)S(1)} %bitcast.207), channel_id=1, source_target_pairs={{0,2},{1,3},{2,0},{3,1},{4,6},{5,7},{6,4},{7,5},{8,10},{9,11},{10,... | collective-permute-start | bytes 2304008 | tf_op jit(solution)/shard_map/ppermute | solution.py:26
  9.3 20.6 %collective-permute-start.2 = (bf16[1,1,2,240]{3,2,1,0:T(2,128)(2,1)S(1)}, bf16[1,1,2,240]{3,2,1,0:T(2,128)(2,1)S(1)}, u32[]{:S(2)}, u32[]{:S(2)}) collective-permute-start(bf16[1,1,2,240]{3,2,1,0:T(2,128)(2,1)S(1)} %maximum_bitcast_fusion.3), channel_id=1, source_target_pairs={{0,2},{1,3},{2,0},{3,1},{4,6},{5,7},{6,4},{7,5},{8,10},{9,11},{10,... | collective-permute-start | bytes 2888 | tf_op jit(solution)/shard_map/ppermute | solution.py:26
  11.3 34.7 %collective-permute-start.33 = (bf16[128,960]{0,1:T(8,128)(2,1)}, bf16[128,960]{0,1:T(8,128)(2,1)}, u32[]{:S(2)}, u32[]{:S(2)}) collective-permute-start(bf16[128,960]{0,1:T(8,128)(2,1)} %get-tuple-element.101), channel_id=1, source_target_pairs={{0,2},{1,3},{2,0},{3,1},{4,6},{5,7},{6,4},{7,5},{8,10},{9,11},{10,... | collective-permute-start | bytes 737288 | tf_op jit(solution)/shard_map/ppermute | solution.py:26
  31.1 18.2 %collective-permute-start.34 = (bf16[128,960]{0,1:T(8,128)(2,1)}, bf16[128,960]{0,1:T(8,128)(2,1)}, u32[]{:S(2)}, u32[]{:S(2)}) collective-permute-start(bf16[128,960]{0,1:T(8,128)(2,1)} %get-tuple-element.101), channel_id=1, source_target_pairs={{0,1},{1,0},{2,3},{3,2},{4,5},{5,4},{6,7},{7,6},{8,9},{9,8},{10,11... | collective-permute-start | bytes 737288 | tf_op jit(solution)/shard_map/ppermute | solution.py:26
  32.1 13.7 %collective-permute-start.7 = (bf16[1,1,240,960]{3,2,1,0:T(8,128)(2,1)S(1)}, bf16[1,1,240,960]{3,2,1,0:T(8,128)(2,1)S(1)}, u32[]{:S(2)}, u32[]{:S(2)}) collective-permute-start(bf16[1,1,240,960]{3,2,1,0:T(8,128)(2,1)S(1)} %bitcast.225), channel_id=1, source_target_pairs={{0,2},{1,3},{2,0},{3,1},{4,6},{5,7},{6,4},{7,5},{8,10},{9,11},{10,... | collective-permute-start | bytes 1382408 | tf_op jit(solution)/shard_map/ppermute | solution.py:26
  35.8 27.8 %collective-permute-start.1 = (bf16[2,1,240,1600]{3,2,1,0:T(8,128)(2,1)S(1)}, bf16[2,1,240,1600]{3,2,1,0:T(8,128)(2,1)S(1)}, u32[]{:S(2)}, u32[]{:S(2)}) collective-permute-start(bf16[2,1,240,1600]{3,2,1,0:T(8,128)(2,1)S(1)} %maximum_select_fusion.3), channel_id=1, source_target_pairs={{0,1},{1,0},{2,3},{3,2},{4,5},{5,4},{6,7},{7,6},{8,9},{9,8},{10,11... | collective-permute-start | bytes 4608008 | tf_op jit(solution)/shard_map/ppermute | solution.py:26
  46.0 16.7 %collective-permute-start.13 = (bf16[240,1280]{1,0:T(8,128)(2,1)S(1)}, bf16[240,1280]{1,0:T(8,128)(2,1)S(1)}, u32[]{:S(2)}, u32[]{:S(2)}) collective-permute-start(bf16[240,1280]{1,0:T(8,128)(2,1)S(1)} %copy-done.63), channel_id=1, source_target_pairs={{0,2},{1,3},{2,0},{3,1},{4,6},{5,7},{6,4},{7,5},{8,10},{9,11},{10,... | collective-permute-start | bytes 1843208 | tf_op jit(solution)/shard_map/ppermute | solution.py:81
  49.3 25.8 %collective-permute-start.14 = (bf16[240,1280]{1,0:T(8,128)(2,1)S(1)}, bf16[240,1280]{1,0:T(8,128)(2,1)S(1)}, u32[]{:S(2)}, u32[]{:S(2)}) collective-permute-start(bf16[240,1280]{1,0:T(8,128)(2,1)S(1)} %copy-done.62), channel_id=1, source_target_pairs={{0,3},{1,2},{2,1},{3,0},{4,7},{5,6},{6,5},{7,4},{8,11},{9,10},{10,... | collective-permute-start | bytes 1843208 | tf_op jit(solution)/shard_map/ppermute | solution.py:81
  50.6 31.2 %collective-permute-start.8 = (bf16[2,1,240,960]{3,2,1,0:T(8,128)(2,1)S(1)}, bf16[2,1,240,960]{3,2,1,0:T(8,128)(2,1)S(1)}, u32[]{:S(2)}, u32[]{:S(2)}) collective-permute-start(bf16[2,1,240,960]{3,2,1,0:T(8,128)(2,1)S(1)} %maximum_select_fusion.6), channel_id=1, source_target_pairs={{0,1},{1,0},{2,3},{3,2},{4,5},{5,4},{6,7},{7,6},{8,9},{9,8},{10,11... | collective-permute-start | bytes 2764808 | tf_op jit(solution)/shard_map/ppermute | solution.py:26
  90.1 23.6 %collective-permute-start.6 = (bf16[4,640,128]{2,1,0:T(8,128)(2,1)S(1)}, bf16[4,640,128]{2,1,0:T(8,128)(2,1)S(1)}, u32[]{:S(2)}, u32[]{:S(2)}) collective-permute-start(bf16[4,640,128]{2,1,0:T(8,128)(2,1)S(1)} %pad_maximum_fusion.2), channel_id=1, source_target_pairs={{0,4},{4,0},{8,12},{12,8},{16,20},{20,16},{24,28},{28,24},{1,5},{5... | collective-permute-start | bytes 1966088 | tf_op jit(solution)/shard_map/ppermute | solution.py:26
  91.4 20.7 %collective-permute-start.18 = (bf16[2,640,128]{2,1,0:T(8,128)(2,1)S(1)}, bf16[2,640,128]{2,1,0:T(8,128)(2,1)S(1)}, u32[]{:S(2)}, u32[]{:S(2)}) collective-permute-start(bf16[2,640,128]{2,1,0:T(8,128)(2,1)S(1)} %pad_maximum_fusion.13), channel_id=1, source_target_pairs={{0,4},{4,0},{8,12},{12,8},{16,20},{20,16},{24,28},{28,24},{1,5},{5... | collective-permute-start | bytes 983048 | tf_op jit(solution)/shard_map/ppermute | solution.py:26
  113.7 14.2 %collective-permute-start.19 = (bf16[4,640,128]{2,1,0:T(8,128)(2,1)}, bf16[4,640,128]{2,1,0:T(8,128)(2,1)}, u32[]{:S(2)}, u32[]{:S(2)}) collective-permute-start(bf16[4,640,128]{2,1,0:T(8,128)(2,1)} %pad_maximum_fusion.3), channel_id=1, source_target_pairs={{0,8},{4,12},{8,0},{12,4},{16,24},{20,28},{24,16},{28,20},{1,9},{5... | collective-permute-start | bytes 1966088 | tf_op jit(solution)/shard_map/ppermute | solution.py:26
  124.9 14.1 %collective-permute-start.9 = (bf16[128,960]{0,1:T(8,128)(2,1)}, bf16[128,960]{0,1:T(8,128)(2,1)}, u32[]{:S(2)}, u32[]{:S(2)}) collective-permute-start(bf16[128,960]{0,1:T(8,128)(2,1)} %get-tuple-element.59), channel_id=1, source_target_pairs={{0,2},{1,3},{2,0},{3,1},{4,6},{5,7},{6,4},{7,5},{8,10},{9,11},{10,... | collective-permute-start | bytes 737288 | tf_op jit(solution)/shard_map/ppermute | solution.py:26
  126.7 13.4 %collective-permute-start.10 = (bf16[128,960]{0,1:T(8,128)(2,1)}, bf16[128,960]{0,1:T(8,128)(2,1)}, u32[]{:S(2)}, u32[]{:S(2)}) collective-permute-start(bf16[128,960]{0,1:T(8,128)(2,1)} %get-tuple-element.59), channel_id=1, source_target_pairs={{0,1},{1,0},{2,3},{3,2},{4,5},{5,4},{6,7},{7,6},{8,9},{9,8},{10,11... | collective-permute-start | bytes 737288 | tf_op jit(solution)/shard_map/ppermute | solution.py:26
  154.7 15.1 %collective-permute-start.15 = (bf16[256,960]{0,1:T(8,128)(2,1)S(1)}, bf16[256,960]{0,1:T(8,128)(2,1)S(1)}, u32[]{:S(2)}, u32[]{:S(2)}) collective-permute-start(bf16[256,960]{0,1:T(8,128)(2,1)S(1)} %slice.569), channel_id=1, source_target_pairs={{0,1},{1,0},{2,3},{3,2},{4,5},{5,4},{6,7},{7,6},{8,9},{9,8},{10,11... | collective-permute-start | bytes 1474568 | tf_op jit(solution)/shard_map/ppermute | solution.py:26
  157.3 48.3 %collective-permute-start.29 = (bf16[128,960]{0,1:T(8,128)(2,1)}, bf16[128,960]{0,1:T(8,128)(2,1)}, u32[]{:S(2)}, u32[]{:S(2)}) collective-permute-start(bf16[128,960]{0,1:T(8,128)(2,1)} %slice.571), channel_id=1, source_target_pairs={{0,2},{1,3},{2,0},{3,1},{4,6},{5,7},{6,4},{7,5},{8,10},{9,11},{10,... | collective-permute-start | bytes 737288 | tf_op jit(solution)/shard_map/ppermute | solution.py:26
  167.5 17.5 %collective-permute-start.36 = (bf16[256,960]{0,1:T(8,128)(2,1)}, bf16[256,960]{0,1:T(8,128)(2,1)}, u32[]{:S(2)}, u32[]{:S(2)}) collective-permute-start(bf16[256,960]{0,1:T(8,128)(2,1)} %slice.566), channel_id=1, source_target_pairs={{0,1},{1,0},{2,3},{3,2},{4,5},{5,4},{6,7},{7,6},{8,9},{9,8},{10,11... | collective-permute-start | bytes 1474568 | tf_op jit(solution)/shard_map/ppermute | solution.py:26
  168.6 18.9 %collective-permute-start.23 = (bf16[256,960]{0,1:T(8,128)(2,1)S(1)}, bf16[256,960]{0,1:T(8,128)(2,1)}, u32[]{:S(2)}, u32[]{:S(2)}) collective-permute-start(bf16[256,960]{0,1:T(8,128)(2,1)S(1)} %slice.568), channel_id=1, source_target_pairs={{0,1},{1,0},{2,3},{3,2},{4,5},{5,4},{6,7},{7,6},{8,9},{9,8},{10,11... | collective-permute-start | bytes 1474568 | tf_op jit(solution)/shard_map/ppermute | solution.py:26
  171.7 40.4 %collective-permute-start.16 = (bf16[128,960]{0,1:T(8,128)(2,1)}, bf16[128,960]{0,1:T(8,128)(2,1)}, u32[]{:S(2)}, u32[]{:S(2)}) collective-permute-start(bf16[128,960]{0,1:T(8,128)(2,1)} %slice.573), channel_id=1, source_target_pairs={{0,2},{1,3},{2,0},{3,1},{4,6},{5,7},{6,4},{7,5},{8,10},{9,11},{10,... | collective-permute-start | bytes 737288 | tf_op jit(solution)/shard_map/ppermute | solution.py:26
  182.1 17.1 %collective-permute-start.66 = (bf16[320,960]{1,0:T(8,128)(2,1)}, bf16[320,960]{1,0:T(8,128)(2,1)S(1)}, u32[]{:S(2)}, u32[]{:S(2)}) collective-permute-start(bf16[320,960]{1,0:T(8,128)(2,1)} %copy.46), channel_id=1, source_target_pairs={{0,8},{4,12},{8,0},{12,4},{16,24},{20,28},{24,16},{28,20},{1,9},{5... | collective-permute-start | bytes 1843208 | tf_op jit(solution)/shard_map/ppermute | solution.py:26
  184.9 87.9 %collective-permute-start.57 = (bf16[4,240,640]{2,1,0:T(8,128)(2,1)}, bf16[4,240,640]{2,1,0:T(8,128)(2,1)}, u32[]{:S(2)}, u32[]{:S(2)}) collective-permute-start(bf16[4,240,640]{2,1,0:T(8,128)(2,1)} %constant_dynamic-slice_fusion.9), channel_id=1, source_target_pairs={{0,4},{4,0},{8,12},{12,8},{16,20},{20,16},{24,28},{28,24},{1,5},{5... | collective-permute-start | bytes 3686408 | tf_op jit(solution)/shard_map/ppermute | solution.py:26
  187.5 22.9 %collective-permute-start.37 = (bf16[128,960]{0,1:T(8,128)(2,1)}, bf16[128,960]{0,1:T(8,128)(2,1)S(1)}, u32[]{:S(2)}, u32[]{:S(2)}) collective-permute-start(bf16[128,960]{0,1:T(8,128)(2,1)} %slice.570), channel_id=1, source_target_pairs={{0,2},{1,3},{2,0},{3,1},{4,6},{5,7},{6,4},{7,5},{8,10},{9,11},{10,... | collective-permute-start | bytes 737288 | tf_op jit(solution)/shard_map/ppermute | solution.py:26
  205.6 37.9 %collective-permute-start.67 = (bf16[160,960]{0,1:T(8,128)(2,1)S(1)}, bf16[160,960]{0,1:T(8,128)(2,1)}, u32[]{:S(2)}, u32[]{:S(2)}) collective-permute-start(bf16[160,960]{0,1:T(8,128)(2,1)S(1)} %constant_dynamic-slice_fusion.1), channel_id=1, source_target_pairs={{0,16},{4,20},{8,24},{12,28},{16,0},{20,4},{24,8},{28,12},{1,17},{... | collective-permute-start | bytes 921608 | tf_op jit(solution)/shard_map/ppermute | solution.py:26
  227.0 41.2 %collective-permute-start.38 = (bf16[4,640,128]{2,1,0:T(8,128)(2,1)}, bf16[4,640,128]{2,1,0:T(8,128)(2,1)}, u32[]{:S(2)}, u32[]{:S(2)}) collective-permute-start(bf16[4,640,128]{2,1,0:T(8,128)(2,1)} %slice.321), channel_id=1, source_target_pairs={{0,8},{4,12},{8,0},{12,4},{16,24},{20,28},{24,16},{28,20},{1,9},{5... | collective-permute-start | bytes 1966088 | tf_op jit(solution)/shard_map/ppermute | solution.py:26
  240.0 31.2 %collective-permute-start.30 = (bf16[4,640,128]{2,1,0:T(8,128)(2,1)}, bf16[4,640,128]{2,1,0:T(8,128)(2,1)}, u32[]{:S(2)}, u32[]{:S(2)}) collective-permute-start(bf16[4,640,128]{2,1,0:T(8,128)(2,1)} %slice.302), channel_id=1, source_target_pairs={{0,4},{4,0},{8,12},{12,8},{16,20},{20,16},{24,28},{28,24},{1,5},{5... | collective-permute-start | bytes 1966088 | tf_op jit(solution)/shard_map/ppermute | solution.py:26
  245.0 15.7 %collective-permute-start.68 = (bf16[80,960]{0,1:T(8,128)(2,1)S(1)}, bf16[80,960]{0,1:T(8,128)(2,1)S(1)}, u32[]{:S(2)}, u32[]{:S(2)}) collective-permute-start(bf16[80,960]{0,1:T(8,128)(2,1)S(1)} %constant_dynamic-slice_fusion), channel_id=1, source_target_pairs={{0,4},{4,0},{8,12},{12,8},{16,20},{20,16},{24,28},{28,24},{1,5},{5... | collective-permute-start | bytes 460808 | tf_op jit(solution)/shard_map/ppermute | solution.py:26
  267.6 46.4 %collective-permute-start.70 = (bf16[160,960]{0,1:T(8,128)(2,1)S(1)}, bf16[160,960]{0,1:T(8,128)(2,1)}, u32[]{:S(2)}, u32[]{:S(2)}) collective-permute-start(bf16[160,960]{0,1:T(8,128)(2,1)S(1)} %maximum_select_fusion.9), channel_id=1, source_target_pairs={{0,16},{4,20},{8,24},{12,28},{16,0},{20,4},{24,8},{28,12},{1,17},{... | collective-permute-start | bytes 921608 | tf_op jit(solution)/shard_map/ppermute | solution.py:26
  272.4 13.8 %collective-permute-start.31 = (bf16[2,640,128]{2,1,0:T(8,128)(2,1)S(1)}, bf16[2,640,128]{2,1,0:T(8,128)(2,1)S(1)}, u32[]{:S(2)}, u32[]{:S(2)}) collective-permute-start(bf16[2,640,128]{2,1,0:T(8,128)(2,1)S(1)} %slice.379), channel_id=1, source_target_pairs={{0,8},{4,12},{8,0},{12,4},{16,24},{20,28},{24,16},{28,20},{1,9},{5... | collective-permute-start | bytes 983048 | tf_op jit(solution)/shard_map/ppermute | solution.py:26
  276.8 22.5 %collective-permute-start.40 = (bf16[1,640,128]{2,1,0:T(8,128)(2,1)S(1)}, bf16[1,640,128]{2,1,0:T(8,128)(2,1)S(1)}, u32[]{:S(2)}, u32[]{:S(2)}) collective-permute-start(bf16[1,640,128]{2,1,0:T(8,128)(2,1)S(1)} %slice.395), channel_id=1, source_target_pairs={{0,16},{4,20},{8,24},{12,28},{16,0},{20,4},{24,8},{28,12},{1,17},{... | collective-permute-start | bytes 491528 | tf_op jit(solution)/shard_map/ppermute | solution.py:26
  286.3 16.4 %collective-permute-start.32 = (bf16[1,640,128]{2,1,0:T(8,128)(2,1)S(1)}, bf16[1,640,128]{2,1,0:T(8,128)(2,1)S(1)}, u32[]{:S(2)}, u32[]{:S(2)}) collective-permute-start(bf16[1,640,128]{2,1,0:T(8,128)(2,1)S(1)} %slice.381), channel_id=1, source_target_pairs={{0,16},{4,20},{8,24},{12,28},{16,0},{20,4},{24,8},{28,12},{1,17},{... | collective-permute-start | bytes 491528 | tf_op jit(solution)/shard_map/ppermute | solution.py:26
  314.0 17.0 %collective-permute-start.58 = (bf16[4,120,640]{2,1,0:T(8,128)(2,1)}, bf16[4,120,640]{2,1,0:T(8,128)(2,1)}, u32[]{:S(2)}, u32[]{:S(2)}) collective-permute-start(bf16[4,120,640]{2,1,0:T(8,128)(2,1)} %constant_dynamic-slice_fusion.8), channel_id=1, source_target_pairs={{0,8},{4,12},{8,0},{12,4},{16,24},{20,28},{24,16},{28,20},{1,9},{5... | collective-permute-start | bytes 1843208 | tf_op jit(solution)/shard_map/ppermute | solution.py:26
  316.9 34.7 %collective-permute-start.71 = (bf16[320,960]{1,0:T(8,128)(2,1)}, bf16[320,960]{1,0:T(8,128)(2,1)}, u32[]{:S(2)}, u32[]{:S(2)}) collective-permute-start(bf16[320,960]{1,0:T(8,128)(2,1)} %copy.48), channel_id=1, source_target_pairs={{0,8},{4,12},{8,0},{12,4},{16,24},{20,28},{24,16},{28,20},{1,9},{5... | collective-permute-start | bytes 1843208 | tf_op jit(solution)/shard_map/ppermute | solution.py:26
  322.7 38.3 %collective-permute-start.41 = (bf16[2,1,240,1920]{3,2,1,0:T(8,128)(2,1)}, bf16[2,1,240,1920]{3,2,1,0:T(8,128)(2,1)}, u32[]{:S(2)}, u32[]{:S(2)}) collective-permute-start(bf16[2,1,240,1920]{3,2,1,0:T(8,128)(2,1)} %fusion.7), channel_id=1, source_target_pairs={{0,1},{1,0},{2,3},{3,2},{4,5},{5,4},{6,7},{7,6},{8,9},{9,8},{10,11... | collective-permute-start | bytes 5529608 | tf_op jit(solution)/shard_map/ppermute | solution.py:26
  325.1 28.0 %collective-permute-start.50 = (bf16[1,1,248,640]{3,2,1,0:T(8,128)(2,1)}, bf16[1,1,248,640]{3,2,1,0:T(8,128)(2,1)}, u32[]{:S(2)}, u32[]{:S(2)}) collective-permute-start(bf16[1,1,248,640]{3,2,1,0:T(8,128)(2,1)} %constant_dynamic-slice_fusion.12), channel_id=1, source_target_pairs={{0,2},{1,3},{2,0},{3,1},{4,6},{5,7},{6,4},{7,5},{8,10},{9,11},{10,... | collective-permute-start | bytes 952328 | tf_op jit(solution)/shard_map/ppermute | solution.py:26
  333.0 23.0 %collective-permute-start.59 = (bf16[4,64,640]{2,1,0:T(8,128)(2,1)}, bf16[4,64,640]{2,1,0:T(8,128)(2,1)}, u32[]{:S(2)}, u32[]{:S(2)}) collective-permute-start(bf16[4,64,640]{2,1,0:T(8,128)(2,1)} %constant_dynamic-slice_fusion.7), channel_id=1, source_target_pairs={{0,16},{4,20},{8,24},{12,28},{16,0},{20,4},{24,8},{28,12},{1,17},{... | collective-permute-start | bytes 983048 | tf_op jit(solution)/shard_map/ppermute | solution.py:26
  357.9 13.5 %collective-permute-start.60 = (bf16[1,64,640]{2,1,0:T(8,128)(2,1)}, bf16[1,64,640]{2,1,0:T(8,128)(2,1)}, u32[]{:S(2)}, u32[]{:S(2)}) collective-permute-start(bf16[1,64,640]{2,1,0:T(8,128)(2,1)} %get-tuple-element.104), channel_id=1, source_target_pairs={{0,1},{1,0},{2,3},{3,2},{4,5},{5,4},{6,7},{7,6},{8,9},{9,8},{10,11... | collective-permute-start | bytes 245768 | tf_op jit(solution)/shard_map/ppermute | solution.py:81
  357.9 17.2 %collective-permute-start.61 = (bf16[1,64,640]{2,1,0:T(8,128)(2,1)}, bf16[1,64,640]{2,1,0:T(8,128)(2,1)}, u32[]{:S(2)}, u32[]{:S(2)}) collective-permute-start(bf16[1,64,640]{2,1,0:T(8,128)(2,1)} %get-tuple-element.103), channel_id=1, source_target_pairs={{0,2},{1,3},{2,0},{3,1},{4,6},{5,7},{6,4},{7,5},{8,10},{9,11},{10,... | collective-permute-start | bytes 245768 | tf_op jit(solution)/shard_map/ppermute | solution.py:81
  359.6 19.2 %collective-permute-start.62 = (bf16[1,64,640]{2,1,0:T(8,128)(2,1)S(1)}, bf16[1,64,640]{2,1,0:T(8,128)(2,1)}, u32[]{:S(2)}, u32[]{:S(2)}) collective-permute-start(bf16[1,64,640]{2,1,0:T(8,128)(2,1)S(1)} %get-tuple-element.102), channel_id=1, source_target_pairs={{0,3},{1,2},{2,1},{3,0},{4,7},{5,6},{6,5},{7,4},{8,11},{9,10},{10,... | collective-permute-start | bytes 245768 | tf_op jit(solution)/shard_map/ppermute | solution.py:81
  361.0 22.8 %collective-permute-start.52 = (bf16[64,640]{1,0:T(8,128)(2,1)}, bf16[64,640]{1,0:T(8,128)(2,1)}, u32[]{:S(2)}, u32[]{:S(2)}) collective-permute-start(bf16[64,640]{1,0:T(8,128)(2,1)} %constant_dynamic-slice_fusion.11), channel_id=1, source_target_pairs={{0,8},{4,12},{8,0},{12,4},{16,24},{20,28},{24,16},{28,20},{1,9},{5... | collective-permute-start | bytes 245768 | tf_op jit(solution)/shard_map/ppermute | solution.py:26
  364.5 36.8 %collective-permute-start.42 = (bf16[1,1,240,1920]{3,2,1,0:T(8,128)(2,1)}, bf16[1,1,240,1920]{3,2,1,0:T(8,128)(2,1)}, u32[]{:S(2)}, u32[]{:S(2)}) collective-permute-start(bf16[1,1,240,1920]{3,2,1,0:T(8,128)(2,1)} %constant_dynamic-slice_fusion.15), channel_id=1, source_target_pairs={{0,2},{1,3},{2,0},{3,1},{4,6},{5,7},{6,4},{7,5},{8,10},{9,11},{10,... | collective-permute-start | bytes 2764808 | tf_op jit(solution)/shard_map/ppermute | solution.py:26
  382.4 18.4 %collective-permute-start.63 = (bf16[4,64,640]{2,0,1:T(4,128)(2,1)S(1)}, bf16[4,64,640]{2,0,1:T(4,128)(2,1)S(1)}, u32[]{:S(2)}, u32[]{:S(2)}) collective-permute-start(bf16[4,64,640]{2,0,1:T(4,128)(2,1)S(1)} %dynamic_update_slice.31), channel_id=1, source_target_pairs={{0,16},{4,20},{8,24},{12,28},{16,0},{20,4},{24,8},{28,12},{1,17},{... | collective-permute-start | bytes 983048 | tf_op jit(solution)/shard_map/ppermute | solution.py:26
  384.8 16.4 %collective-permute-start.53 = (bf16[32,640]{1,0:T(8,128)(2,1)S(1)}, bf16[32,640]{1,0:T(8,128)(2,1)S(1)}, u32[]{:S(2)}, u32[]{:S(2)}) collective-permute-start(bf16[32,640]{1,0:T(8,128)(2,1)S(1)} %constant_dynamic-slice_fusion.10), channel_id=1, source_target_pairs={{0,16},{4,20},{8,24},{12,28},{16,0},{20,4},{24,8},{28,12},{1,17},{... | collective-permute-start | bytes 122888 | tf_op jit(solution)/shard_map/ppermute | solution.py:26
  406.7 17.4 %collective-permute-start.64 = (bf16[4,120,640]{2,0,1:T(4,128)(2,1)S(1)}, bf16[4,120,640]{2,0,1:T(4,128)(2,1)S(1)}, u32[]{:S(2)}, u32[]{:S(2)}) collective-permute-start(bf16[4,120,640]{2,0,1:T(4,128)(2,1)S(1)} %pad_maximum_fusion.7), channel_id=1, source_target_pairs={{0,8},{4,12},{8,0},{12,4},{16,24},{20,28},{24,16},{28,20},{1,9},{5... | collective-permute-start | bytes 1843208 | tf_op jit(solution)/shard_map/ppermute | solution.py:26
  411.7 18.0 %collective-permute-start.56 = (bf16[128,640]{1,0:T(8,128)(2,1)S(1)}, bf16[128,640]{1,0:T(8,128)(2,1)S(1)}, u32[]{:S(2)}, u32[]{:S(2)}) collective-permute-start(bf16[128,640]{1,0:T(8,128)(2,1)S(1)} %maximum_select_fusion.11), channel_id=1, source_target_pairs={{0,4},{4,0},{8,12},{12,8},{16,20},{20,16},{24,28},{28,24},{1,5},{5... | collective-permute-start | bytes 491528 | tf_op jit(solution)/shard_map/ppermute | solution.py:26
  416.0 13.7 %collective-permute-start.44 = (bf16[64,1920]{1,0:T(8,128)(2,1)S(1)}, bf16[64,1920]{1,0:T(8,128)(2,1)S(1)}, u32[]{:S(2)}, u32[]{:S(2)}) collective-permute-start(bf16[64,1920]{1,0:T(8,128)(2,1)S(1)} %constant_dynamic-slice_fusion.14), channel_id=1, source_target_pairs={{0,8},{4,12},{8,0},{12,4},{16,24},{20,28},{24,16},{28,20},{1,9},{5... | collective-permute-start | bytes 737288 | tf_op jit(solution)/shard_map/ppermute | solution.py:26
  428.3 27.4 %collective-permute-start.65 = (bf16[4,240,640]{2,0,1:T(4,128)(2,1)S(1)}, bf16[4,240,640]{2,0,1:T(4,128)(2,1)}, u32[]{:S(2)}, u32[]{:S(2)}) collective-permute-start(bf16[4,240,640]{2,0,1:T(4,128)(2,1)S(1)} %maximum_select_fusion.4), channel_id=1, source_target_pairs={{0,4},{4,0},{8,12},{12,8},{16,20},{20,16},{24,28},{28,24},{1,5},{5... | collective-permute-start | bytes 3686408 | tf_op jit(solution)/shard_map/ppermute | solution.py:26
  (122 other events, 1034.8 us)

commit v2 on v1

--- a/solution.py
+++ b/solution.py
@@ -38,13 +38,47 @@
     )
 
 
-def gather_rows(a, n):
+def after(value, other):
+    return lax.optimization_barrier((value, other))[0]
+
+
+class Chain:
+    def __init__(self, steps):
+        self.steps = steps
+        self.pending = next(steps)
+        self.result = None
+
+    def issue(self, value=None):
+        if self.pending is None:
+            return value
+        if value is not None:
+            value = after(value, self.pending)
+        try:
+            self.pending = self.steps.send(self.pending)
+        except StopIteration as stop:
+            self.pending, self.result = None, stop.value
+        return value
+
+    def finish(self):
+        while self.pending is not None:
+            self.issue()
+        return self.result
+
+
+def gather_rows(a, n, lead=None):
+    lead = lead or a.shape[0]
     nb = bits_of(n)
     out = a.reshape((1,) * nb + a.shape)
     for bit in reversed(range(nb)):
-        dim = nb - 1 - bit
-        out = ordered(out, swap(out, "wa", n, bit), my_bit("wa", bit), dim)
-    return out.reshape((n,) + a.shape)
+        dim, mine = nb - 1 - bit, my_bit("wa", bit)
+        got = swap(out, "wa", n, bit)
+        wait = yield got
+        got = got if wait is None else after(got, wait)
+        if bit == 0:
+            rest = ordered(out[..., lead:, :], got[..., lead:, :], mine, dim)
+            out, got = out[..., :lead, :], got[..., :lead, :]
+        out = ordered(out, got, mine, dim)
+    return out.reshape(-1, a.shape[1]), rest.reshape(n, -1, a.shape[1])
 
 
 def gather_relative(a, n):
@@ -70,61 +104,71 @@
         mine = my_bit("wa", bit)
         keep = lax.dynamic_slice_in_dim(a, mine, 1, dim)
         send = lax.dynamic_slice_in_dim(a, 1 - mine, 1, dim).astype(BF)
+        send = yield send
         a = (keep.astype(F32) + swap(send, "wa", n, bit).astype(F32)).astype(BF)
     return a.reshape(a.shape[nb:])
 
 
-def exchange_blocks(take, n, place):
-    me = lax.axis_index("wa")
-    result = place(None, take(me), me)
-    for step in range(1, n):
-        got = lax.ppermute(take(me ^ step), "wa", [(i, i ^ step) for i in range(n)])
-        result = place(result, got, me ^ step)
-    return result
-
-
-def reduce_halves(a, n, plan):
+def exchange_blocks(a, n):
+    nb = bits_of(n)
+    out = a.reshape((2,) * nb + a.shape[1:])
+    for bit in reversed(range(nb)):
+        dim, mine = nb - 1 - bit, my_bit("wa", bit)
+        keep = lax.dynamic_slice_in_dim(out, mine, 1, dim)
+        got = swap(lax.dynamic_slice_in_dim(out, 1 - mine, 1, dim), "wa", n, bit)
+        wait = yield got
+        got = got if wait is None else after(got, wait)
+        out = ordered(keep, got, mine, dim)
+    return out.reshape(a.shape)
+
+
+def complete(steps, wait=None):
+    try:
+        steps.send(wait)
+        while True:
+            next(steps)
+    except StopIteration as stop:
+        return stop.value
+
+
+def all_reduce_ctx(a, n, plan):
     trail = []
-    for bit, dim in plan:
-        size = a.shape[dim]
+    for bit in plan:
+        size = a.shape[0]
         half = -(-size // 16) * 8
         mine = my_bit("ctx", bit)
         if half >= size:
-            got = swap(a.astype(BF), "ctx", n, bit)
-            a = (a.astype(F32) + got.astype(F32)).astype(BF)
-            trail.append((bit, dim, None))
+            send = a.astype(BF)
+            yield send
+            a = (a.astype(F32) + swap(send, "ctx", n, bit).astype(F32)).astype(BF)
             continue
-        keep = lax.dynamic_slice_in_dim(a, mine * (size - half), half, dim)
-        send = lax.dynamic_slice_in_dim(a, (1 - mine) * (size - half), half, dim).astype(BF)
+        keep = lax.dynamic_slice_in_dim(a, mine * (size - half), half, 0)
+        send = lax.dynamic_slice_in_dim(a, (1 - mine) * (size - half), half, 0).astype(BF)
+        yield send
         a = (keep.astype(F32) + swap(send, "ctx", n, bit).astype(F32)).astype(BF)
-        trail.append((bit, dim, size))
-    return a, trail
-
-
-def gather_halves(a, n, trail):
-    for bit, dim, size in reversed(trail):
-        if size is None:
-            continue
+        trail.append((bit, size))
+    for bit, size in reversed(trail):
+        yield a
         got = swap(a, "ctx", n, bit)
         mine = my_bit("ctx", bit)
-        if 2 * a.shape[dim] == size:
-            a = ordered(a, got, mine, dim)
+        extra = 2 * a.shape[0] - size
+        if extra == 0:
+            a = ordered(a, got, mine, 0)
         else:
             low = jnp.where(mine == 0, a, got)
             high = jnp.where(mine == 0, got, a)
-            extra = 2 * a.shape[dim] - size
-            high = lax.slice_in_dim(high, extra, a.shape[dim], axis=dim)
-            a = jnp.concatenate([low, high], axis=dim)
+            a = jnp.concatenate([low, high[extra:]], axis=0)
     return a
 
 
-def all_reduce_ctx(a, n, plan):
-    part, trail = reduce_halves(a, n, plan)
-    return gather_halves(part, n, trail)
+def all_reduce_rows(a, n_wa, n_ctx, plan):
+    own = yield from scatter_rows(a, n_wa)
+    return (yield from all_reduce_ctx(own, n_ctx, plan))
 
 
 def doubled(a, n, order):
     for bit in order:
+        yield a
         a = jnp.concatenate([a, swap(a, "ctx", n, bit)], axis=0)
     return a
 
@@ -132,7 +176,8 @@
 def halved(a, n, order):
     for bit in reversed(order):
         half = a.shape[0] // 2
-        got = swap(a[half:], "ctx", n, bit)
+        send = yield a[half:]
+        got = swap(send, "ctx", n, bit)
         a = (a[:half].astype(F32) + got.astype(F32)).astype(BF if half > 1 else F32)
     return a
 
@@ -338,28 +383,27 @@
     each = range(seqs)
     here = lax.axis_index("ctx")
 
-    gains = gather_rows(jnp.stack([norm_attn, norm_ffn]), n_wa)
-    gains = gains.transpose(1, 0, 2).reshape(2, width).astype(F32)
-    w_qkv = gather_rows(jnp.concatenate([w_query, w_key, w_value], axis=1), n_wa)
-    w_qkv = w_qkv.reshape(width, q_width + 2 * k_width)
-    w_o = gather_rows(w_out, n_wa).reshape(q_width, width)
-
-    def take_columns(device):
-        return jnp.concatenate(
-            [
-                lax.dynamic_slice_in_dim(w, device * ff_part, ff_part, 1)
-                for w in (w_gate, w_up)
-            ],
-            axis=1,
-        )
-
-    def place_rows(result, block, device):
-        if result is None:
-            result = jnp.zeros((width, 2 * ff_part), BF)
-        return lax.dynamic_update_slice_in_dim(result, block, device * shard, 0)
-
-    w_gu = exchange_blocks(take_columns, n_wa, place_rows)
-    dy_all = [gather_relative(cotangent[i], n_wa) for i in each]
+    gain_rows = jnp.pad(jnp.stack([norm_attn, norm_ffn]), ((0, 6), (0, 2 * k_width - shard)))
+    kv_steps = gather_rows(
+        jnp.concatenate([jnp.concatenate([w_key, w_value], axis=1), gain_rows], axis=0), n_wa, shard
+    )
+    got = next(kv_steps)
+    q_steps = gather_rows(after(w_query, got), n_wa)
+    got = next(q_steps)
+    o_steps = gather_rows(after(w_out, got), n_wa)
+    got = next(o_steps)
+    w_gu = jnp.stack(
+        [
+            jnp.concatenate([w[:, j * ff_part : (j + 1) * ff_part] for w in (w_gate, w_up)], axis=1)
+            for j in range(n_wa)
+        ]
+    )
+    gu_steps = exchange_blocks(after(w_gu, got), n_wa)
+    got = next(gu_steps)
+    dy_all = gather_relative(after(cotangent, got)[None], n_wa)
+    dy_all = [dy_all[:, i].reshape(-1, width) for i in each]
+    w_kv, gains = complete(kv_steps)
+    gains = gains[:, :2, :shard].transpose(1, 0, 2).reshape(2, width).astype(F32)
 
     half = HEAD // 2
     frequency = 10000.0 ** (-jnp.arange(half).astype(F32) / half)
@@ -378,20 +422,32 @@
 
     biases = [bias_of(order) for order in orders]
 
-    x, h1, r1, q, kv = [], [], [], [], []
+    x, h1, r1, kv = [], [], [], []
     for i in each:
         xi = tokens[i].astype(F32)
         hi, ri = rms(xi, gains[0])
         hi = hi.astype(BF)
-        qkv = mm(w_qkv, hi, 0, 1)
-        qi = turn(qkv[:q_width], cosines, sines).astype(BF) * BF(HEAD ** (-0.5))
-        ki = turn(qkv[q_width : q_width + k_width], cosines, sines).astype(BF)
-        vi = qkv[q_width + k_width :].astype(BF)
+        kvi = mm(w_kv, hi, 0, 1)
+        ki = turn(kvi[:k_width], cosines, sines).astype(BF)
+        vi = kvi[k_width:].astype(BF)
         x.append(xi)
         h1.append(hi)
         r1.append(ri)
-        q.append(qi)
-        kv.append(doubled(jnp.concatenate([ki, vi], axis=0)[None], n_ctx, orders[i]))
+        kv.append(Chain(doubled(jnp.concatenate([ki, vi], axis=0)[None], n_ctx, orders[i])))
+    sent = [chain.pending for chain in kv]
+    for chain in kv:
+        chain.issue()
+    w_q, _ = complete(q_steps, sent)
+    q = [
+        turn(mm(w_q, hi, 0, 1), cosines, sines).astype(BF) * BF(HEAD ** (-0.5)) for hi in h1
+    ]
+    sent = [chain.pending for chain in kv]
+    for chain in kv:
+        chain.issue()
+    w_o, _ = complete(o_steps, sent)
+    sent = [chain.pending for chain in kv]
+    w_gu = complete(gu_steps, sent).reshape(width, 2 * ff_part)
+    kv = [chain.finish() for chain in kv]
 
     o, lse, o_b, x1, r2, h2_all = [], [], [], [], [], []
     for i in each:
@@ -427,56 +483,48 @@
     dy_cat = jnp.concatenate(dy_all, axis=0)
 
     low_first = list(range(c_bits))
-    middle_first = low_first[1:] + low_first[:1]
     g_gu = mm(h2_cat, dgu_all, 0, 0).astype(BF).reshape(n_wa, shard, 2 * ff_part)
     g_down = mm(act_all, dy_cat, 0, 0).astype(BF)
-    gu_part, gu_trail = reduce_halves(
-        g_gu, n_ctx, [(bit, 2 if index == 0 else 1) for index, bit in enumerate(low_first)]
-    )
-
-    def place_sources(result, block, device):
-        if result is None:
-            result = jnp.zeros_like(gu_part)
-        return lax.dynamic_update_slice_in_dim(result, block, device, 0)
-
-    gu_part = exchange_blocks(
-        lambda device: lax.dynamic_slice_in_dim(gu_part, device, 1, 0), n_wa, place_sources
-    )
-    g_gu = gather_halves(gu_part, n_ctx, gu_trail)
-    g_gate, g_up = [
-        g_gu[:, :, s * ff_part : (s + 1) * ff_part]
-        .transpose(1, 0, 2)
-        .reshape(shard, n_wa * ff_part)
-        .astype(F32)
-        for s in range(2)
-    ]
-    g_down = all_reduce_ctx(g_down, n_ctx, [(bit, 0) for bit in middle_first]).astype(F32)
-
-    dx1, dx1_b, dq_b, dkv, dg2 = [], [], [], [], []
+    g_down_sum = lax.psum(g_down, "ctx")
+    g_gu_sum = lax.psum(g_gu, "ctx")
+    dh2[0] = after(dh2[0], g_gu)
+    dh2[0] = after(dh2[0], g_down)
+
+    dx1, dx1_b, dq_b, dkv, dg2, do = [], [], [], [], [], []
     for i in each:
         norm_part, dgi = rms_back(dh2[i], x1[i], r2[i], gains[1])
         dx1i = cotangent[i].astype(F32) + norm_part
         dx1b = dx1i.astype(BF)
-        do = mm(w_o, dx1b, 1, 1).astype(BF)
-        dqi, dkvi = attend_back(groups, per_group, q[i], kv[i], biases[i], lse[i], do, o[i])
         dx1.append(dx1i)
         dx1_b.append(dx1b)
         dg2.append(dgi)
+        do.append(mm(w_o, dx1b, 1, 1).astype(BF))
+    for i in each:
+        doi = do[i]
+        if i > 0:
+            doi = dkv[-1].issue(doi)
+        dqi, dkvi = attend_back(groups, per_group, q[i], kv[i], biases[i], lse[i], doi, o[i])
         dq_b.append(turn(dqi, cosines, sines, back=True).astype(BF))
-        dkv.append(halved(dkvi, n_ctx, orders[i])[0])
+        dkv.append(Chain(halved(dkvi, n_ctx, orders[i])))
 
     h1_cat = jnp.concatenate(h1, axis=0)
-    g_out = mm(jnp.concatenate(o_b, axis=1), jnp.concatenate(dx1_b, axis=0), 1, 0)
+    dx1_cat = dkv[-1].issue(jnp.concatenate(dx1_b, axis=0))
+    g_out = mm(jnp.concatenate(o_b, axis=1), dx1_cat, 1, 0)
     g_query = mm(h1_cat, jnp.concatenate(dq_b, axis=1), 0, 1)
     g_oq = jnp.concatenate([g_out, g_query], axis=1).astype(BF).reshape(n_wa, shard, -1)
-    plan = [(bit, 0) for bit in low_first]
-    g_oq = all_reduce_ctx(scatter_rows(g_oq, n_wa), n_ctx, plan).astype(F32)
+    oq = Chain(all_reduce_rows(g_oq, n_wa, n_ctx, low_first))
+    dkv[0].pending = oq.issue(dkv[0].pending)
+    for chain in dkv:
+        chain.issue()
+    dkv[0].pending = oq.issue(dkv[0].pending)
+    dkv = [chain.finish() for chain in dkv]
+    dkv[0] = oq.issue(dkv[0])
 
     input_grad, dkv_b, dg1 = [], [], []
     for i in each:
-        dk = turn(dkv[i][:k_width], cosines, sines, back=True)
-        dkvb = jnp.concatenate([dk, dkv[i][k_width:]], axis=0).astype(BF)
-        dh1 = mm(dq_b[i], w_qkv[:, :q_width], 0, 1) + mm(dkvb, w_qkv[:, q_width:], 0, 1)
+        dk = turn(dkv[i][0, :k_width], cosines, sines, back=True)
+        dkvb = jnp.concatenate([dk, dkv[i][0, k_width:]], axis=0).astype(BF)
+        dh1 = mm(dq_b[i], w_q, 0, 1) + mm(dkvb, w_kv, 0, 1)
         norm_part, dgi = rms_back(dh1, x[i], r1[i], gains[0])
         input_grad.append((dx1[i] + norm_part).astype(BF))
         dkv_b.append(dkvb)
@@ -485,7 +533,20 @@
     g_gain = jnp.stack([sum(dg1), sum(dg2)]).reshape(2, n_wa, shard).transpose(1, 0, 2)
     g_gain = jnp.pad(g_gain, ((0, 0), (0, 6), (0, g_kv.shape[2] - shard)))
     g_kv = jnp.concatenate([g_kv, g_gain], axis=1).astype(BF)
-    g_kv = all_reduce_ctx(scatter_rows(g_kv, n_wa), n_ctx, plan).astype(F32)
+    kvw = Chain(all_reduce_rows(g_kv, n_wa, n_ctx, low_first))
+    kvw.pending = oq.issue(kvw.pending)
+    g_oq, g_kv = [chain.finish().astype(F32) for chain in (oq, kvw)]
+    g_down = g_down_sum.astype(F32)
+    gu_steps = exchange_blocks(g_gu_sum, n_wa)
+    next(gu_steps)
+    g_gu = complete(gu_steps)
+    g_gate, g_up = [
+        g_gu[:, :, s * ff_part : (s + 1) * ff_part]
+        .transpose(1, 0, 2)
+        .reshape(shard, n_wa * ff_part)
+        .astype(F32)
+        for s in range(2)
+    ]
 
     return (
         jnp.stack(mixed),

time: 471 us -> 449 us (0.953)
  waiting for transfers between devices: 179 us -> 214 us
  local copies, waits for them, and re-layouts: 73.2 us -> 45.6 us
  starting transfers between devices: 69.9 us -> 45.6 us
  between operations: 2.82 us -> 16.6 us
  other arithmetic: 70.6 us -> 59.3 us
  matrix products: 41.3 us -> 33.8 us
    psum x0 -> x1, waiting for transfers between devices: none -> 60.5 us  [local(): g_gu_sum = lax.psum(g_gu, 'ctx')]
    ppermute x66 -> x55, starting transfers between devices: 66 us -> 45.5 us  [swap(): return lax.ppermute(a, axis, [(i, i ^ 1 << bit) for i in range(n)])]
    ppermute x6 -> x0, waiting for transfers between devices: 15.6 us -> none  [exchange_blocks(): got = lax.ppermute(take(me ^ step), 'wa', [(i, i ^ step) for i in range(n)])]
    dynamic_update_slice x7 -> x0, local copies, waits for them, and re-layouts: 13.2 us -> none  [the longest x4 10.5 us: place_sources(): return lax.dynamic_update_slice_in_dim(result, block, device, 0)]
    ppermute x66 -> x55, waiting for transfers between devices: 164 us -> 153 us  [swap(): return lax.ppermute(a, axis, [(i, i ^ 1 << bit) for i in range(n)])]
    convert_element_type x16 -> x12, other arithmetic: 12.2 us -> 3.13 us  [the longest x1 1.6 us: local(): g_down = g_down_sum.astype(F32)]
    dot_general x23 -> x25, matrix products: 41.3 us -> 33.8 us  [mm(): lax.dot_general(a, b, (((ca,), (cb,)), ((), ())), preferred_element_type=...]
    ppermute x5 -> x0, local copies, waits for them, and re-layouts: 6.74 us -> none  [the longest x2 3.7 us: swap(): return lax.ppermute(a, axis, [(i, i ^ 1 << bit) for i in range(n)])]
  transfers between devices with their start and end apart: 72 -> 56, of which waited for: 29 -> 27; matrix products, arithmetic and copies ran while one was open for 37% -> 25% of each run, Pallas kernels for 6% -> 6%
where the time goes in v2:
time: 449 us; the launch traced here: 443 us
  waiting for transfers between devices  214 us (48%)
  other arithmetic  59.3 us (13%)
  local copies, waits for them, and re-layouts  45.6 us (10%)
  starting transfers between devices  45.6 us (10%)
  matrix products  33.8 us (8%)
  Pallas kernels  28.1 us (6%)
  between operations  16.6 us (4%)
    ppermute x55, waiting for transfers between devices, swap(): return lax.ppermute(a, axis, [(i, i ^ 1 << bit) for i in range(n)])  153 us
    psum x1, waiting for transfers between devices, local(): g_gu_sum = lax.psum(g_gu, 'ctx')  60.5 us
    ppermute x55, starting transfers between devices, swap(): return lax.ppermute(a, axis, [(i, i ^ 1 << bit) for i in range(n)])  45.5 us
    dot_general x25, matrix products, mm(): lax.dot_general(a, b, (((ca,), (cb,)), ((), ())), preferred_element_type=...  33.8 us
    unnamed x206, local copies, waits for them, and re-layouts  18.3 us
    pallas_call x2, Pallas kernels, attend_back(): pl.pallas_call(functools.partial(attend_back_kernel, groups, per_group, m...  15.9 us
    select_n x14, other arithmetic, ordered(): jnp.where(bit == 0, jnp.concatenate([mine, theirs], axis=dim), jnp.concat...  13.9 us
    pallas_call x2, Pallas kernels, attend(): pl.pallas_call(functools.partial(attend_kernel, groups, per_group, min(sl...  12.2 us
  transfers between devices with their start and end apart: 56, of which 27 were waited for; matrix products, arithmetic and copies ran while one was open for 25% of the time, Pallas kernels for 6%

profile of v2, /device:TPU:0, one launch (start us, length us, event | category | flops | bytes accessed | tf_op | source)
XLA Modules:
  0.0 442.6 jit_solution(12932746442560067551)
XLA Ops:
  11.0 3.0 collective-permute-start
  19.2 2.3 maximum_bitcast_fusion.2
  25.0 3.2 pad_maximum_fusion
  28.3 8.8 %collective-permute-done.1 = bf16[1,1,240,960]{3,2,1,0:T(8,128)(2,1)} collective-permute-done((bf16[1,1,240,960]{3,2,1,0:T(8,128)(2,1)}, bf16[1,1,240,960]{3,2,1,0:T(8,128)(2,1)}, u32[]{:S(2)}, u32[]{:S(2)}) %collective-permute-start.1) | collective-permute-done | bytes 460832 | tf_op jit(solution)/shard_map/ppermute | solution.py:26
  42.8 2.6 collective-permute-start.4
  48.4 9.1 %collective-permute-done.4 = bf16[1,640,128]{2,1,0:T(8,128)(2,1)S(1)} collective-permute-done((bf16[1,640,128]{2,1,0:T(8,128)(2,1)S(1)}, bf16[1,640,128]{2,1,0:T(8,128)(2,1)S(1)}, u32[]{:S(2)}, u32[]{:S(2)}) %collective-permute-start.4) | collective-permute-done | bytes 163872 | tf_op jit(solution)/shard_map/ppermute | solution.py:26
  57.6 2.3 collective-permute-done.8
  61.5 2.3 maximum_select_fusion.8
  71.6 2.8 copy.41
  74.4 2.5 fusion.103
  79.4 6.3 %collective-permute-done.18 = bf16[4,640,128]{2,1,0:T(8,128)(2,1)} collective-permute-done((bf16[4,640,128]{2,1,0:T(8,128)(2,1)}, bf16[4,640,128]{2,1,0:T(8,128)(2,1)}, u32[]{:S(2)}, u32[]{:S(2)}) %collective-permute-start.18) | collective-permute-done | bytes 655392 | tf_op jit(solution)/shard_map/ppermute | solution.py:26
  85.7 2.3 pad_maximum_fusion.3.kv_ref
  88.0 6.1 %shard_map.213 = (f32[960,128]{1,0:T(8,128)}, f32[15,128]{1,0:T(8,128)}) custom-call(bf16[960,128]{1,0:T(8,128)(2,1)} %bitcast.281, bf16[8,640,128]{2,1,0:T(8,128)(2,1)} %pad_maximum_fusion.3.kv_ref, f32[1024,128]{1,0:T(8,128)} %get-tuple-element.162.bias_ref), custom_call_target="tpu_custom_call" | custom-call | flops 1006632960 | bytes 2572288 | tf_op jit(solution)/shard_map/pallas_call | solution.py:308
  95.2 2.3 pad_maximum_fusion.2.kv_ref
  97.5 6.0 %shard_map.212 = (f32[960,128]{1,0:T(8,128)}, f32[15,128]{1,0:T(8,128)}) custom-call(bf16[960,128]{1,0:T(8,128)(2,1)} %bitcast.283, bf16[8,640,128]{2,1,0:T(8,128)(2,1)} %pad_maximum_fusion.2.kv_ref, f32[1024,128]{1,0:T(8,128)} %get-tuple-element.161.bias_ref), custom_call_target="tpu_custom_call" | custom-call | flops 1006632960 | bytes 2572288 | tf_op jit(solution)/shard_map/pallas_call | solution.py:308
  104.6 2.5 maximum_select_fusion.5
  110.6 6.2 %collective-permute-done.10 = bf16[128,960]{0,1:T(8,128)(2,1)S(1)} collective-permute-done((bf16[128,960]{0,1:T(8,128)(2,1)S(1)}, bf16[128,960]{0,1:T(8,128)(2,1)S(1)}, u32[]{:S(2)}, u32[]{:S(2)}) %collective-permute-start.10) | collective-permute-done | bytes 245792 | tf_op jit(solution)/shard_map/ppermute | solution.py:26
  118.2 2.4 maximum_select_fusion
  124.9 11.3 %collective-permute-done.19 = bf16[128,960]{0,1:T(8,128)(2,1)} collective-permute-done((bf16[128,960]{0,1:T(8,128)(2,1)}, bf16[128,960]{0,1:T(8,128)(2,1)}, u32[]{:S(2)}, u32[]{:S(2)}) %collective-permute-start.19) | collective-permute-done | bytes 245792 | tf_op jit(solution)/shard_map/ppermute | solution.py:26
  136.8 2.0 fusion.71
  145.7 2.1 maximum_select_fusion.1
  147.8 2.6 fusion.37
  163.7 2.7 fusion.13
  170.5 5.0 %collective-permute-done.28 = bf16[128,960]{0,1:T(8,128)(2,1)S(1)} collective-permute-done((bf16[128,960]{0,1:T(8,128)(2,1)S(1)}, bf16[128,960]{0,1:T(8,128)(2,1)S(1)}, u32[]{:S(2)}, u32[]{:S(2)}) %collective-permute-start.28) | collective-permute-done | bytes 245792 | tf_op jit(solution)/shard_map/ppermute | solution.py:26
  175.6 5.2 %collective-permute-done.31 = bf16[128,960]{0,1:T(8,128)(2,1)S(1)} collective-permute-done((bf16[128,960]{0,1:T(8,128)(2,1)S(1)}, bf16[128,960]{0,1:T(8,128)(2,1)S(1)}, u32[]{:S(2)}, u32[]{:S(2)}) %collective-permute-start.31) | collective-permute-done | bytes 245792 | tf_op jit(solution)/shard_map/ppermute | solution.py:26
  181.4 3.8 collective-permute-done.23
  185.2 2.3 fusion.146
  190.3 7.8 %shard_map.214 = (f32[960,128]{1,0:T(8,128)}, bf16[8,640,128]{2,1,0:T(8,128)(2,1)}) custom-call(bf16[960,128]{1,0:T(8,128)(2,1)} %bitcast.284, bf16[8,640,128]{2,1,0:T(8,128)(2,1)} %pad_maximum_fusion.2.kv_ref, f32[1024,128]{1,0:T(8,128)} %get-tuple-element.161.bias_ref, f32[15,128]{1,0:T(8,128)} %get-tuple-element.49.lse_ref, ...), custom_call_target="tpu_custom_call" | custom-call | flops 2516582400 | bytes 4620288 | tf_op jit(solution)/shard_map/pallas_call | solution.py:327
  198.2 2.0 slice.332
  200.1 8.1 %shard_map.215 = (f32[960,128]{1,0:T(8,128)}, bf16[8,640,128]{2,1,0:T(8,128)(2,1)}) custom-call(bf16[960,128]{1,0:T(8,128)(2,1)} %bitcast.282, bf16[8,640,128]{2,1,0:T(8,128)(2,1)} %pad_maximum_fusion.3.kv_ref, f32[1024,128]{1,0:T(8,128)} %get-tuple-element.162.bias_ref, f32[15,128]{1,0:T(8,128)} %get-tuple-element.52.lse_ref, ...), custom_call_target="tpu_custom_call" | custom-call | flops 2516582400 | bytes 4620288 | tf_op jit(solution)/shard_map/pallas_call | solution.py:327
  208.2 2.1 slice.340
  214.4 1.8 fusion.12
  218.0 4.1 convolution_convert_fusion
  230.4 15.2 %collective-permute-done.29 = bf16[4,640,128]{2,1,0:T(8,128)(2,1)} collective-permute-done((bf16[4,640,128]{2,1,0:T(8,128)(2,1)}, bf16[4,640,128]{2,1,0:T(8,128)(2,1)}, u32[]{:S(2)}, u32[]{:S(2)}) %collective-permute-start.29) | collective-permute-done | bytes 655392 | tf_op jit(solution)/shard_map/ppermute | solution.py:26
  247.2 10.2 %collective-permute-done.37 = bf16[2,640,128]{2,1,0:T(8,128)(2,1)} collective-permute-done((bf16[2,640,128]{2,1,0:T(8,128)(2,1)}, bf16[2,640,128]{2,1,0:T(8,128)(2,1)}, u32[]{:S(2)}, u32[]{:S(2)}) %collective-permute-start.37) | collective-permute-done | bytes 327712 | tf_op jit(solution)/shard_map/ppermute | solution.py:26
  258.6 4.4 %collective-permute-start.38 = (bf16[1,640,128]{2,1,0:T(8,128)(2,1)S(1)}, bf16[1,640,128]{2,1,0:T(8,128)(2,1)S(1)}, u32[]{:S(2)}, u32[]{:S(2)}) collective-permute-start(bf16[1,640,128]{2,1,0:T(8,128)(2,1)S(1)} %slice.423), channel_id=1, source_target_pairs={{0,16},{4,20},{8,24},{12,28},{16,0},{20,4},{24,8},{28,12},{1,17},{... | collective-permute-start | bytes 491528 | tf_op jit(solution)/shard_map/ppermute | solution.py:26
  263.0 2.4 add_convert_fusion
  265.6 6.0 %collective-permute-done.32 = bf16[2,640,128]{2,1,0:T(8,128)(2,1)S(1)} collective-permute-done((bf16[2,640,128]{2,1,0:T(8,128)(2,1)S(1)}, bf16[2,640,128]{2,1,0:T(8,128)(2,1)S(1)}, u32[]{:S(2)}, u32[]{:S(2)}) %collective-permute-start.32) | collective-permute-done | bytes 327712 | tf_op jit(solution)/shard_map/ppermute | solution.py:26
  271.7 9.2 %collective-permute-done.38 = bf16[1,640,128]{2,1,0:T(8,128)(2,1)S(1)} collective-permute-done((bf16[1,640,128]{2,1,0:T(8,128)(2,1)S(1)}, bf16[1,640,128]{2,1,0:T(8,128)(2,1)S(1)}, u32[]{:S(2)}, u32[]{:S(2)}) %collective-permute-start.38) | collective-permute-done | bytes 163872 | tf_op jit(solution)/shard_map/ppermute | solution.py:26
  281.1 11.9 %collective-permute-done.34 = bf16[1,640,128]{2,1,0:T(8,128)(2,1)S(1)} collective-permute-done((bf16[1,640,128]{2,1,0:T(8,128)(2,1)S(1)}, bf16[1,640,128]{2,1,0:T(8,128)(2,1)S(1)}, u32[]{:S(2)}, u32[]{:S(2)}) %collective-permute-start.34) | collective-permute-done | bytes 163872 | tf_op jit(solution)/shard_map/ppermute | solution.py:26
  301.2 8.5 %collective-permute-done.39 = bf16[120,1920]{1,0:T(8,128)(2,1)} collective-permute-done((bf16[120,1920]{1,0:T(8,128)(2,1)}, bf16[120,1920]{1,0:T(8,128)(2,1)}, u32[]{:S(2)}, u32[]{:S(2)}) %collective-permute-start.39) | collective-permute-done | bytes 460832 | tf_op jit(solution)/shard_map/ppermute | solution.py:26
  312.6 6.4 %collective-permute-done.40 = bf16[64,1920]{1,0:T(8,128)(2,1)S(1)} collective-permute-done((bf16[64,1920]{1,0:T(8,128)(2,1)S(1)}, bf16[64,1920]{1,0:T(8,128)(2,1)S(1)}, u32[]{:S(2)}, u32[]{:S(2)}) %collective-permute-start.40) | collective-permute-done | bytes 245792 | tf_op jit(solution)/shard_map/ppermute | solution.py:26
  320.9 9.1 %collective-permute-done.41 = bf16[32,1920]{1,0:T(8,128)(2,1)S(1)} collective-permute-done((bf16[32,1920]{1,0:T(8,128)(2,1)S(1)}, bf16[32,1920]{1,0:T(8,128)(2,1)S(1)}, u32[]{:S(2)}, u32[]{:S(2)}) %collective-permute-start.41) | collective-permute-done | bytes 122912 | tf_op jit(solution)/shard_map/ppermute | solution.py:26
  330.4 60.5 %all-reduce.5.cloned.1.call-done = (bf16[2,2,240,1280]{3,2,1,0:T(8,128)(2,1)}, bf16[640,960]{0,1:T(8,128)(2,1)}) async-done(((bf16[2,2,240,1280]{3,2,1,0:T(8,128)(2,1)}, bf16[640,960]{0,1:T(8,128)(2,1)}), (bf16[2,2,240,1280]{3,2,1,0:T(8,128)(2,1)}, bf16[640,960]{0,1:T(8,128)(2,1)})) %all-reduce.5.cloned.1.call-update) | async-done | bytes 3686416 | tf_op jit(solution)/shard_map/psum | solution.py:489
  396.1 5.7 %collective-permute-done.43 = bf16[64,1920]{1,0:T(8,128)(2,1)S(1)} collective-permute-done((bf16[64,1920]{1,0:T(8,128)(2,1)S(1)}, bf16[64,1920]{1,0:T(8,128)(2,1)S(1)}, u32[]{:S(2)}, u32[]{:S(2)}) %collective-permute-start.43) | collective-permute-done | bytes 245792 | tf_op jit(solution)/shard_map/ppermute | solution.py:26
  402.3 4.1 collective-permute-done.48
  409.6 2.0 collective-permute-done.49
  418.3 3.1 collective-permute-done.51
  (460 shorter events, 131.2 us)
Async XLA Ops:
  7.2 383.7 %all-reduce.5.cloned.1.call-start = ((), (), s32[]{:S(2)}) async-start(), calls=%async_computation | async-start | bytes 7372800 | tf_op jit(solution)/shard_map/psum | solution.py:489
  11.0 10.6 %collective-permute-start = (bf16[1,1,248,640]{3,2,1,0:T(8,128)(2,1)S(1)}, bf16[1,1,248,640]{3,2,1,0:T(8,128)(2,1)}, u32[]{:S(2)}, u32[]{:S(2)}) collective-permute-start(bf16[1,1,248,640]{3,2,1,0:T(8,128)(2,1)S(1)} %maximum_bitcast_fusion.4), channel_id=1, source_target_pairs={{0,2},{1,3},{2,0},{3,1},{4,6},{5,7},{6,4},{7,5},{8,10},{9,11},{10,... | collective-permute-start | bytes 952328 | tf_op jit(solution)/shard_map/ppermute | solution.py:26
  22.9 16.0 %collective-permute-start.2 = (bf16[2,1,248,640]{3,2,1,0:T(8,128)(2,1)S(1)}, bf16[2,1,248,640]{3,2,1,0:T(8,128)(2,1)}, u32[]{:S(2)}, u32[]{:S(2)}) collective-permute-start(bf16[2,1,248,640]{3,2,1,0:T(8,128)(2,1)S(1)} %maximum_select_fusion.10), channel_id=1, source_target_pairs={{0,1},{1,0},{2,3},{3,2},{4,5},{5,4},{6,7},{7,6},{8,9},{9,8},{10,11... | collective-permute-start | bytes 1904648 | tf_op jit(solution)/shard_map/ppermute | solution.py:26
  23.1 14.0 %collective-permute-start.1 = (bf16[1,1,240,960]{3,2,1,0:T(8,128)(2,1)}, bf16[1,1,240,960]{3,2,1,0:T(8,128)(2,1)}, u32[]{:S(2)}, u32[]{:S(2)}) collective-permute-start(bf16[1,1,240,960]{3,2,1,0:T(8,128)(2,1)} %bitcast.2), channel_id=1, source_target_pairs={{0,2},{1,3},{2,0},{3,1},{4,6},{5,7},{6,4},{7,5},{8,10},{9,11},{10,... | collective-permute-start | bytes 1382408 | tf_op jit(solution)/shard_map/ppermute | solution.py:26
  37.1 24.4 %collective-permute-start.7 = (bf16[1,1,240,960]{3,2,1,0:T(8,128)(2,1)S(1)}, bf16[1,1,240,960]{3,2,1,0:T(8,128)(2,1)}, u32[]{:S(2)}, u32[]{:S(2)}) collective-permute-start(bf16[1,1,240,960]{3,2,1,0:T(8,128)(2,1)S(1)} %bitcast.269), channel_id=1, source_target_pairs={{0,2},{1,3},{2,0},{3,1},{4,6},{5,7},{6,4},{7,5},{8,10},{9,11},{10,... | collective-permute-start | bytes 1382408 | tf_op jit(solution)/shard_map/ppermute | solution.py:26
  42.8 14.7 %collective-permute-start.4 = (bf16[1,640,128]{2,1,0:T(8,128)(2,1)S(1)}, bf16[1,640,128]{2,1,0:T(8,128)(2,1)S(1)}, u32[]{:S(2)}, u32[]{:S(2)}) collective-permute-start(bf16[1,640,128]{2,1,0:T(8,128)(2,1)S(1)} %maximum_bitcast_fusion.5), channel_id=1, source_target_pairs={{0,16},{4,20},{8,24},{12,28},{16,0},{20,4},{24,8},{28,12},{1,17},{... | collective-permute-start | bytes 491528 | tf_op jit(solution)/shard_map/ppermute | solution.py:26
  45.5 14.5 %collective-permute-start.8 = (bf16[1,640,128]{2,1,0:T(8,128)(2,1)S(1)}, bf16[1,640,128]{2,1,0:T(8,128)(2,1)S(1)}, u32[]{:S(2)}, u32[]{:S(2)}) collective-permute-start(bf16[1,640,128]{2,1,0:T(8,128)(2,1)S(1)} %maximum_bitcast_fusion.6), channel_id=1, source_target_pairs={{0,16},{4,20},{8,24},{12,28},{16,0},{20,4},{24,8},{28,12},{1,17},{... | collective-permute-start | bytes 491528 | tf_op jit(solution)/shard_map/ppermute | solution.py:26
  48.4 22.8 %collective-permute-start.3 = (bf16[2,1,240,960]{3,2,1,0:T(8,128)(2,1)S(1)}, bf16[2,1,240,960]{3,2,1,0:T(8,128)(2,1)S(1)}, u32[]{:S(2)}, u32[]{:S(2)}) collective-permute-start(bf16[2,1,240,960]{3,2,1,0:T(8,128)(2,1)S(1)} %maximum_select_fusion.7), channel_id=1, source_target_pairs={{0,1},{1,0},{2,3},{3,2},{4,5},{5,4},{6,7},{7,6},{8,9},{9,8},{10,11... | collective-permute-start | bytes 2764808 | tf_op jit(solution)/shard_map/ppermute | solution.py:26
  57.5 9.3 %collective-permute-start.5 = (bf16[2,640,128]{2,1,0:T(8,128)(2,1)S(1)}, bf16[2,640,128]{2,1,0:T(8,128)(2,1)S(1)}, u32[]{:S(2)}, u32[]{:S(2)}) collective-permute-start(bf16[2,640,128]{2,1,0:T(8,128)(2,1)S(1)} %pad_maximum_fusion.11), channel_id=1, source_target_pairs={{0,8},{4,12},{8,0},{12,4},{16,24},{20,28},{24,16},{28,20},{1,9},{5... | collective-permute-start | bytes 983048 | tf_op jit(solution)/shard_map/ppermute | solution.py:26
  60.0 9.3 %collective-permute-start.14 = (bf16[2,640,128]{2,1,0:T(8,128)(2,1)S(1)}, bf16[2,640,128]{2,1,0:T(8,128)(2,1)S(1)}, u32[]{:S(2)}, u32[]{:S(2)}) collective-permute-start(bf16[2,640,128]{2,1,0:T(8,128)(2,1)S(1)} %pad_maximum_fusion.12), channel_id=1, source_target_pairs={{0,4},{4,0},{8,12},{12,8},{16,20},{20,16},{24,28},{28,24},{1,5},{5... | collective-permute-start | bytes 983048 | tf_op jit(solution)/shard_map/ppermute | solution.py:26
  63.9 40.7 %collective-permute-start.9 = (bf16[2,1,240,960]{3,2,1,0:T(8,128)(2,1)}, bf16[2,1,240,960]{3,2,1,0:T(8,128)(2,1)}, u32[]{:S(2)}, u32[]{:S(2)}) collective-permute-start(bf16[2,1,240,960]{3,2,1,0:T(8,128)(2,1)} %maximum_select_fusion.8), channel_id=1, source_target_pairs={{0,1},{1,0},{2,3},{3,2},{4,5},{5,4},{6,7},{7,6},{8,9},{9,8},{10,11... | collective-permute-start | bytes 2764808 | tf_op jit(solution)/shard_map/ppermute | solution.py:26
  65.5 51.5 %collective-permute-start.13 = (bf16[1,2,240,1280]{3,2,1,0:T(8,128)(2,1)}, bf16[1,2,240,1280]{3,2,1,0:T(8,128)(2,1)}, u32[]{:S(2)}, u32[]{:S(2)}) collective-permute-start(bf16[1,2,240,1280]{3,2,1,0:T(8,128)(2,1)} %get-tuple-element.107), channel_id=1, source_target_pairs={{0,2},{1,3},{2,0},{3,1},{4,6},{5,7},{6,4},{7,5},{8,10},{9,11},{10,... | collective-permute-start | bytes 3686408 | tf_op jit(solution)/shard_map/ppermute | solution.py:26
  67.8 27.4 %collective-permute-start.6 = (bf16[4,640,128]{2,1,0:T(8,128)(2,1)}, bf16[4,640,128]{2,1,0:T(8,128)(2,1)}, u32[]{:S(2)}, u32[]{:S(2)}) collective-permute-start(bf16[4,640,128]{2,1,0:T(8,128)(2,1)} %pad_maximum_fusion.4), channel_id=1, source_target_pairs={{0,4},{4,0},{8,12},{12,8},{16,20},{20,16},{24,28},{28,24},{1,5},{5... | collective-permute-start | bytes 1966088 | tf_op jit(solution)/shard_map/ppermute | solution.py:26
  70.3 15.4 %collective-permute-start.18 = (bf16[4,640,128]{2,1,0:T(8,128)(2,1)}, bf16[4,640,128]{2,1,0:T(8,128)(2,1)}, u32[]{:S(2)}, u32[]{:S(2)}) collective-permute-start(bf16[4,640,128]{2,1,0:T(8,128)(2,1)} %pad_maximum_fusion.5), channel_id=1, source_target_pairs={{0,8},{4,12},{8,0},{12,4},{16,24},{20,28},{24,16},{28,20},{1,9},{5... | collective-permute-start | bytes 1966088 | tf_op jit(solution)/shard_map/ppermute | solution.py:26
  108.3 8.5 %collective-permute-start.11 = (bf16[128,960]{0,1:T(8,128)(2,1)S(1)}, bf16[128,960]{0,1:T(8,128)(2,1)S(1)}, u32[]{:S(2)}, u32[]{:S(2)}) collective-permute-start(bf16[128,960]{0,1:T(8,128)(2,1)S(1)} %get-tuple-element.89), channel_id=1, source_target_pairs={{0,1},{1,0},{2,3},{3,2},{4,5},{5,4},{6,7},{7,6},{8,9},{9,8},{10,11... | collective-permute-start | bytes 737288 | tf_op jit(solution)/shard_map/ppermute | solution.py:26
  108.4 8.4 %collective-permute-start.10 = (bf16[128,960]{0,1:T(8,128)(2,1)S(1)}, bf16[128,960]{0,1:T(8,128)(2,1)S(1)}, u32[]{:S(2)}, u32[]{:S(2)}) collective-permute-start(bf16[128,960]{0,1:T(8,128)(2,1)S(1)} %get-tuple-element.89), channel_id=1, source_target_pairs={{0,2},{1,3},{2,0},{3,1},{4,6},{5,7},{6,4},{7,5},{8,10},{9,11},{10,... | collective-permute-start | bytes 737288 | tf_op jit(solution)/shard_map/ppermute | solution.py:26
  117.0 19.3 %collective-permute-start.24 = (bf16[1,2,128,960]{2,3,1,0:T(8,128)(2,1)}, bf16[1,2,128,960]{2,3,1,0:T(8,128)(2,1)}, u32[]{:S(2)}, u32[]{:S(2)}) collective-permute-start(bf16[1,2,128,960]{2,3,1,0:T(8,128)(2,1)} %bitcast.35), channel_id=1, source_target_pairs={{0,2},{1,3},{2,0},{3,1},{4,6},{5,7},{6,4},{7,5},{8,10},{9,11},{10,... | collective-permute-start | bytes 1474568 | tf_op jit(solution)/shard_map/ppermute | solution.py:26
  121.8 14.5 %collective-permute-start.19 = (bf16[128,960]{0,1:T(8,128)(2,1)}, bf16[128,960]{0,1:T(8,128)(2,1)}, u32[]{:S(2)}, u32[]{:S(2)}) collective-permute-start(bf16[128,960]{0,1:T(8,128)(2,1)} %get-tuple-element.87), channel_id=1, source_target_pairs={{0,2},{1,3},{2,0},{3,1},{4,6},{5,7},{6,4},{7,5},{8,10},{9,11},{10,... | collective-permute-start | bytes 737288 | tf_op jit(solution)/shard_map/ppermute | solution.py:26
  124.3 21.1 %collective-permute-start.15 = (bf16[2,1,240,1280]{3,2,1,0:T(8,128)(2,1)}, bf16[2,1,240,1280]{3,2,1,0:T(8,128)(2,1)}, u32[]{:S(2)}, u32[]{:S(2)}) collective-permute-start(bf16[2,1,240,1280]{3,2,1,0:T(8,128)(2,1)} %get-tuple-element.105), channel_id=1, source_target_pairs={{0,1},{1,0},{2,3},{3,2},{4,5},{5,4},{6,7},{7,6},{8,9},{9,8},{10,11... | collective-permute-start | bytes 3686408 | tf_op jit(solution)/shard_map/ppermute | solution.py:26
  124.4 17.6 %collective-permute-start.25 = (bf16[1,2,128,960]{2,3,1,0:T(8,128)(2,1)}, bf16[1,2,128,960]{2,3,1,0:T(8,128)(2,1)S(1)}, u32[]{:S(2)}, u32[]{:S(2)}) collective-permute-start(bf16[1,2,128,960]{2,3,1,0:T(8,128)(2,1)} %bitcast.35), channel_id=1, source_target_pairs={{0,1},{1,0},{2,3},{3,2},{4,5},{5,4},{6,7},{7,6},{8,9},{9,8},{10,11... | collective-permute-start | bytes 1474568 | tf_op jit(solution)/shard_map/ppermute | solution.py:26
  124.8 15.7 %collective-permute-start.20 = (bf16[128,960]{0,1:T(8,128)(2,1)}, bf16[128,960]{0,1:T(8,128)(2,1)S(1)}, u32[]{:S(2)}, u32[]{:S(2)}) collective-permute-start(bf16[128,960]{0,1:T(8,128)(2,1)} %get-tuple-element.87), channel_id=1, source_target_pairs={{0,1},{1,0},{2,3},{3,2},{4,5},{5,4},{6,7},{7,6},{8,9},{9,8},{10,11... | collective-permute-start | bytes 737288 | tf_op jit(solution)/shard_map/ppermute | solution.py:26
  136.3 5.6 %collective-permute-start.26 = (bf16[1,2,128,960]{2,3,1,0:T(8,128)(2,1)}, bf16[1,2,128,960]{2,3,1,0:T(8,128)(2,1)S(1)}, u32[]{:S(2)}, u32[]{:S(2)}) collective-permute-start(bf16[1,2,128,960]{2,3,1,0:T(8,128)(2,1)} %collective-permute-done.24), channel_id=1, source_target_pairs={{0,1},{1,0},{2,3},{3,2},{4,5},{5,4},{6,7},{7,6},{8,9},{9,8},{10,11... | collective-permute-start | bytes 1474568 | tf_op jit(solution)/shard_map/ppermute | solution.py:26
  158.2 8.2 %collective-permute-start.27 = (bf16[256,960]{0,1:T(8,128)(2,1)S(1)}, bf16[256,960]{0,1:T(8,128)(2,1)S(1)}, u32[]{:S(2)}, u32[]{:S(2)}) collective-permute-start(bf16[256,960]{0,1:T(8,128)(2,1)S(1)} %slice.573), channel_id=1, source_target_pairs={{0,1},{1,0},{2,3},{3,2},{4,5},{5,4},{6,7},{7,6},{8,9},{9,8},{10,11... | collective-permute-start | bytes 1474568 | tf_op jit(solution)/shard_map/ppermute | solution.py:26
  158.3 9.6 %collective-permute-start.30 = (bf16[256,960]{0,1:T(8,128)(2,1)S(1)}, bf16[256,960]{0,1:T(8,128)(2,1)S(1)}, u32[]{:S(2)}, u32[]{:S(2)}) collective-permute-start(bf16[256,960]{0,1:T(8,128)(2,1)S(1)} %slice.572), channel_id=1, source_target_pairs={{0,1},{1,0},{2,3},{3,2},{4,5},{5,4},{6,7},{7,6},{8,9},{9,8},{10,11... | collective-permute-start | bytes 1474568 | tf_op jit(solution)/shard_map/ppermute | solution.py:26
  160.0 9.0 %collective-permute-start.22 = (bf16[256,960]{0,1:T(8,128)(2,1)S(1)}, bf16[256,960]{0,1:T(8,128)(2,1)S(1)}, u32[]{:S(2)}, u32[]{:S(2)}) collective-permute-start(bf16[256,960]{0,1:T(8,128)(2,1)S(1)} %slice.574), channel_id=1, source_target_pairs={{0,1},{1,0},{2,3},{3,2},{4,5},{5,4},{6,7},{7,6},{8,9},{9,8},{10,11... | collective-permute-start | bytes 1474568 | tf_op jit(solution)/shard_map/ppermute | solution.py:26
  163.3 60.5 %collective-permute-start.16 = (bf16[256,960]{0,1:T(8,128)(2,1)}, bf16[256,960]{0,1:T(8,128)(2,1)}, u32[]{:S(2)}, u32[]{:S(2)}) collective-permute-start(bf16[256,960]{0,1:T(8,128)(2,1)} %slice.575), channel_id=1, source_target_pairs={{0,1},{1,0},{2,3},{3,2},{4,5},{5,4},{6,7},{7,6},{8,9},{9,8},{10,11... | collective-permute-start | bytes 1474568 | tf_op jit(solution)/shard_map/ppermute | solution.py:26
  166.6 8.9 %collective-permute-start.28 = (bf16[128,960]{0,1:T(8,128)(2,1)S(1)}, bf16[128,960]{0,1:T(8,128)(2,1)S(1)}, u32[]{:S(2)}, u32[]{:S(2)}) collective-permute-start(bf16[128,960]{0,1:T(8,128)(2,1)S(1)} %slice.577), channel_id=1, source_target_pairs={{0,2},{1,3},{2,0},{3,1},{4,6},{5,7},{6,4},{7,5},{8,10},{9,11},{10,... | collective-permute-start | bytes 737288 | tf_op jit(solution)/shard_map/ppermute | solution.py:26
  168.1 12.7 %collective-permute-start.31 = (bf16[128,960]{0,1:T(8,128)(2,1)S(1)}, bf16[128,960]{0,1:T(8,128)(2,1)S(1)}, u32[]{:S(2)}, u32[]{:S(2)}) collective-permute-start(bf16[128,960]{0,1:T(8,128)(2,1)S(1)} %slice.576), channel_id=1, source_target_pairs={{0,2},{1,3},{2,0},{3,1},{4,6},{5,7},{6,4},{7,5},{8,10},{9,11},{10,... | collective-permute-start | bytes 737288 | tf_op jit(solution)/shard_map/ppermute | solution.py:26
  169.2 16.0 %collective-permute-start.23 = (bf16[128,960]{0,1:T(8,128)(2,1)S(1)}, bf16[128,960]{0,1:T(8,128)(2,1)S(1)}, u32[]{:S(2)}, u32[]{:S(2)}) collective-permute-start(bf16[128,960]{0,1:T(8,128)(2,1)S(1)} %slice.578), channel_id=1, source_target_pairs={{0,2},{1,3},{2,0},{3,1},{4,6},{5,7},{6,4},{7,5},{8,10},{9,11},{10,... | collective-permute-start | bytes 737288 | tf_op jit(solution)/shard_map/ppermute | solution.py:26
  210.3 16.9 %collective-permute-start.36 = (bf16[4,640,128]{2,1,0:T(8,128)(2,1)}, bf16[4,640,128]{2,1,0:T(8,128)(2,1)}, u32[]{:S(2)}, u32[]{:S(2)}) collective-permute-start(bf16[4,640,128]{2,1,0:T(8,128)(2,1)} %slice.340), channel_id=1, source_target_pairs={{0,8},{4,12},{8,0},{12,4},{16,24},{20,28},{24,16},{28,20},{1,9},{5... | collective-permute-start | bytes 1966088 | tf_op jit(solution)/shard_map/ppermute | solution.py:26
  216.3 46.7 %collective-permute-start.33 = (bf16[2,1,240,1920]{3,2,1,0:T(8,128)(2,1)}, bf16[2,1,240,1920]{3,2,1,0:T(8,128)(2,1)}, u32[]{:S(2)}, u32[]{:S(2)}) collective-permute-start(bf16[2,1,240,1920]{3,2,1,0:T(8,128)(2,1)} %fusion.12), channel_id=1, source_target_pairs={{0,1},{1,0},{2,3},{3,2},{4,5},{5,4},{6,7},{7,6},{8,9},{9,8},{10,11... | collective-permute-start | bytes 5529608 | tf_op jit(solution)/shard_map/ppermute | solution.py:26
  222.1 23.5 %collective-permute-start.29 = (bf16[4,640,128]{2,1,0:T(8,128)(2,1)}, bf16[4,640,128]{2,1,0:T(8,128)(2,1)}, u32[]{:S(2)}, u32[]{:S(2)}) collective-permute-start(bf16[4,640,128]{2,1,0:T(8,128)(2,1)} %slice.332), channel_id=1, source_target_pairs={{0,4},{4,0},{8,12},{12,8},{16,20},{20,16},{24,28},{28,24},{1,5},{5... | collective-permute-start | bytes 1966088 | tf_op jit(solution)/shard_map/ppermute | solution.py:26
  226.6 84.3 %collective-permute-start.17 = (bf16[128,960]{0,1:T(8,128)(2,1)}, bf16[128,960]{0,1:T(8,128)(2,1)}, u32[]{:S(2)}, u32[]{:S(2)}) collective-permute-start(bf16[128,960]{0,1:T(8,128)(2,1)} %slice.579), channel_id=1, source_target_pairs={{0,2},{1,3},{2,0},{3,1},{4,6},{5,7},{6,4},{7,5},{8,10},{9,11},{10,... | collective-permute-start | bytes 737288 | tf_op jit(solution)/shard_map/ppermute | solution.py:26
  229.4 28.0 %collective-permute-start.37 = (bf16[2,640,128]{2,1,0:T(8,128)(2,1)}, bf16[2,640,128]{2,1,0:T(8,128)(2,1)}, u32[]{:S(2)}, u32[]{:S(2)}) collective-permute-start(bf16[2,640,128]{2,1,0:T(8,128)(2,1)} %slice.421), channel_id=1, source_target_pairs={{0,4},{4,0},{8,12},{12,8},{16,20},{20,16},{24,28},{28,24},{1,5},{5... | collective-permute-start | bytes 983048 | tf_op jit(solution)/shard_map/ppermute | solution.py:26
  247.2 24.4 %collective-permute-start.32 = (bf16[2,640,128]{2,1,0:T(8,128)(2,1)S(1)}, bf16[2,640,128]{2,1,0:T(8,128)(2,1)S(1)}, u32[]{:S(2)}, u32[]{:S(2)}) collective-permute-start(bf16[2,640,128]{2,1,0:T(8,128)(2,1)S(1)} %slice.408), channel_id=1, source_target_pairs={{0,8},{4,12},{8,0},{12,4},{16,24},{20,28},{24,16},{28,20},{1,9},{5... | collective-permute-start | bytes 983048 | tf_op jit(solution)/shard_map/ppermute | solution.py:26
  258.6 22.3 %collective-permute-start.38 = (bf16[1,640,128]{2,1,0:T(8,128)(2,1)S(1)}, bf16[1,640,128]{2,1,0:T(8,128)(2,1)S(1)}, u32[]{:S(2)}, u32[]{:S(2)}) collective-permute-start(bf16[1,640,128]{2,1,0:T(8,128)(2,1)S(1)} %slice.423), channel_id=1, source_target_pairs={{0,16},{4,20},{8,24},{12,28},{16,0},{20,4},{24,8},{28,12},{1,17},{... | collective-permute-start | bytes 491528 | tf_op jit(solution)/shard_map/ppermute | solution.py:26
  265.5 27.5 %collective-permute-start.35 = (bf16[1,1,240,1920]{3,2,1,0:T(8,128)(2,1)S(1)}, bf16[1,1,240,1920]{3,2,1,0:T(8,128)(2,1)S(1)}, u32[]{:S(2)}, u32[]{:S(2)}) collective-permute-start(bf16[1,1,240,1920]{3,2,1,0:T(8,128)(2,1)S(1)} %constant_dynamic-slice_fusion.9), channel_id=1, source_target_pairs={{0,2},{1,3},{2,0},{3,1},{4,6},{5,7},{6,4},{7,5},{8,10},{9,11},{10,... | collective-permute-start | bytes 2764808 | tf_op jit(solution)/shard_map/ppermute | solution.py:26
  281.0 11.9 %collective-permute-start.34 = (bf16[1,640,128]{2,1,0:T(8,128)(2,1)S(1)}, bf16[1,640,128]{2,1,0:T(8,128)(2,1)S(1)}, u32[]{:S(2)}, u32[]{:S(2)}) collective-permute-start(bf16[1,640,128]{2,1,0:T(8,128)(2,1)S(1)} %slice.416), channel_id=1, source_target_pairs={{0,16},{4,20},{8,24},{12,28},{16,0},{20,4},{24,8},{28,12},{1,17},{... | collective-permute-start | bytes 491528 | tf_op jit(solution)/shard_map/ppermute | solution.py:26
  294.1 15.6 %collective-permute-start.39 = (bf16[120,1920]{1,0:T(8,128)(2,1)}, bf16[120,1920]{1,0:T(8,128)(2,1)}, u32[]{:S(2)}, u32[]{:S(2)}) collective-permute-start(bf16[120,1920]{1,0:T(8,128)(2,1)} %dynamic-slice_bitcast_fusion), channel_id=1, source_target_pairs={{0,4},{4,0},{8,12},{12,8},{16,20},{20,16},{24,28},{28,24},{1,5},{5... | collective-permute-start | bytes 1382408 | tf_op jit(solution)/shard_map/ppermute | solution.py:26
  310.8 8.2 %collective-permute-start.40 = (bf16[64,1920]{1,0:T(8,128)(2,1)S(1)}, bf16[64,1920]{1,0:T(8,128)(2,1)S(1)}, u32[]{:S(2)}, u32[]{:S(2)}) collective-permute-start(bf16[64,1920]{1,0:T(8,128)(2,1)S(1)} %constant_dynamic-slice_fusion.8), channel_id=1, source_target_pairs={{0,8},{4,12},{8,0},{12,4},{16,24},{20,28},{24,16},{28,20},{1,9},{5... | collective-permute-start | bytes 737288 | tf_op jit(solution)/shard_map/ppermute | solution.py:26
  312.5 17.6 %collective-permute-start.45 = (bf16[2,1,248,640]{3,2,1,0:T(8,128)(2,1)S(1)}, bf16[2,1,248,640]{3,2,1,0:T(8,128)(2,1)S(1)}, u32[]{:S(2)}, u32[]{:S(2)}) collective-permute-start(bf16[2,1,248,640]{3,2,1,0:T(8,128)(2,1)S(1)} %fusion.47), channel_id=1, source_target_pairs={{0,1},{1,0},{2,3},{3,2},{4,5},{5,4},{6,7},{7,6},{8,9},{9,8},{10,11... | collective-permute-start | bytes 1904648 | tf_op jit(solution)/shard_map/ppermute | solution.py:26
  319.1 10.9 %collective-permute-start.41 = (bf16[32,1920]{1,0:T(8,128)(2,1)S(1)}, bf16[32,1920]{1,0:T(8,128)(2,1)S(1)}, u32[]{:S(2)}, u32[]{:S(2)}) collective-permute-start(bf16[32,1920]{1,0:T(8,128)(2,1)S(1)} %constant_dynamic-slice_fusion.7), channel_id=1, source_target_pairs={{0,16},{4,20},{8,24},{12,28},{16,0},{20,4},{24,8},{28,12},{1,17},{... | collective-permute-start | bytes 368648 | tf_op jit(solution)/shard_map/ppermute | solution.py:26
  330.0 64.3 %collective-permute-start.42 = (bf16[32,1920]{1,0:T(8,128)(2,1)S(1)}, bf16[32,1920]{1,0:T(8,128)(2,1)S(1)}, u32[]{:S(2)}, u32[]{:S(2)}) collective-permute-start(bf16[32,1920]{1,0:T(8,128)(2,1)S(1)} %add_convert_fusion.9), channel_id=1, source_target_pairs={{0,16},{4,20},{8,24},{12,28},{16,0},{20,4},{24,8},{28,12},{1,17},{... | collective-permute-start | bytes 368648 | tf_op jit(solution)/shard_map/ppermute | solution.py:26
  330.3 64.1 %collective-permute-start.46 = (bf16[1,1,248,640]{3,2,1,0:T(8,128)(2,1)S(1)}, bf16[1,1,248,640]{3,2,1,0:T(8,128)(2,1)S(1)}, u32[]{:S(2)}, u32[]{:S(2)}) collective-permute-start(bf16[1,1,248,640]{3,2,1,0:T(8,128)(2,1)S(1)} %constant_dynamic-slice_fusion.6), channel_id=1, source_target_pairs={{0,2},{1,3},{2,0},{3,1},{4,6},{5,7},{6,4},{7,5},{8,10},{9,11},{10,... | collective-permute-start | bytes 952328 | tf_op jit(solution)/shard_map/ppermute | solution.py:26
  392.8 30.2 %collective-permute-start.53 = (bf16[1,2,240,1280]{3,2,1,0:T(8,128)(2,1)S(1)}, bf16[1,2,240,1280]{3,2,1,0:T(8,128)(2,1)S(1)}, u32[]{:S(2)}, u32[]{:S(2)}) collective-permute-start(bf16[1,2,240,1280]{3,2,1,0:T(8,128)(2,1)S(1)} %get-tuple-element.103), channel_id=1, source_target_pairs={{0,2},{1,3},{2,0},{3,1},{4,6},{5,7},{6,4},{7,5},{8,10},{9,11},{10,... | collective-permute-start | bytes 3686408 | tf_op jit(solution)/shard_map/ppermute | solution.py:26
  394.3 7.4 %collective-permute-start.43 = (bf16[64,1920]{1,0:T(8,128)(2,1)S(1)}, bf16[64,1920]{1,0:T(8,128)(2,1)S(1)}, u32[]{:S(2)}, u32[]{:S(2)}) collective-permute-start(bf16[64,1920]{1,0:T(8,128)(2,1)S(1)} %maximum_select_fusion.11), channel_id=1, source_target_pairs={{0,8},{4,12},{8,0},{12,4},{16,24},{20,28},{24,16},{28,20},{1,9},{5... | collective-permute-start | bytes 737288 | tf_op jit(solution)/shard_map/ppermute | solution.py:26
  394.6 7.3 %collective-permute-start.47 = (bf16[128,640]{1,0:T(8,128)(2,1)S(1)}, bf16[128,640]{1,0:T(8,128)(2,1)S(1)}, u32[]{:S(2)}, u32[]{:S(2)}) collective-permute-start(bf16[128,640]{1,0:T(8,128)(2,1)S(1)} %dynamic-slice_bitcast_fusion.1), channel_id=1, source_target_pairs={{0,4},{4,0},{8,12},{12,8},{16,20},{20,16},{24,28},{28,24},{1,5},{5... | collective-permute-start | bytes 491528 | tf_op jit(solution)/shard_map/ppermute | solution.py:26
  408.1 10.0 %collective-permute-start.44 = (bf16[120,1920]{1,0:T(8,128)(2,1)S(1)}, bf16[120,1920]{1,0:T(8,128)(2,1)S(1)}, u32[]{:S(2)}, u32[]{:S(2)}) collective-permute-start(bf16[120,1920]{1,0:T(8,128)(2,1)S(1)} %pad_maximum_fusion.10), channel_id=1, source_target_pairs={{0,4},{4,0},{8,12},{12,8},{16,20},{20,16},{24,28},{28,24},{1,5},{5... | collective-permute-start | bytes 1382408 | tf_op jit(solution)/shard_map/ppermute | solution.py:26
  (103 other events, 957.4 us)
Sparse Core Ops, SparseCore 0:
  227.3 163.6 all-reduce.4

commit v3 on v2

--- a/solution.py
+++ b/solution.py
@@ -512,7 +512,7 @@
     g_out = mm(jnp.concatenate(o_b, axis=1), dx1_cat, 1, 0)
     g_query = mm(h1_cat, jnp.concatenate(dq_b, axis=1), 0, 1)
     g_oq = jnp.concatenate([g_out, g_query], axis=1).astype(BF).reshape(n_wa, shard, -1)
-    oq = Chain(all_reduce_rows(g_oq, n_wa, n_ctx, low_first))
+    oq = Chain(all_reduce_rows(g_oq, n_wa, n_ctx, low_first[1:] + low_first[:1]))
     dkv[0].pending = oq.issue(dkv[0].pending)
     for chain in dkv:
         chain.issue()

time: 449 us -> 458 us (1.020)
  waiting for transfers between devices: 214 us -> 219 us
    ppermute x55, waiting for transfers between devices: 153 us -> 162 us  [swap(): return lax.ppermute(a, axis, [(i, i ^ 1 << bit) for i in range(n)])]
  transfers between devices with their start and end apart: 56 -> 56, of which waited for: 27 -> 26; matrix products, arithmetic and copies ran while one was open for 25% -> 24% of each run, Pallas kernels for 6% -> 6%
where the time goes in v3:
time: 458 us; the launch traced here: 452 us
  waiting for transfers between devices  219 us (48%)
  other arithmetic  59.3 us (13%)
  starting transfers between devices  49.9 us (11%)
  local copies, waits for them, and re-layouts  45.4 us (10%)
  matrix products  33.8 us (7%)
  Pallas kernels  28.1 us (6%)
  between operations  16.5 us (4%)
    ppermute x55, waiting for transfers between devices, swap(): return lax.ppermute(a, axis, [(i, i ^ 1 << bit) for i in range(n)])  162 us
    psum x1, waiting for transfers between devices, local(): g_gu_sum = lax.psum(g_gu, 'ctx')  56.8 us
    ppermute x55, starting transfers between devices, swap(): return lax.ppermute(a, axis, [(i, i ^ 1 << bit) for i in range(n)])  49.9 us
    dot_general x25, matrix products, mm(): lax.dot_general(a, b, (((ca,), (cb,)), ((), ())), preferred_element_type=...  33.8 us
    unnamed x206, local copies, waits for them, and re-layouts  18.2 us
    pallas_call x2, Pallas kernels, attend_back(): pl.pallas_call(functools.partial(attend_back_kernel, groups, per_group, m...  15.9 us
    select_n x14, other arithmetic, ordered(): jnp.where(bit == 0, jnp.concatenate([mine, theirs], axis=dim), jnp.concat...  13.9 us
    pallas_call x2, Pallas kernels, attend(): pl.pallas_call(functools.partial(attend_kernel, groups, per_group, min(sl...  12.2 us
  transfers between devices with their start and end apart: 56, of which 26 were waited for; matrix products, arithmetic and copies ran while one was open for 24% of the time, Pallas kernels for 6%

profile of v3, /device:TPU:0, one launch (start us, length us, event | category | flops | bytes accessed | tf_op | source)
XLA Modules:
  0.0 451.9 jit_solution(1346586099651760128)
XLA Ops:
  11.0 3.0 collective-permute-start
  19.2 2.3 maximum_bitcast_fusion.2
  25.0 3.2 pad_maximum_fusion
  28.3 8.8 %collective-permute-done.1 = bf16[1,1,240,960]{3,2,1,0:T(8,128)(2,1)} collective-permute-done((bf16[1,1,240,960]{3,2,1,0:T(8,128)(2,1)}, bf16[1,1,240,960]{3,2,1,0:T(8,128)(2,1)}, u32[]{:S(2)}, u32[]{:S(2)}) %collective-permute-start.1) | collective-permute-done | bytes 460832 | tf_op jit(solution)/shard_map/ppermute | solution.py:26
  42.8 2.6 collective-permute-start.4
  48.4 9.1 %collective-permute-done.4 = bf16[1,640,128]{2,1,0:T(8,128)(2,1)S(1)} collective-permute-done((bf16[1,640,128]{2,1,0:T(8,128)(2,1)S(1)}, bf16[1,640,128]{2,1,0:T(8,128)(2,1)S(1)}, u32[]{:S(2)}, u32[]{:S(2)}) %collective-permute-start.4) | collective-permute-done | bytes 163872 | tf_op jit(solution)/shard_map/ppermute | solution.py:26
  57.6 2.3 collective-permute-done.8
  61.5 2.3 maximum_select_fusion.8
  71.6 2.8 copy.41
  74.4 2.5 fusion.103
  79.4 6.3 %collective-permute-done.18 = bf16[4,640,128]{2,1,0:T(8,128)(2,1)} collective-permute-done((bf16[4,640,128]{2,1,0:T(8,128)(2,1)}, bf16[4,640,128]{2,1,0:T(8,128)(2,1)}, u32[]{:S(2)}, u32[]{:S(2)}) %collective-permute-start.18) | collective-permute-done | bytes 655392 | tf_op jit(solution)/shard_map/ppermute | solution.py:26
  85.7 2.3 pad_maximum_fusion.3.kv_ref
  88.0 6.1 %shard_map.213 = (f32[960,128]{1,0:T(8,128)}, f32[15,128]{1,0:T(8,128)}) custom-call(bf16[960,128]{1,0:T(8,128)(2,1)} %bitcast.281, bf16[8,640,128]{2,1,0:T(8,128)(2,1)} %pad_maximum_fusion.3.kv_ref, f32[1024,128]{1,0:T(8,128)} %get-tuple-element.162.bias_ref), custom_call_target="tpu_custom_call" | custom-call | flops 1006632960 | bytes 2572288 | tf_op jit(solution)/shard_map/pallas_call | solution.py:308
  95.2 2.3 pad_maximum_fusion.2.kv_ref
  97.5 6.0 %shard_map.212 = (f32[960,128]{1,0:T(8,128)}, f32[15,128]{1,0:T(8,128)}) custom-call(bf16[960,128]{1,0:T(8,128)(2,1)} %bitcast.283, bf16[8,640,128]{2,1,0:T(8,128)(2,1)} %pad_maximum_fusion.2.kv_ref, f32[1024,128]{1,0:T(8,128)} %get-tuple-element.161.bias_ref), custom_call_target="tpu_custom_call" | custom-call | flops 1006632960 | bytes 2572288 | tf_op jit(solution)/shard_map/pallas_call | solution.py:308
  104.6 2.5 maximum_select_fusion.5
  110.6 6.2 %collective-permute-done.10 = bf16[128,960]{0,1:T(8,128)(2,1)S(1)} collective-permute-done((bf16[128,960]{0,1:T(8,128)(2,1)S(1)}, bf16[128,960]{0,1:T(8,128)(2,1)S(1)}, u32[]{:S(2)}, u32[]{:S(2)}) %collective-permute-start.10) | collective-permute-done | bytes 245792 | tf_op jit(solution)/shard_map/ppermute | solution.py:26
  118.2 2.4 maximum_select_fusion
  124.9 11.3 %collective-permute-done.19 = bf16[128,960]{0,1:T(8,128)(2,1)} collective-permute-done((bf16[128,960]{0,1:T(8,128)(2,1)}, bf16[128,960]{0,1:T(8,128)(2,1)}, u32[]{:S(2)}, u32[]{:S(2)}) %collective-permute-start.19) | collective-permute-done | bytes 245792 | tf_op jit(solution)/shard_map/ppermute | solution.py:26
  145.7 2.1 maximum_select_fusion.1
  147.8 2.6 fusion.37
  163.7 2.7 fusion.13
  170.5 5.0 %collective-permute-done.28 = bf16[128,960]{0,1:T(8,128)(2,1)S(1)} collective-permute-done((bf16[128,960]{0,1:T(8,128)(2,1)S(1)}, bf16[128,960]{0,1:T(8,128)(2,1)S(1)}, u32[]{:S(2)}, u32[]{:S(2)}) %collective-permute-start.28) | collective-permute-done | bytes 245792 | tf_op jit(solution)/shard_map/ppermute | solution.py:26
  175.6 5.2 %collective-permute-done.31 = bf16[128,960]{0,1:T(8,128)(2,1)S(1)} collective-permute-done((bf16[128,960]{0,1:T(8,128)(2,1)S(1)}, bf16[128,960]{0,1:T(8,128)(2,1)S(1)}, u32[]{:S(2)}, u32[]{:S(2)}) %collective-permute-start.31) | collective-permute-done | bytes 245792 | tf_op jit(solution)/shard_map/ppermute | solution.py:26
  181.4 3.8 collective-permute-done.23
  185.2 2.3 fusion.146
  190.3 7.8 %shard_map.214 = (f32[960,128]{1,0:T(8,128)}, bf16[8,640,128]{2,1,0:T(8,128)(2,1)}) custom-call(bf16[960,128]{1,0:T(8,128)(2,1)} %bitcast.284, bf16[8,640,128]{2,1,0:T(8,128)(2,1)} %pad_maximum_fusion.2.kv_ref, f32[1024,128]{1,0:T(8,128)} %get-tuple-element.161.bias_ref, f32[15,128]{1,0:T(8,128)} %get-tuple-element.49.lse_ref, ...), custom_call_target="tpu_custom_call" | custom-call | flops 2516582400 | bytes 4620288 | tf_op jit(solution)/shard_map/pallas_call | solution.py:327
  200.1 8.1 %shard_map.215 = (f32[960,128]{1,0:T(8,128)}, bf16[8,640,128]{2,1,0:T(8,128)(2,1)}) custom-call(bf16[960,128]{1,0:T(8,128)(2,1)} %bitcast.282, bf16[8,640,128]{2,1,0:T(8,128)(2,1)} %pad_maximum_fusion.3.kv_ref, f32[1024,128]{1,0:T(8,128)} %get-tuple-element.162.bias_ref, f32[15,128]{1,0:T(8,128)} %get-tuple-element.52.lse_ref, ...), custom_call_target="tpu_custom_call" | custom-call | flops 2516582400 | bytes 4620288 | tf_op jit(solution)/shard_map/pallas_call | solution.py:327
  208.2 2.1 slice.340
  218.0 4.1 convolution_convert_fusion
  230.4 15.2 %collective-permute-done.29 = bf16[4,640,128]{2,1,0:T(8,128)(2,1)} collective-permute-done((bf16[4,640,128]{2,1,0:T(8,128)(2,1)}, bf16[4,640,128]{2,1,0:T(8,128)(2,1)}, u32[]{:S(2)}, u32[]{:S(2)}) %collective-permute-start.29) | collective-permute-done | bytes 655392 | tf_op jit(solution)/shard_map/ppermute | solution.py:26
  247.3 10.2 %collective-permute-done.37 = bf16[2,640,128]{2,1,0:T(8,128)(2,1)} collective-permute-done((bf16[2,640,128]{2,1,0:T(8,128)(2,1)}, bf16[2,640,128]{2,1,0:T(8,128)(2,1)}, u32[]{:S(2)}, u32[]{:S(2)}) %collective-permute-start.37) | collective-permute-done | bytes 327712 | tf_op jit(solution)/shard_map/ppermute | solution.py:26
  258.5 4.4 collective-permute-start.38
  263.0 2.4 add_convert_fusion
  265.5 6.1 %collective-permute-done.32 = bf16[2,640,128]{2,1,0:T(8,128)(2,1)S(1)} collective-permute-done((bf16[2,640,128]{2,1,0:T(8,128)(2,1)S(1)}, bf16[2,640,128]{2,1,0:T(8,128)(2,1)S(1)}, u32[]{:S(2)}, u32[]{:S(2)}) %collective-permute-start.32) | collective-permute-done | bytes 327712 | tf_op jit(solution)/shard_map/ppermute | solution.py:26
  271.7 9.1 %collective-permute-done.38 = bf16[1,640,128]{2,1,0:T(8,128)(2,1)S(1)} collective-permute-done((bf16[1,640,128]{2,1,0:T(8,128)(2,1)S(1)}, bf16[1,640,128]{2,1,0:T(8,128)(2,1)S(1)}, u32[]{:S(2)}, u32[]{:S(2)}) %collective-permute-start.38) | collective-permute-done | bytes 163872 | tf_op jit(solution)/shard_map/ppermute | solution.py:26
  281.0 12.0 %collective-permute-done.34 = bf16[1,640,128]{2,1,0:T(8,128)(2,1)S(1)} collective-permute-done((bf16[1,640,128]{2,1,0:T(8,128)(2,1)S(1)}, bf16[1,640,128]{2,1,0:T(8,128)(2,1)S(1)}, u32[]{:S(2)}, u32[]{:S(2)}) %collective-permute-start.34) | collective-permute-done | bytes 163872 | tf_op jit(solution)/shard_map/ppermute | solution.py:26
  299.5 16.1 %collective-permute-done.39 = bf16[120,1920]{1,0:T(8,128)(2,1)} collective-permute-done((bf16[120,1920]{1,0:T(8,128)(2,1)}, bf16[120,1920]{1,0:T(8,128)(2,1)}, u32[]{:S(2)}, u32[]{:S(2)}) %collective-permute-start.39) | collective-permute-done | bytes 460832 | tf_op jit(solution)/shard_map/ppermute | solution.py:26
  318.6 6.3 %collective-permute-done.40 = bf16[64,1920]{1,0:T(8,128)(2,1)S(1)} collective-permute-done((bf16[64,1920]{1,0:T(8,128)(2,1)S(1)}, bf16[64,1920]{1,0:T(8,128)(2,1)S(1)}, u32[]{:S(2)}, u32[]{:S(2)}) %collective-permute-start.40) | collective-permute-done | bytes 245792 | tf_op jit(solution)/shard_map/ppermute | solution.py:26
  327.6 5.3 %collective-permute-done.41 = bf16[32,1920]{1,0:T(8,128)(2,1)S(1)} collective-permute-done((bf16[32,1920]{1,0:T(8,128)(2,1)S(1)}, bf16[32,1920]{1,0:T(8,128)(2,1)S(1)}, u32[]{:S(2)}, u32[]{:S(2)}) %collective-permute-start.41) | collective-permute-done | bytes 122912 | tf_op jit(solution)/shard_map/ppermute | solution.py:26
  334.6 56.8 %all-reduce.5.cloned.1.call-done = (bf16[2,2,240,1280]{3,2,1,0:T(8,128)(2,1)}, bf16[640,960]{0,1:T(8,128)(2,1)}) async-done(((bf16[2,2,240,1280]{3,2,1,0:T(8,128)(2,1)}, bf16[640,960]{0,1:T(8,128)(2,1)}), (bf16[2,2,240,1280]{3,2,1,0:T(8,128)(2,1)}, bf16[640,960]{0,1:T(8,128)(2,1)})) %all-reduce.5.cloned.1.call-update) | async-done | bytes 3686416 | tf_op jit(solution)/shard_map/psum | solution.py:489
  398.0 9.7 %collective-permute-done.43 = bf16[64,1920]{1,0:T(8,128)(2,1)S(1)} collective-permute-done((bf16[64,1920]{1,0:T(8,128)(2,1)S(1)}, bf16[64,1920]{1,0:T(8,128)(2,1)S(1)}, u32[]{:S(2)}, u32[]{:S(2)}) %collective-permute-start.43) | collective-permute-done | bytes 245792 | tf_op jit(solution)/shard_map/ppermute | solution.py:26
  407.9 4.4 collective-permute-done.48
  413.3 2.1 collective-permute-start.44
  415.4 2.3 collective-permute-done.49
  421.1 3.7 collective-permute-done.50
  424.8 3.4 collective-permute-start.51
  428.3 2.3 collective-permute-done.51
  (460 shorter events, 133.4 us)
Async XLA Ops:
  7.2 384.2 %all-reduce.5.cloned.1.call-start = ((), (), s32[]{:S(2)}) async-start(), calls=%async_computation | async-start | bytes 7372800 | tf_op jit(solution)/shard_map/psum | solution.py:489
  11.0 10.6 %collective-permute-start = (bf16[1,1,248,640]{3,2,1,0:T(8,128)(2,1)S(1)}, bf16[1,1,248,640]{3,2,1,0:T(8,128)(2,1)}, u32[]{:S(2)}, u32[]{:S(2)}) collective-permute-start(bf16[1,1,248,640]{3,2,1,0:T(8,128)(2,1)S(1)} %maximum_bitcast_fusion.4), channel_id=1, source_target_pairs={{0,2},{1,3},{2,0},{3,1},{4,6},{5,7},{6,4},{7,5},{8,10},{9,11},{10,... | collective-permute-start | bytes 952328 | tf_op jit(solution)/shard_map/ppermute | solution.py:26
  22.9 16.0 %collective-permute-start.2 = (bf16[2,1,248,640]{3,2,1,0:T(8,128)(2,1)S(1)}, bf16[2,1,248,640]{3,2,1,0:T(8,128)(2,1)}, u32[]{:S(2)}, u32[]{:S(2)}) collective-permute-start(bf16[2,1,248,640]{3,2,1,0:T(8,128)(2,1)S(1)} %maximum_select_fusion.10), channel_id=1, source_target_pairs={{0,1},{1,0},{2,3},{3,2},{4,5},{5,4},{6,7},{7,6},{8,9},{9,8},{10,11... | collective-permute-start | bytes 1904648 | tf_op jit(solution)/shard_map/ppermute | solution.py:26
  23.1 14.0 %collective-permute-start.1 = (bf16[1,1,240,960]{3,2,1,0:T(8,128)(2,1)}, bf16[1,1,240,960]{3,2,1,0:T(8,128)(2,1)}, u32[]{:S(2)}, u32[]{:S(2)}) collective-permute-start(bf16[1,1,240,960]{3,2,1,0:T(8,128)(2,1)} %bitcast.2), channel_id=1, source_target_pairs={{0,2},{1,3},{2,0},{3,1},{4,6},{5,7},{6,4},{7,5},{8,10},{9,11},{10,... | collective-permute-start | bytes 1382408 | tf_op jit(solution)/shard_map/ppermute | solution.py:26
  37.1 24.4 %collective-permute-start.7 = (bf16[1,1,240,960]{3,2,1,0:T(8,128)(2,1)S(1)}, bf16[1,1,240,960]{3,2,1,0:T(8,128)(2,1)}, u32[]{:S(2)}, u32[]{:S(2)}) collective-permute-start(bf16[1,1,240,960]{3,2,1,0:T(8,128)(2,1)S(1)} %bitcast.269), channel_id=1, source_target_pairs={{0,2},{1,3},{2,0},{3,1},{4,6},{5,7},{6,4},{7,5},{8,10},{9,11},{10,... | collective-permute-start | bytes 1382408 | tf_op jit(solution)/shard_map/ppermute | solution.py:26
  42.8 14.7 %collective-permute-start.4 = (bf16[1,640,128]{2,1,0:T(8,128)(2,1)S(1)}, bf16[1,640,128]{2,1,0:T(8,128)(2,1)S(1)}, u32[]{:S(2)}, u32[]{:S(2)}) collective-permute-start(bf16[1,640,128]{2,1,0:T(8,128)(2,1)S(1)} %maximum_bitcast_fusion.5), channel_id=1, source_target_pairs={{0,16},{4,20},{8,24},{12,28},{16,0},{20,4},{24,8},{28,12},{1,17},{... | collective-permute-start | bytes 491528 | tf_op jit(solution)/shard_map/ppermute | solution.py:26
  45.5 14.5 %collective-permute-start.8 = (bf16[1,640,128]{2,1,0:T(8,128)(2,1)S(1)}, bf16[1,640,128]{2,1,0:T(8,128)(2,1)S(1)}, u32[]{:S(2)}, u32[]{:S(2)}) collective-permute-start(bf16[1,640,128]{2,1,0:T(8,128)(2,1)S(1)} %maximum_bitcast_fusion.6), channel_id=1, source_target_pairs={{0,16},{4,20},{8,24},{12,28},{16,0},{20,4},{24,8},{28,12},{1,17},{... | collective-permute-start | bytes 491528 | tf_op jit(solution)/shard_map/ppermute | solution.py:26
  48.4 22.8 %collective-permute-start.3 = (bf16[2,1,240,960]{3,2,1,0:T(8,128)(2,1)S(1)}, bf16[2,1,240,960]{3,2,1,0:T(8,128)(2,1)S(1)}, u32[]{:S(2)}, u32[]{:S(2)}) collective-permute-start(bf16[2,1,240,960]{3,2,1,0:T(8,128)(2,1)S(1)} %maximum_select_fusion.7), channel_id=1, source_target_pairs={{0,1},{1,0},{2,3},{3,2},{4,5},{5,4},{6,7},{7,6},{8,9},{9,8},{10,11... | collective-permute-start | bytes 2764808 | tf_op jit(solution)/shard_map/ppermute | solution.py:26
  57.5 9.3 %collective-permute-start.5 = (bf16[2,640,128]{2,1,0:T(8,128)(2,1)S(1)}, bf16[2,640,128]{2,1,0:T(8,128)(2,1)S(1)}, u32[]{:S(2)}, u32[]{:S(2)}) collective-permute-start(bf16[2,640,128]{2,1,0:T(8,128)(2,1)S(1)} %pad_maximum_fusion.11), channel_id=1, source_target_pairs={{0,8},{4,12},{8,0},{12,4},{16,24},{20,28},{24,16},{28,20},{1,9},{5... | collective-permute-start | bytes 983048 | tf_op jit(solution)/shard_map/ppermute | solution.py:26
  60.0 9.3 %collective-permute-start.14 = (bf16[2,640,128]{2,1,0:T(8,128)(2,1)S(1)}, bf16[2,640,128]{2,1,0:T(8,128)(2,1)S(1)}, u32[]{:S(2)}, u32[]{:S(2)}) collective-permute-start(bf16[2,640,128]{2,1,0:T(8,128)(2,1)S(1)} %pad_maximum_fusion.12), channel_id=1, source_target_pairs={{0,4},{4,0},{8,12},{12,8},{16,20},{20,16},{24,28},{28,24},{1,5},{5... | collective-permute-start | bytes 983048 | tf_op jit(solution)/shard_map/ppermute | solution.py:26
  63.9 40.7 %collective-permute-start.9 = (bf16[2,1,240,960]{3,2,1,0:T(8,128)(2,1)}, bf16[2,1,240,960]{3,2,1,0:T(8,128)(2,1)}, u32[]{:S(2)}, u32[]{:S(2)}) collective-permute-start(bf16[2,1,240,960]{3,2,1,0:T(8,128)(2,1)} %maximum_select_fusion.8), channel_id=1, source_target_pairs={{0,1},{1,0},{2,3},{3,2},{4,5},{5,4},{6,7},{7,6},{8,9},{9,8},{10,11... | collective-permute-start | bytes 2764808 | tf_op jit(solution)/shard_map/ppermute | solution.py:26
  65.5 51.5 %collective-permute-start.13 = (bf16[1,2,240,1280]{3,2,1,0:T(8,128)(2,1)}, bf16[1,2,240,1280]{3,2,1,0:T(8,128)(2,1)}, u32[]{:S(2)}, u32[]{:S(2)}) collective-permute-start(bf16[1,2,240,1280]{3,2,1,0:T(8,128)(2,1)} %get-tuple-element.107), channel_id=1, source_target_pairs={{0,2},{1,3},{2,0},{3,1},{4,6},{5,7},{6,4},{7,5},{8,10},{9,11},{10,... | collective-permute-start | bytes 3686408 | tf_op jit(solution)/shard_map/ppermute | solution.py:26
  67.8 27.4 %collective-permute-start.6 = (bf16[4,640,128]{2,1,0:T(8,128)(2,1)}, bf16[4,640,128]{2,1,0:T(8,128)(2,1)}, u32[]{:S(2)}, u32[]{:S(2)}) collective-permute-start(bf16[4,640,128]{2,1,0:T(8,128)(2,1)} %pad_maximum_fusion.4), channel_id=1, source_target_pairs={{0,4},{4,0},{8,12},{12,8},{16,20},{20,16},{24,28},{28,24},{1,5},{5... | collective-permute-start | bytes 1966088 | tf_op jit(solution)/shard_map/ppermute | solution.py:26
  70.3 15.4 %collective-permute-start.18 = (bf16[4,640,128]{2,1,0:T(8,128)(2,1)}, bf16[4,640,128]{2,1,0:T(8,128)(2,1)}, u32[]{:S(2)}, u32[]{:S(2)}) collective-permute-start(bf16[4,640,128]{2,1,0:T(8,128)(2,1)} %pad_maximum_fusion.5), channel_id=1, source_target_pairs={{0,8},{4,12},{8,0},{12,4},{16,24},{20,28},{24,16},{28,20},{1,9},{5... | collective-permute-start | bytes 1966088 | tf_op jit(solution)/shard_map/ppermute | solution.py:26
  108.3 8.5 %collective-permute-start.11 = (bf16[128,960]{0,1:T(8,128)(2,1)S(1)}, bf16[128,960]{0,1:T(8,128)(2,1)S(1)}, u32[]{:S(2)}, u32[]{:S(2)}) collective-permute-start(bf16[128,960]{0,1:T(8,128)(2,1)S(1)} %get-tuple-element.89), channel_id=1, source_target_pairs={{0,1},{1,0},{2,3},{3,2},{4,5},{5,4},{6,7},{7,6},{8,9},{9,8},{10,11... | collective-permute-start | bytes 737288 | tf_op jit(solution)/shard_map/ppermute | solution.py:26
  108.4 8.4 %collective-permute-start.10 = (bf16[128,960]{0,1:T(8,128)(2,1)S(1)}, bf16[128,960]{0,1:T(8,128)(2,1)S(1)}, u32[]{:S(2)}, u32[]{:S(2)}) collective-permute-start(bf16[128,960]{0,1:T(8,128)(2,1)S(1)} %get-tuple-element.89), channel_id=1, source_target_pairs={{0,2},{1,3},{2,0},{3,1},{4,6},{5,7},{6,4},{7,5},{8,10},{9,11},{10,... | collective-permute-start | bytes 737288 | tf_op jit(solution)/shard_map/ppermute | solution.py:26
  117.0 19.3 %collective-permute-start.24 = (bf16[1,2,128,960]{2,3,1,0:T(8,128)(2,1)}, bf16[1,2,128,960]{2,3,1,0:T(8,128)(2,1)}, u32[]{:S(2)}, u32[]{:S(2)}) collective-permute-start(bf16[1,2,128,960]{2,3,1,0:T(8,128)(2,1)} %bitcast.35), channel_id=1, source_target_pairs={{0,2},{1,3},{2,0},{3,1},{4,6},{5,7},{6,4},{7,5},{8,10},{9,11},{10,... | collective-permute-start | bytes 1474568 | tf_op jit(solution)/shard_map/ppermute | solution.py:26
  121.8 14.5 %collective-permute-start.19 = (bf16[128,960]{0,1:T(8,128)(2,1)}, bf16[128,960]{0,1:T(8,128)(2,1)}, u32[]{:S(2)}, u32[]{:S(2)}) collective-permute-start(bf16[128,960]{0,1:T(8,128)(2,1)} %get-tuple-element.87), channel_id=1, source_target_pairs={{0,2},{1,3},{2,0},{3,1},{4,6},{5,7},{6,4},{7,5},{8,10},{9,11},{10,... | collective-permute-start | bytes 737288 | tf_op jit(solution)/shard_map/ppermute | solution.py:26
  124.3 21.1 %collective-permute-start.15 = (bf16[2,1,240,1280]{3,2,1,0:T(8,128)(2,1)}, bf16[2,1,240,1280]{3,2,1,0:T(8,128)(2,1)}, u32[]{:S(2)}, u32[]{:S(2)}) collective-permute-start(bf16[2,1,240,1280]{3,2,1,0:T(8,128)(2,1)} %get-tuple-element.105), channel_id=1, source_target_pairs={{0,1},{1,0},{2,3},{3,2},{4,5},{5,4},{6,7},{7,6},{8,9},{9,8},{10,11... | collective-permute-start | bytes 3686408 | tf_op jit(solution)/shard_map/ppermute | solution.py:26
  124.4 17.6 %collective-permute-start.25 = (bf16[1,2,128,960]{2,3,1,0:T(8,128)(2,1)}, bf16[1,2,128,960]{2,3,1,0:T(8,128)(2,1)S(1)}, u32[]{:S(2)}, u32[]{:S(2)}) collective-permute-start(bf16[1,2,128,960]{2,3,1,0:T(8,128)(2,1)} %bitcast.35), channel_id=1, source_target_pairs={{0,1},{1,0},{2,3},{3,2},{4,5},{5,4},{6,7},{7,6},{8,9},{9,8},{10,11... | collective-permute-start | bytes 1474568 | tf_op jit(solution)/shard_map/ppermute | solution.py:26
  124.8 15.7 %collective-permute-start.20 = (bf16[128,960]{0,1:T(8,128)(2,1)}, bf16[128,960]{0,1:T(8,128)(2,1)S(1)}, u32[]{:S(2)}, u32[]{:S(2)}) collective-permute-start(bf16[128,960]{0,1:T(8,128)(2,1)} %get-tuple-element.87), channel_id=1, source_target_pairs={{0,1},{1,0},{2,3},{3,2},{4,5},{5,4},{6,7},{7,6},{8,9},{9,8},{10,11... | collective-permute-start | bytes 737288 | tf_op jit(solution)/shard_map/ppermute | solution.py:26
  158.2 8.2 %collective-permute-start.27 = (bf16[256,960]{0,1:T(8,128)(2,1)S(1)}, bf16[256,960]{0,1:T(8,128)(2,1)S(1)}, u32[]{:S(2)}, u32[]{:S(2)}) collective-permute-start(bf16[256,960]{0,1:T(8,128)(2,1)S(1)} %slice.573), channel_id=1, source_target_pairs={{0,1},{1,0},{2,3},{3,2},{4,5},{5,4},{6,7},{7,6},{8,9},{9,8},{10,11... | collective-permute-start | bytes 1474568 | tf_op jit(solution)/shard_map/ppermute | solution.py:26
  158.3 9.6 %collective-permute-start.30 = (bf16[256,960]{0,1:T(8,128)(2,1)S(1)}, bf16[256,960]{0,1:T(8,128)(2,1)S(1)}, u32[]{:S(2)}, u32[]{:S(2)}) collective-permute-start(bf16[256,960]{0,1:T(8,128)(2,1)S(1)} %slice.572), channel_id=1, source_target_pairs={{0,1},{1,0},{2,3},{3,2},{4,5},{5,4},{6,7},{7,6},{8,9},{9,8},{10,11... | collective-permute-start | bytes 1474568 | tf_op jit(solution)/shard_map/ppermute | solution.py:26
  160.0 9.0 %collective-permute-start.22 = (bf16[256,960]{0,1:T(8,128)(2,1)S(1)}, bf16[256,960]{0,1:T(8,128)(2,1)S(1)}, u32[]{:S(2)}, u32[]{:S(2)}) collective-permute-start(bf16[256,960]{0,1:T(8,128)(2,1)S(1)} %slice.574), channel_id=1, source_target_pairs={{0,1},{1,0},{2,3},{3,2},{4,5},{5,4},{6,7},{7,6},{8,9},{9,8},{10,11... | collective-permute-start | bytes 1474568 | tf_op jit(solution)/shard_map/ppermute | solution.py:26
  163.3 60.5 %collective-permute-start.16 = (bf16[256,960]{0,1:T(8,128)(2,1)}, bf16[256,960]{0,1:T(8,128)(2,1)}, u32[]{:S(2)}, u32[]{:S(2)}) collective-permute-start(bf16[256,960]{0,1:T(8,128)(2,1)} %slice.575), channel_id=1, source_target_pairs={{0,1},{1,0},{2,3},{3,2},{4,5},{5,4},{6,7},{7,6},{8,9},{9,8},{10,11... | collective-permute-start | bytes 1474568 | tf_op jit(solution)/shard_map/ppermute | solution.py:26
  166.6 8.9 %collective-permute-start.28 = (bf16[128,960]{0,1:T(8,128)(2,1)S(1)}, bf16[128,960]{0,1:T(8,128)(2,1)S(1)}, u32[]{:S(2)}, u32[]{:S(2)}) collective-permute-start(bf16[128,960]{0,1:T(8,128)(2,1)S(1)} %slice.577), channel_id=1, source_target_pairs={{0,2},{1,3},{2,0},{3,1},{4,6},{5,7},{6,4},{7,5},{8,10},{9,11},{10,... | collective-permute-start | bytes 737288 | tf_op jit(solution)/shard_map/ppermute | solution.py:26
  168.1 12.7 %collective-permute-start.31 = (bf16[128,960]{0,1:T(8,128)(2,1)S(1)}, bf16[128,960]{0,1:T(8,128)(2,1)S(1)}, u32[]{:S(2)}, u32[]{:S(2)}) collective-permute-start(bf16[128,960]{0,1:T(8,128)(2,1)S(1)} %slice.576), channel_id=1, source_target_pairs={{0,2},{1,3},{2,0},{3,1},{4,6},{5,7},{6,4},{7,5},{8,10},{9,11},{10,... | collective-permute-start | bytes 737288 | tf_op jit(solution)/shard_map/ppermute | solution.py:26
  169.2 16.0 %collective-permute-start.23 = (bf16[128,960]{0,1:T(8,128)(2,1)S(1)}, bf16[128,960]{0,1:T(8,128)(2,1)S(1)}, u32[]{:S(2)}, u32[]{:S(2)}) collective-permute-start(bf16[128,960]{0,1:T(8,128)(2,1)S(1)} %slice.578), channel_id=1, source_target_pairs={{0,2},{1,3},{2,0},{3,1},{4,6},{5,7},{6,4},{7,5},{8,10},{9,11},{10,... | collective-permute-start | bytes 737288 | tf_op jit(solution)/shard_map/ppermute | solution.py:26
  210.3 16.9 %collective-permute-start.36 = (bf16[4,640,128]{2,1,0:T(8,128)(2,1)}, bf16[4,640,128]{2,1,0:T(8,128)(2,1)}, u32[]{:S(2)}, u32[]{:S(2)}) collective-permute-start(bf16[4,640,128]{2,1,0:T(8,128)(2,1)} %slice.340), channel_id=1, source_target_pairs={{0,8},{4,12},{8,0},{12,4},{16,24},{20,28},{24,16},{28,20},{1,9},{5... | collective-permute-start | bytes 1966088 | tf_op jit(solution)/shard_map/ppermute | solution.py:26
  216.3 46.7 %collective-permute-start.33 = (bf16[2,1,240,1920]{3,2,1,0:T(8,128)(2,1)}, bf16[2,1,240,1920]{3,2,1,0:T(8,128)(2,1)}, u32[]{:S(2)}, u32[]{:S(2)}) collective-permute-start(bf16[2,1,240,1920]{3,2,1,0:T(8,128)(2,1)} %fusion.12), channel_id=1, source_target_pairs={{0,1},{1,0},{2,3},{3,2},{4,5},{5,4},{6,7},{7,6},{8,9},{9,8},{10,11... | collective-permute-start | bytes 5529608 | tf_op jit(solution)/shard_map/ppermute | solution.py:26
  222.1 23.5 %collective-permute-start.29 = (bf16[4,640,128]{2,1,0:T(8,128)(2,1)}, bf16[4,640,128]{2,1,0:T(8,128)(2,1)}, u32[]{:S(2)}, u32[]{:S(2)}) collective-permute-start(bf16[4,640,128]{2,1,0:T(8,128)(2,1)} %slice.332), channel_id=1, source_target_pairs={{0,4},{4,0},{8,12},{12,8},{16,20},{20,16},{24,28},{28,24},{1,5},{5... | collective-permute-start | bytes 1966088 | tf_op jit(solution)/shard_map/ppermute | solution.py:26
  226.6 90.3 %collective-permute-start.17 = (bf16[128,960]{0,1:T(8,128)(2,1)}, bf16[128,960]{0,1:T(8,128)(2,1)}, u32[]{:S(2)}, u32[]{:S(2)}) collective-permute-start(bf16[128,960]{0,1:T(8,128)(2,1)} %slice.579), channel_id=1, source_target_pairs={{0,2},{1,3},{2,0},{3,1},{4,6},{5,7},{6,4},{7,5},{8,10},{9,11},{10,... | collective-permute-start | bytes 737288 | tf_op jit(solution)/shard_map/ppermute | solution.py:26
  229.4 28.0 %collective-permute-start.37 = (bf16[2,640,128]{2,1,0:T(8,128)(2,1)}, bf16[2,640,128]{2,1,0:T(8,128)(2,1)}, u32[]{:S(2)}, u32[]{:S(2)}) collective-permute-start(bf16[2,640,128]{2,1,0:T(8,128)(2,1)} %slice.421), channel_id=1, source_target_pairs={{0,4},{4,0},{8,12},{12,8},{16,20},{20,16},{24,28},{28,24},{1,5},{5... | collective-permute-start | bytes 983048 | tf_op jit(solution)/shard_map/ppermute | solution.py:26
  247.2 24.4 %collective-permute-start.32 = (bf16[2,640,128]{2,1,0:T(8,128)(2,1)S(1)}, bf16[2,640,128]{2,1,0:T(8,128)(2,1)S(1)}, u32[]{:S(2)}, u32[]{:S(2)}) collective-permute-start(bf16[2,640,128]{2,1,0:T(8,128)(2,1)S(1)} %slice.408), channel_id=1, source_target_pairs={{0,8},{4,12},{8,0},{12,4},{16,24},{20,28},{24,16},{28,20},{1,9},{5... | collective-permute-start | bytes 983048 | tf_op jit(solution)/shard_map/ppermute | solution.py:26
  258.5 22.3 %collective-permute-start.38 = (bf16[1,640,128]{2,1,0:T(8,128)(2,1)S(1)}, bf16[1,640,128]{2,1,0:T(8,128)(2,1)S(1)}, u32[]{:S(2)}, u32[]{:S(2)}) collective-permute-start(bf16[1,640,128]{2,1,0:T(8,128)(2,1)S(1)} %slice.423), channel_id=1, source_target_pairs={{0,16},{4,20},{8,24},{12,28},{16,0},{20,4},{24,8},{28,12},{1,17},{... | collective-permute-start | bytes 491528 | tf_op jit(solution)/shard_map/ppermute | solution.py:26
  265.5 27.5 %collective-permute-start.35 = (bf16[1,1,240,1920]{3,2,1,0:T(8,128)(2,1)S(1)}, bf16[1,1,240,1920]{3,2,1,0:T(8,128)(2,1)S(1)}, u32[]{:S(2)}, u32[]{:S(2)}) collective-permute-start(bf16[1,1,240,1920]{3,2,1,0:T(8,128)(2,1)S(1)} %constant_dynamic-slice_fusion.9), channel_id=1, source_target_pairs={{0,2},{1,3},{2,0},{3,1},{4,6},{5,7},{6,4},{7,5},{8,10},{9,11},{10,... | collective-permute-start | bytes 2764808 | tf_op jit(solution)/shard_map/ppermute | solution.py:26
  280.9 12.1 %collective-permute-start.34 = (bf16[1,640,128]{2,1,0:T(8,128)(2,1)S(1)}, bf16[1,640,128]{2,1,0:T(8,128)(2,1)S(1)}, u32[]{:S(2)}, u32[]{:S(2)}) collective-permute-start(bf16[1,640,128]{2,1,0:T(8,128)(2,1)S(1)} %slice.416), channel_id=1, source_target_pairs={{0,16},{4,20},{8,24},{12,28},{16,0},{20,4},{24,8},{28,12},{1,17},{... | collective-permute-start | bytes 491528 | tf_op jit(solution)/shard_map/ppermute | solution.py:26
  294.1 21.5 %collective-permute-start.39 = (bf16[120,1920]{1,0:T(8,128)(2,1)}, bf16[120,1920]{1,0:T(8,128)(2,1)}, u32[]{:S(2)}, u32[]{:S(2)}) collective-permute-start(bf16[120,1920]{1,0:T(8,128)(2,1)} %dynamic-slice_bitcast_fusion), channel_id=1, source_target_pairs={{0,8},{4,12},{8,0},{12,4},{16,24},{20,28},{24,16},{28,20},{1,9},{5... | collective-permute-start | bytes 1382408 | tf_op jit(solution)/shard_map/ppermute | solution.py:26
  316.8 8.1 %collective-permute-start.40 = (bf16[64,1920]{1,0:T(8,128)(2,1)S(1)}, bf16[64,1920]{1,0:T(8,128)(2,1)S(1)}, u32[]{:S(2)}, u32[]{:S(2)}) collective-permute-start(bf16[64,1920]{1,0:T(8,128)(2,1)S(1)} %constant_dynamic-slice_fusion.8), channel_id=1, source_target_pairs={{0,16},{4,20},{8,24},{12,28},{16,0},{20,4},{24,8},{28,12},{1,17},{... | collective-permute-start | bytes 737288 | tf_op jit(solution)/shard_map/ppermute | solution.py:26
  318.5 15.8 %collective-permute-start.45 = (bf16[2,1,248,640]{3,2,1,0:T(8,128)(2,1)S(1)}, bf16[2,1,248,640]{3,2,1,0:T(8,128)(2,1)S(1)}, u32[]{:S(2)}, u32[]{:S(2)}) collective-permute-start(bf16[2,1,248,640]{3,2,1,0:T(8,128)(2,1)S(1)} %fusion.47), channel_id=1, source_target_pairs={{0,1},{1,0},{2,3},{3,2},{4,5},{5,4},{6,7},{7,6},{8,9},{9,8},{10,11... | collective-permute-start | bytes 1904648 | tf_op jit(solution)/shard_map/ppermute | solution.py:26
  324.9 7.9 %collective-permute-start.41 = (bf16[32,1920]{1,0:T(8,128)(2,1)S(1)}, bf16[32,1920]{1,0:T(8,128)(2,1)S(1)}, u32[]{:S(2)}, u32[]{:S(2)}) collective-permute-start(bf16[32,1920]{1,0:T(8,128)(2,1)S(1)} %constant_dynamic-slice_fusion.7), channel_id=1, source_target_pairs={{0,4},{4,0},{8,12},{12,8},{16,20},{20,16},{24,28},{28,24},{1,5},{5... | collective-permute-start | bytes 368648 | tf_op jit(solution)/shard_map/ppermute | solution.py:26
  332.9 61.9 %collective-permute-start.42 = (bf16[32,1920]{1,0:T(8,128)(2,1)S(1)}, bf16[32,1920]{1,0:T(8,128)(2,1)S(1)}, u32[]{:S(2)}, u32[]{:S(2)}) collective-permute-start(bf16[32,1920]{1,0:T(8,128)(2,1)S(1)} %add_convert_fusion.9), channel_id=1, source_target_pairs={{0,4},{4,0},{8,12},{12,8},{16,20},{20,16},{24,28},{28,24},{1,5},{5... | collective-permute-start | bytes 368648 | tf_op jit(solution)/shard_map/ppermute | solution.py:26
  334.5 61.8 %collective-permute-start.46 = (bf16[1,1,248,640]{3,2,1,0:T(8,128)(2,1)S(1)}, bf16[1,1,248,640]{3,2,1,0:T(8,128)(2,1)S(1)}, u32[]{:S(2)}, u32[]{:S(2)}) collective-permute-start(bf16[1,1,248,640]{3,2,1,0:T(8,128)(2,1)S(1)} %constant_dynamic-slice_fusion.6), channel_id=1, source_target_pairs={{0,2},{1,3},{2,0},{3,1},{4,6},{5,7},{6,4},{7,5},{8,10},{9,11},{10,... | collective-permute-start | bytes 952328 | tf_op jit(solution)/shard_map/ppermute | solution.py:26
  393.2 39.0 %collective-permute-start.53 = (bf16[1,2,240,1280]{3,2,1,0:T(8,128)(2,1)S(1)}, bf16[1,2,240,1280]{3,2,1,0:T(8,128)(2,1)S(1)}, u32[]{:S(2)}, u32[]{:S(2)}) collective-permute-start(bf16[1,2,240,1280]{3,2,1,0:T(8,128)(2,1)S(1)} %get-tuple-element.103), channel_id=1, source_target_pairs={{0,2},{1,3},{2,0},{3,1},{4,6},{5,7},{6,4},{7,5},{8,10},{9,11},{10,... | collective-permute-start | bytes 3686408 | tf_op jit(solution)/shard_map/ppermute | solution.py:26
  394.8 12.9 %collective-permute-start.43 = (bf16[64,1920]{1,0:T(8,128)(2,1)S(1)}, bf16[64,1920]{1,0:T(8,128)(2,1)S(1)}, u32[]{:S(2)}, u32[]{:S(2)}) collective-permute-start(bf16[64,1920]{1,0:T(8,128)(2,1)S(1)} %maximum_select_fusion.11), channel_id=1, source_target_pairs={{0,16},{4,20},{8,24},{12,28},{16,0},{20,4},{24,8},{28,12},{1,17},{... | collective-permute-start | bytes 737288 | tf_op jit(solution)/shard_map/ppermute | solution.py:26
  396.4 11.3 %collective-permute-start.47 = (bf16[128,640]{1,0:T(8,128)(2,1)S(1)}, bf16[128,640]{1,0:T(8,128)(2,1)S(1)}, u32[]{:S(2)}, u32[]{:S(2)}) collective-permute-start(bf16[128,640]{1,0:T(8,128)(2,1)S(1)} %dynamic-slice_bitcast_fusion.1), channel_id=1, source_target_pairs={{0,4},{4,0},{8,12},{12,8},{16,20},{20,16},{24,28},{28,24},{1,5},{5... | collective-permute-start | bytes 491528 | tf_op jit(solution)/shard_map/ppermute | solution.py:26
  413.3 14.9 %collective-permute-start.44 = (bf16[120,1920]{1,0:T(8,128)(2,1)S(1)}, bf16[120,1920]{1,0:T(8,128)(2,1)S(1)}, u32[]{:S(2)}, u32[]{:S(2)}) collective-permute-start(bf16[120,1920]{1,0:T(8,128)(2,1)S(1)} %pad_maximum_fusion.10), channel_id=1, source_target_pairs={{0,8},{4,12},{8,0},{12,4},{16,24},{20,28},{24,16},{28,20},{1,9},{5... | collective-permute-start | bytes 1382408 | tf_op jit(solution)/shard_map/ppermute | solution.py:26
  417.7 7.0 %collective-permute-start.50 = (bf16[32,640]{1,0:T(8,128)(2,1)S(1)}, bf16[32,640]{1,0:T(8,128)(2,1)S(1)}, u32[]{:S(2)}, u32[]{:S(2)}) collective-permute-start(bf16[32,640]{1,0:T(8,128)(2,1)S(1)} %add_convert_fusion.13), channel_id=1, source_target_pairs={{0,16},{4,20},{8,24},{12,28},{16,0},{20,4},{24,8},{28,12},{1,17},{... | collective-permute-start | bytes 122888 | tf_op jit(solution)/shard_map/ppermute | solution.py:26
  (103 other events, 1003.0 us)
Sparse Core Ops, SparseCore 0:
  227.3 164.0 all-reduce.4
